TPU v7x, 32 devices: a whole 2x2x4 slice. The times are simulated.
32 devices in a mesh: replica: 8 (over y, x, core), shard: 4 (over z).
Axes of the slice: x: 2, y: 2, z: 4, core: 2. Of those that a mesh axis runs over, the one named last changes fastest.
Arguments:
- layer_input: bfloat16 [8192, 2048], P(('replica', 'shard')), may hold values from -6 to 6
- attn_gain: bfloat16 [2048], P('shard'), may hold values from 0.5 to 1.5
- attn_shift: bfloat16 [2048], P('shard'), may hold values from -1.796875 to 1.796875
- qkv_weight: bfloat16 [2048, 6144], P('shard'), may hold values from -0.125 to 0.125
- qkv_bias: bfloat16 [6144], P('shard'), may hold values from -1.796875 to 1.796875
- out_weight: bfloat16 [2048, 2048], P('shard'), may hold values from -2 to 2
- out_bias: bfloat16 [2048], P('shard'), may hold values from -1.796875 to 1.796875
- mlp_gain: bfloat16 [2048], P('shard'), may hold values from 0.5 to 1.5
- mlp_shift: bfloat16 [2048], P('shard'), may hold values from -1.796875 to 1.796875
- up_weight: bfloat16 [2048, 8192], P('shard'), may hold values from -0.125 to 0.125
- up_bias: bfloat16 [8192], P('shard'), may hold values from -1.796875 to 1.796875
- down_weight: bfloat16 [8192, 2048], P('shard'), may hold values from -0.0625 to 0.0625
- down_bias: bfloat16 [2048], P('shard'), may hold values from -1.796875 to 1.796875
- seq_lengths: int32 [8, 4], P('replica'), may hold values from 1 to 896, 1024 in all within a row
- upstream: bfloat16 [8192, 2048], P(('replica', 'shard')), may hold values from -6 to 6
Outputs:
- layer_output: bfloat16 [8192, 2048], P(('replica', 'shard'))
- input_grad: float32 [8192, 2048], P(('replica', 'shard'))
- attn_gain_grad: float32 [2048], P('shard')
- attn_shift_grad: float32 [2048], P('shard')
- qkv_weight_grad: float32 [2048, 6144], P('shard')
- qkv_bias_grad: float32 [6144], P('shard')
- out_weight_grad: float32 [2048, 2048], P('shard')
- out_bias_grad: float32 [2048], P('shard')
- mlp_gain_grad: float32 [2048], P('shard')
- mlp_shift_grad: float32 [2048], P('shard')
- up_weight_grad: float32 [2048, 8192], P('shard')
- up_bias_grad: float32 [8192], P('shard')
- down_weight_grad: float32 [8192, 2048], P('shard')
- down_bias_grad: float32 [2048], P('shard')
Inputs may be any that keep to these rules, and one draw needn't show every extreme that they name: `seq_lengths`: each row sums to 1024; its largest entry is exactly 896, so one sequence of every group spans all of its stretches.
All inputs are finite; a program needn't handle non-finite values.
Results may differ from a plain program's by a relative error of at most 0.0092.
Values may be sent and summed in bfloat16 or wider, within the bound.
A program may use at most 640 MiB of HBM per device.

v0:
```python
from functools import partial
import math

import jax
import jax.numpy as jnp
from jax import lax
from jax.sharding import PartitionSpec as P

D = 2048
HEADS = 8
HEAD = 256
ROT = 64


EPSILON = 1e-05
ROPE_BASE = 10000.0
NEG_LARGE = -1e30
CONTRACT_ROWS = (((0,), (0,)), ((), ()))
CONTRACT_COLS = (((1,), (1,)), ((), ()))


def normalize(layer_rows):
    centered = layer_rows - jnp.mean(layer_rows, -1, keepdims=True)
    variance = jnp.mean(centered * centered, -1, keepdims=True)
    inverse_std = lax.rsqrt(variance + EPSILON)
    return (centered * inverse_std, inverse_std)


def norm_backward(grad_normed, normed, inverse_std):
    mean_grad = jnp.mean(grad_normed, -1, keepdims=True)
    mean_cross = jnp.mean(grad_normed * normed, -1, keepdims=True)
    return (grad_normed - mean_grad - normed * mean_cross) * inverse_std


def rotation_tables(positions):
    exponent = jnp.arange(ROT // 2, dtype=jnp.float32) * (2.0 / ROT)
    inv_freq = jnp.power(jnp.float32(ROPE_BASE), -exponent)
    angles = positions.astype(jnp.float32)[:, None] * inv_freq[None, :]
    cosine_table = jnp.cos(angles)
    sine_table = jnp.sin(angles)
    return (
        jnp.concatenate([cosine_table, cosine_table], 1),
        jnp.concatenate([sine_table, sine_table], 1),
    )


def turn(values, cosine_table, sine_table):
    rotary = values[..., :ROT]
    first_half = rotary[..., : ROT // 2]
    second_half = rotary[..., ROT // 2 :]
    swapped = jnp.concatenate([-second_half, first_half], -1)
    turned = rotary * cosine_table[:, None, :] + swapped * sine_table[:, None, :]
    return jnp.concatenate([turned, values[..., ROT:]], -1)


def sequence_layout(lengths, group_rows):
    seq_count = lengths.shape[0]
    seq_ends = jnp.cumsum(lengths)
    where_in = jnp.arange(group_rows, dtype=jnp.int32)
    seg_ids = jnp.sum((where_in[:, None] >= seq_ends[None, :]).astype(jnp.int32), 1)
    starts = seq_ends - lengths
    chosen = (seg_ids[:, None] == jnp.arange(seq_count, dtype=jnp.int32)[None, :]).astype(jnp.int32)
    positions = where_in - jnp.sum(chosen * starts[None, :], 1)
    return (seg_ids, positions)


def fetch_attention(attn_gain, attn_shift, qkv_weight, qkv_bias, out_weight, out_bias):
    return (
        lax.all_gather(attn_gain, "shard", axis=0, tiled=True),
        lax.all_gather(attn_shift, "shard", axis=0, tiled=True),
        lax.all_gather(qkv_weight, "shard", axis=0, tiled=True),
        lax.all_gather(qkv_bias, "shard", axis=0, tiled=True),
        lax.all_gather(out_weight, "shard", axis=0, tiled=True),
        lax.all_gather(out_bias, "shard", axis=0, tiled=True),
    )


def fetch_mlp(mlp_gain, mlp_shift, up_weight, up_bias, down_weight, down_bias):
    return (
        lax.all_gather(mlp_gain, "shard", axis=0, tiled=True),
        lax.all_gather(mlp_shift, "shard", axis=0, tiled=True),
        lax.all_gather(up_weight, "shard", axis=0, tiled=True),
        lax.all_gather(up_bias, "shard", axis=0, tiled=True),
        lax.all_gather(down_weight, "shard", axis=0, tiled=True),
        lax.all_gather(down_bias, "shard", axis=0, tiled=True),
    )


def attention_scores(queries, keys_heads, allowed, score_scale):
    scores = (
        jnp.einsum("qhd,khd->hqk", queries, keys_heads, preferred_element_type=jnp.float32)
        * score_scale
    )
    return jnp.where(allowed[None], scores, NEG_LARGE)


def shards(
    layer_input,
    attn_gain,
    attn_shift,
    qkv_weight,
    qkv_bias,
    out_weight,
    out_bias,
    mlp_gain,
    mlp_shift,
    up_weight,
    up_bias,
    down_weight,
    down_bias,
    seq_lengths,
    upstream,
):
    local_rows = layer_input.shape[0]
    shard_count = lax.axis_size("shard")
    group_rows = local_rows * shard_count
    score_scale = 1.0 / math.sqrt(HEAD)
    seg_ids, positions = sequence_layout(seq_lengths[0], group_rows)
    shard_place = lax.axis_index("shard")
    offset = shard_place * local_rows
    own_segs = lax.dynamic_slice_in_dim(seg_ids, offset, local_rows, 0)
    own_pos = lax.dynamic_slice_in_dim(positions, offset, local_rows, 0)
    query_index = offset + jnp.arange(local_rows, dtype=jnp.int32)
    key_index = jnp.arange(group_rows, dtype=jnp.int32)
    allowed = (own_segs[:, None] == seg_ids[None, :]) & (key_index[None, :] <= query_index[:, None])
    cosine_table, sine_table = rotation_tables(own_pos)
    rows_f = layer_input.astype(jnp.float32)
    normed, inverse_std = normalize(rows_f)
    gain_a_all, shift_a_all, joined_weight_all, joined_bias_all, proj_weight_all, proj_bias_all = (
        fetch_attention(attn_gain, attn_shift, qkv_weight, qkv_bias, out_weight, out_bias)
    )
    attn_in = (normed * gain_a_all.astype(jnp.float32) + shift_a_all.astype(jnp.float32)).astype(
        jnp.bfloat16
    )
    joined_qkv = jnp.dot(
        attn_in, joined_weight_all, preferred_element_type=jnp.float32
    ) + joined_bias_all.astype(jnp.float32)
    queries = turn(
        joined_qkv[:, :D].reshape(local_rows, HEADS, HEAD), cosine_table, sine_table
    ).astype(jnp.bfloat16)
    keys_own = turn(
        joined_qkv[:, D : 2 * D].reshape(local_rows, HEADS, HEAD), cosine_table, sine_table
    ).astype(jnp.bfloat16)
    values_own = joined_qkv[:, 2 * D :].astype(jnp.bfloat16)
    keys_all, values_all = (
        lax.all_gather(keys_own.reshape(local_rows, D), "shard", axis=0, tiled=True),
        lax.all_gather(values_own, "shard", axis=0, tiled=True),
    )
    keys_heads = keys_all.reshape(group_rows, HEADS, HEAD)
    values_heads = values_all.reshape(group_rows, HEADS, HEAD)
    scores = attention_scores(queries, keys_heads, allowed, score_scale)
    row_max = jnp.max(scores, -1, keepdims=True)
    shifted = jnp.exp(scores - row_max)
    row_total = jnp.sum(shifted, -1, keepdims=True)
    log_total = row_max + jnp.log(row_total)
    probs_low = (shifted / row_total).astype(jnp.bfloat16)
    mixed_heads = jnp.einsum(
        "hqk,khd->qhd", probs_low, values_heads, preferred_element_type=jnp.float32
    )
    mixed_low = mixed_heads.reshape(local_rows, D).astype(jnp.bfloat16)
    attn_out = jnp.dot(
        mixed_low, proj_weight_all, preferred_element_type=jnp.float32
    ) + proj_bias_all.astype(jnp.float32)
    gain_m_all, shift_m_all, up_weight_all, up_bias_all, down_weight_all, down_bias_all = fetch_mlp(
        mlp_gain, mlp_shift, up_weight, up_bias, down_weight, down_bias
    )
    mlp_in = (normed * gain_m_all.astype(jnp.float32) + shift_m_all.astype(jnp.float32)).astype(
        jnp.bfloat16
    )
    up_pre = jnp.dot(
        mlp_in, up_weight_all, preferred_element_type=jnp.float32
    ) + up_bias_all.astype(jnp.float32)
    activated, gelu_back = jax.vjp(partial(jax.nn.gelu, approximate=False), up_pre)
    act_low = activated.astype(jnp.bfloat16)
    mlp_out = jnp.dot(
        act_low, down_weight_all, preferred_element_type=jnp.float32
    ) + down_bias_all.astype(jnp.float32)
    layer_output = (rows_f + attn_out + mlp_out).astype(jnp.bfloat16)
    grad_rows = upstream.astype(jnp.float32)
    gain_m_all, shift_m_all, up_weight_all, up_bias_all, down_weight_all, down_bias_all = fetch_mlp(
        mlp_gain, mlp_shift, up_weight, up_bias, down_weight, down_bias
    )
    grad_act = lax.dot_general(
        upstream, down_weight_all, CONTRACT_COLS, preferred_element_type=jnp.float32
    )
    grad_pre = gelu_back(grad_act)[0].astype(jnp.bfloat16)
    grad_mlp_in = lax.dot_general(
        grad_pre, up_weight_all, CONTRACT_COLS, preferred_element_type=jnp.float32
    )
    mlp_gain_term = jnp.sum(grad_mlp_in * normed, 0)
    mlp_shift_term = jnp.sum(grad_mlp_in, 0)
    grad_from_mlp = norm_backward(grad_mlp_in * gain_m_all.astype(jnp.float32), normed, inverse_std)
    gain_a_all, shift_a_all, joined_weight_all, joined_bias_all, proj_weight_all, proj_bias_all = (
        fetch_attention(attn_gain, attn_shift, qkv_weight, qkv_bias, out_weight, out_bias)
    )
    grad_mixed = lax.dot_general(
        upstream, proj_weight_all, CONTRACT_COLS, preferred_element_type=jnp.float32
    ).astype(jnp.bfloat16)
    scores = attention_scores(queries, keys_heads, allowed, score_scale)
    attn_probs = jnp.exp(scores - log_total)
    probs_low = attn_probs.astype(jnp.bfloat16)
    grad_heads = grad_mixed.reshape(local_rows, HEADS, HEAD)
    grad_probs = jnp.einsum(
        "qhd,khd->hqk", grad_heads, values_heads, preferred_element_type=jnp.float32
    )
    row_delta = jnp.sum(attn_probs * grad_probs, -1, keepdims=True)
    grad_scores = (attn_probs * (grad_probs - row_delta)).astype(jnp.bfloat16)
    grad_queries = (
        jnp.einsum("hqk,khd->qhd", grad_scores, keys_heads, preferred_element_type=jnp.float32)
        * score_scale
    )
    grad_keys_part = (
        jnp.einsum("hqk,qhd->khd", grad_scores, queries, preferred_element_type=jnp.float32)
        * score_scale
    )
    grad_values_part = jnp.einsum(
        "hqk,qhd->khd", probs_low, grad_heads, preferred_element_type=jnp.float32
    )
    grad_keys, grad_values = (
        lax.psum_scatter(
            grad_keys_part.reshape(group_rows, D), "shard", scatter_dimension=0, tiled=True
        ),
        lax.psum_scatter(
            grad_values_part.reshape(group_rows, D), "shard", scatter_dimension=0, tiled=True
        ),
    )
    template = jnp.zeros((local_rows, HEADS, HEAD), jnp.float32)
    unused_value, turn_back = jax.vjp(
        partial(turn, cosine_table=cosine_table, sine_table=sine_table), template
    )
    grad_q_plain = turn_back(grad_queries)[0].reshape(local_rows, D)
    grad_k_plain = turn_back(grad_keys.reshape(local_rows, HEADS, HEAD))[0].reshape(local_rows, D)
    grad_joined = jnp.concatenate([grad_q_plain, grad_k_plain, grad_values], 1).astype(jnp.bfloat16)
    grad_attn_in = lax.dot_general(
        grad_joined, joined_weight_all, CONTRACT_COLS, preferred_element_type=jnp.float32
    )
    attn_gain_term = jnp.sum(grad_attn_in * normed, 0)
    attn_shift_term = jnp.sum(grad_attn_in, 0)
    grad_from_attn = norm_backward(
        grad_attn_in * gain_a_all.astype(jnp.float32), normed, inverse_std
    )
    input_grad = grad_rows + grad_from_mlp + grad_from_attn
    down_weight_term = lax.dot_general(
        act_low, upstream, CONTRACT_ROWS, preferred_element_type=jnp.float32
    )
    bias_term = jnp.sum(grad_rows, 0)
    up_weight_term = lax.dot_general(
        mlp_in, grad_pre, CONTRACT_ROWS, preferred_element_type=jnp.float32
    )
    up_bias_term = jnp.sum(grad_pre.astype(jnp.float32), 0)
    out_weight_term = lax.dot_general(
        mixed_low, upstream, CONTRACT_ROWS, preferred_element_type=jnp.float32
    )
    qkv_weight_term = lax.dot_general(
        attn_in, grad_joined, CONTRACT_ROWS, preferred_element_type=jnp.float32
    )
    qkv_bias_term = jnp.sum(grad_joined.astype(jnp.float32), 0)
    mlp_parts = (
        lax.psum_scatter(mlp_gain_term, "shard", scatter_dimension=0, tiled=True),
        lax.psum_scatter(mlp_shift_term, "shard", scatter_dimension=0, tiled=True),
        lax.psum_scatter(up_weight_term, "shard", scatter_dimension=0, tiled=True),
        lax.psum_scatter(up_bias_term, "shard", scatter_dimension=0, tiled=True),
        lax.psum_scatter(down_weight_term, "shard", scatter_dimension=0, tiled=True),
        lax.psum_scatter(bias_term, "shard", scatter_dimension=0, tiled=True),
    )
    attn_parts = (
        lax.psum_scatter(attn_gain_term, "shard", scatter_dimension=0, tiled=True),
        lax.psum_scatter(attn_shift_term, "shard", scatter_dimension=0, tiled=True),
        lax.psum_scatter(qkv_weight_term, "shard", scatter_dimension=0, tiled=True),
        lax.psum_scatter(qkv_bias_term, "shard", scatter_dimension=0, tiled=True),
        lax.psum_scatter(out_weight_term, "shard", scatter_dimension=0, tiled=True),
        lax.psum_scatter(bias_term, "shard", scatter_dimension=0, tiled=True),
    )
    summed = lax.psum(
        (
            attn_parts[0],
            attn_parts[1],
            attn_parts[2],
            attn_parts[3],
            attn_parts[4],
            attn_parts[5],
            mlp_parts[0],
            mlp_parts[1],
            mlp_parts[2],
            mlp_parts[3],
            mlp_parts[4],
            mlp_parts[5],
        ),
        "replica",
    )
    return (
        layer_output,
        input_grad,
        summed[0],
        summed[1],
        summed[2],
        summed[3],
        summed[4],
        summed[5],
        summed[6],
        summed[7],
        summed[8],
        summed[9],
        summed[10],
        summed[11],
    )


def solution(mesh):
    in_specs = (
        P(("replica", "shard"), None),
        P("shard"),
        P("shard"),
        P("shard", None),
        P("shard"),
        P("shard", None),
        P("shard"),
        P("shard"),
        P("shard"),
        P("shard", None),
        P("shard"),
        P("shard", None),
        P("shard"),
        P("replica", None),
        P(("replica", "shard"), None),
    )
    out_specs = (
        P(("replica", "shard"), None),
        P(("replica", "shard"), None),
        P("shard"),
        P("shard"),
        P("shard", None),
        P("shard"),
        P("shard", None),
        P("shard"),
        P("shard"),
        P("shard"),
        P("shard", None),
        P("shard"),
        P("shard", None),
        P("shard"),
    )
    return jax.shard_map(shards, mesh=mesh, in_specs=in_specs, out_specs=out_specs, check_vma=False)
```

profile of v0, /device:TPU:0, one launch (start us, length us, event | category | flops | bytes accessed | tf_op | source)
XLA Modules:
  0.0 6153.8 jit_solution(16387201858122093098)
XLA Ops:
  9.0 13.5 all-gather.1
  22.5 12.0 all-gather
  34.6 33.0 all-gather.2
  69.3 368.7 %all-gather.14.cloned.1.call-done = bf16[2048,6144]{1,0:T(8,128)(2,1)} async-done(((bf16[512,6144]{1,0:T(8,128)(2,1)}), bf16[2048,6144]{1,0:T(8,128)(2,1)}) %all-gather.14.cloned.1.call-update) | async-done | bytes 25165840 | tf_op jit(solution)/shard_map/all_gather | solution.py:71
  437.9 12.6 convolution_add_fusion.1
  466.5 120.9 %all-gather.20.cloned.1.call-done = bf16[2048,2048]{1,0:T(8,128)(2,1)} async-done(((bf16[512,2048]{1,0:T(8,128)(2,1)}), bf16[2048,2048]{1,0:T(8,128)(2,1)}) %all-gather.20.cloned.1.call-update) | async-done | bytes 8388624 | tf_op jit(solution)/shard_map/all_gather | solution.py:73
  597.3 71.0 %all-gather.18.cloned.1.call-done = bf16[1024,2048]{0,1:T(8,128)(2,1)} async-done(((bf16[256,2048]{0,1:T(8,128)(2,1)}), bf16[1024,2048]{0,1:T(8,128)(2,1)}) %all-gather.18.cloned.1.call-update) | async-done | bytes 4194320 | tf_op jit(solution)/shard_map/all_gather | solution.py:146
  678.6 70.7 %all-gather.16.cloned.1.call-done = bf16[1024,2048]{1,0:T(8,128)(2,1)} async-done(((bf16[256,2048]{1,0:T(8,128)(2,1)}), bf16[1024,2048]{1,0:T(8,128)(2,1)}) %all-gather.16.cloned.1.call-update) | async-done | bytes 4194320 | tf_op jit(solution)/shard_map/all_gather | solution.py:147
  798.7 107.7 %reduce-scatter.11.cloned.1.call-done = f32[256,2048]{0,1:T(8,128)} async-done(((f32[1024,2048]{0,1:T(8,128)}), f32[256,2048]{0,1:T(8,128)}) %reduce-scatter.11.cloned.1.call-update) | async-done | bytes 2097168 | tf_op jit(solution)/shard_map/reduce_scatter | solution.py:220
  928.7 125.8 %reduce-scatter.13.cloned.1.call-done = f32[256,2048]{0,1:T(8,128)} async-done(((f32[1024,2048]{0,1:T(8,128)}), f32[256,2048]{0,1:T(8,128)}) %reduce-scatter.13.cloned.1.call-update) | async-done | bytes 2097168 | tf_op jit(solution)/shard_map/reduce_scatter | solution.py:223
  1057.2 27.7 fusion.57
  1085.6 19.7 all-gather.5
  1105.4 22.5 all-gather.4
  1127.9 42.1 all_gather.59
  1169.9 448.8 %all-gather.22.cloned.1.call-done = bf16[2048,8192]{1,0:T(8,128)(2,1)} async-done(((bf16[512,8192]{1,0:T(8,128)(2,1)}), bf16[2048,8192]{1,0:T(8,128)(2,1)}) %all-gather.22.cloned.1.call-update) | async-done | bytes 33554448 | tf_op jit(solution)/shard_map/all_gather | solution.py:82
  1618.7 22.4 convolution_add_fusion
  1641.1 538.8 %all-gather.24.cloned.1.call-done = bf16[8192,2048]{1,0:T(8,128)(2,1)} async-done(((bf16[2048,2048]{1,0:T(8,128)(2,1)}), bf16[8192,2048]{1,0:T(8,128)(2,1)}) %all-gather.24.cloned.1.call-update) | async-done | bytes 33554448 | tf_op jit(solution)/shard_map/all_gather | solution.py:84
  2179.9 34.3 convert_reduce_fusion
  2214.2 25.9 fusion.54
  2249.7 23.7 fusion.68
  2273.5 17.6 fusion.66
  2291.2 14.9 fusion.40
  2314.6 146.8 %reduce-scatter.17.cloned.1.call-done = f32[512,2048]{1,0:T(8,128)} async-done(((f32[2048,2048]{1,0:T(8,128)}), f32[512,2048]{1,0:T(8,128)}) %reduce-scatter.17.cloned.1.call-update) | async-done | bytes 4194320 | tf_op jit(solution)/shard_map/reduce_scatter | solution.py:271
  2461.4 823.8 %reduce-scatter.15.cloned.1.call-done = f32[512,6144]{1,0:T(8,128)} async-done(((f32[2048,6144]{1,0:T(8,128)}), f32[512,6144]{1,0:T(8,128)}) %reduce-scatter.15.cloned.1.call-update) | async-done | bytes 12582928 | tf_op jit(solution)/shard_map/reduce_scatter | solution.py:269
  3285.1 1099.1 %reduce-scatter.19.cloned.1.call-done = f32[512,8192]{1,0:T(8,128)} async-done(((f32[2048,8192]{1,0:T(8,128)}), f32[512,8192]{1,0:T(8,128)}) %reduce-scatter.19.cloned.1.call-update) | async-done | bytes 16777232
  4384.3 1098.5 %reduce-scatter.21.cloned.1.call-done = f32[2048,2048]{1,0:T(8,128)} async-done(((f32[8192,2048]{1,0:T(8,128)}), f32[2048,2048]{1,0:T(8,128)}) %reduce-scatter.21.cloned.1.call-update) | async-done | bytes 16777232
  5486.0 12.7 all-gather.6
  5498.7 11.9 all-gather.3
  5516.5 16.6 fusion.18
  5538.4 24.6 all-reduce.17
  5563.0 548.2 %all-reduce.23.cloned.1.call-done = (f32[512,6144]{1,0:T(8,128)}, f32[512,2048]{1,0:T(8,128)}, f32[512,8192]{1,0:T(8,128)}, f32[2048,2048]{1,0:T(8,128)}) async-done(((f32[512,6144]{1,0:T(8,128)}, f32[512,2048]{1,0:T(8,128)}, f32[512,8192]{1,0:T(8,128)}, f32[2048,2048]{1,0:T(8,128)}), (f32[512,6144]{1,0:T(8,128)}, f32[512,2048]{1,0:T(8,128)}, f32[512,8192]{1,0:T(8,128)}, ...) | async-done | bytes 50331664 | tf_op jit(solution)/shard_map/psum | solution.py:274
  6124.9 13.9 copy.160
  (199 shorter events, 166.7 us)
Async XLA Ops:
  7.2 27.3 copy-start.23
  7.2 61.4 copy-start.2
  7.2 430.7 %all-gather.14.cloned.1.call-start = ((), (), s32[]{:S(2)}) async-start(), calls=%async_computation.6 | async-start | bytes 31457280 | tf_op jit(solution)/shard_map/all_gather | solution.py:71
  8.0 579.4 %all-gather.20.cloned.1.call-start = ((), (), s32[]{:S(2)}) async-start(), calls=%async_computation.9 | async-start | bytes 10485760 | tf_op jit(solution)/shard_map/all_gather | solution.py:73
  8.7 659.6 %all-gather.18.cloned.1.call-start = ((), (), s32[]{:S(2)}) async-start(), calls=%async_computation.8 | async-start | bytes 5242880 | tf_op jit(solution)/shard_map/all_gather | solution.py:146
  34.5 1021.6 %copy-start.20 = (f32[4,1,512]{2,1,0:T(1,128)}, f32[4,1,512]{2,1,0:T(1,128)S(1)}, u32[]{:S(2)}) copy-start(f32[4,1,512]{2,1,0:T(1,128)S(1)} %convert_element_type.116) | copy-start | bytes 24580
  462.2 287.1 %all-gather.16.cloned.1.call-start = ((), (), s32[]{:S(2)}) async-start(), calls=%async_computation.7 | async-start | bytes 5242880 | tf_op jit(solution)/shard_map/all_gather | solution.py:147
  465.0 441.5 %reduce-scatter.11.cloned.1.call-start = ((), (), s32[]{:S(2)}) async-start(), calls=%async_computation.12 | async-start | bytes 10485760 | tf_op jit(solution)/shard_map/reduce_scatter | solution.py:220
  672.9 76.4 %copy-start.10 = (bf16[256,2048]{0,1:T(8,128)(2,1)S(1)}, bf16[256,2048]{0,1:T(8,128)(2,1)}, u32[]{:S(2)}) copy-start(bf16[256,2048]{0,1:T(8,128)(2,1)} %copy.112) | copy-start | bytes 3145732
  749.3 7.2 copy-start.1
  763.3 291.2 %reduce-scatter.13.cloned.1.call-start = ((), (), s32[]{:S(2)}) async-start(), calls=%async_computation.13 | async-start | bytes 10485760 | tf_op jit(solution)/shard_map/reduce_scatter | solution.py:223
  772.1 846.6 %all-gather.22.cloned.1.call-start = ((), (), s32[]{:S(2)}) async-start(), calls=%async_computation.10 | async-start | bytes 41943040 | tf_op jit(solution)/shard_map/all_gather | solution.py:82
  772.9 1407.1 %all-gather.24.cloned.1.call-start = ((), (), s32[]{:S(2)}) async-start(), calls=%async_computation.11 | async-start | bytes 41943040 | tf_op jit(solution)/shard_map/all_gather | solution.py:84
  773.6 8.3 copy-start.6
  773.6 1687.8 %reduce-scatter.17.cloned.1.call-start = ((), (), s32[]{:S(2)}) async-start(), calls=%async_computation.15 | async-start | bytes 20971520 | tf_op jit(solution)/shard_map/reduce_scatter | solution.py:271
  790.5 2494.7 %reduce-scatter.15.cloned.1.call-start = ((), (), s32[]{:S(2)}) async-start(), calls=%async_computation.14 | async-start | bytes 62914560 | tf_op jit(solution)/shard_map/reduce_scatter | solution.py:269
  1084.9 43.0 copy-start.22
  1084.9 3299.3 %reduce-scatter.19.cloned.1.call-start = ((), (), s32[]{:S(2)}) async-start(), calls=%async_computation.16 | async-start | bytes 83886080
  2240.2 3242.6 %reduce-scatter.21.cloned.1.call-start = ((), (), s32[]{:S(2)}) async-start(), calls=%async_computation.17 | async-start | bytes 83886080
  2273.5 17.7 copy-start.21
  2273.5 3259.7 %all-reduce.25.cloned.1.call-start = ((), (), s32[]{:S(2)}) async-start(), calls=%async_computation.19 | async-start | bytes 196608
  2273.5 17.7 copy-start.8
  2273.5 17.7 copy-start.9
  2314.5 3796.6 %all-reduce.23.cloned.1.call-start = ((), (), s32[]{:S(2)}) async-start(), calls=%async_computation.18 | async-start | bytes 100663296 | tf_op jit(solution)/shard_map/psum | solution.py:274
  5482.8 27.8 copy-start.16
  5510.6 5.9 copy-start.4
  5563.0 559.8 %copy-start.24 = (f32[512]{0:T(512)}, f32[512]{0:T(512)S(1)}, u32[]{:S(2)}) copy-start(f32[512]{0:T(512)S(1)} %get-tuple-element.111) | copy-start | bytes 6148
  6111.7 11.0 copy-start.18
  6122.7 16.0 slice-start
  6124.9 13.9 slice-start.1
  6124.9 14.4 slice-start.2
  6124.9 16.0 slice-start.3
  (19 other events, 40.7 us)
Sparse Core Ops, SparseCore 0:
  9.7 428.2 all-gather.13
  439.5 147.8 all-gather.19
  589.5 78.7 all-gather.17
  670.3 78.9 all-gather.15
  763.4 142.9 reduce-scatter.10
  909.2 145.1 reduce-scatter.12
  1056.0 562.6 all-gather.21
  1620.3 559.6 all-gather.23
  2182.9 278.4 reduce-scatter.16
  2463.7 821.3 reduce-scatter.14
  3287.5 1096.6 reduce-scatter.18
  4386.6 1096.1 reduce-scatter.20
  5486.8 36.6 all-reduce.24
  5528.2 582.9 all-reduce.22
where the time goes:
time: 6160 us; the launch traced here: 6150 us
  waiting for transfers between devices  5570 us (90%)
  matrix products  254 us (4%)
  blocking collectives  192 us (3%)
  local copies, waits for them, and re-layouts  80.7 us (1%)
    unnamed x17, waiting for transfers between devices  2200 us
    reduce_scatter x1, waiting for transfers between devices, shards(): lax.psum_scatter(qkv_weight_term, 'shard', scatter_dimension=0, tiled=True)  824 us
    psum x1, waiting for transfers between devices, shards(): lax.psum((attn_parts[0], attn_parts[1], attn_parts[2], attn_parts[3], att...  548 us
    all_gather x1, waiting for transfers between devices, fetch_mlp(): lax.all_gather(down_weight, 'shard', axis=0, tiled=True)  539 us
    all_gather x1, waiting for transfers between devices, fetch_mlp(): lax.all_gather(up_weight, 'shard', axis=0, tiled=True)  449 us
    all_gather x1, waiting for transfers between devices, fetch_attention(): lax.all_gather(qkv_weight, 'shard', axis=0, tiled=True)  369 us
    reduce_scatter x1, waiting for transfers between devices, shards(): lax.psum_scatter(out_weight_term, 'shard', scatter_dimension=0, tiled=True)  147 us
    reduce_scatter x1, waiting for transfers between devices, shards(): lax.psum_scatter(grad_values_part.reshape(group_rows, D), 'shard', scatte...  126 us
  transfers between devices with their start and end apart: 14, of which 13 were waited for; matrix products, arithmetic and copies ran while one was open for 5% of the time, Pallas kernels for 0%

commit v1 on v0

v1 whole, which is shorter than its diff:
```python
from functools import partial
import math

import jax
import jax.numpy as jnp
from jax import lax
from jax.experimental import pallas as pl
from jax.experimental.pallas import tpu as pltpu
from jax.sharding import PartitionSpec as P

D = 2048
HEADS = 8
HEAD = 256
ROT = 64


EPSILON = 1e-05
ROPE_BASE = 10000.0
NEG_LARGE = -1e30
MESH = pl.DeviceIdType.MESH
CONTRACT_ROWS = (((0,), (0,)), ((), ()))
CONTRACT_COLS = (((1,), (1,)), ((), ()))


def normalize(layer_rows):
    centered = layer_rows - jnp.mean(layer_rows, -1, keepdims=True)
    variance = jnp.mean(centered * centered, -1, keepdims=True)
    inverse_std = lax.rsqrt(variance + EPSILON)
    return (centered * inverse_std, inverse_std)


def norm_backward(grad_normed, normed, inverse_std):
    mean_grad = jnp.mean(grad_normed, -1, keepdims=True)
    mean_cross = jnp.mean(grad_normed * normed, -1, keepdims=True)
    return (grad_normed - mean_grad - normed * mean_cross) * inverse_std


def rotation_tables(positions):
    exponent = jnp.arange(ROT // 2, dtype=jnp.float32) * (2.0 / ROT)
    inv_freq = jnp.power(jnp.float32(ROPE_BASE), -exponent)
    angles = positions.astype(jnp.float32)[:, None] * inv_freq[None, :]
    cosine_table = jnp.cos(angles)
    sine_table = jnp.sin(angles)
    return (
        jnp.concatenate([cosine_table, cosine_table], 1),
        jnp.concatenate([sine_table, sine_table], 1),
    )


def turn(values, cosine_table, sine_table):
    rotary = values[..., :ROT]
    first_half = rotary[..., : ROT // 2]
    second_half = rotary[..., ROT // 2 :]
    swapped = jnp.concatenate([-second_half, first_half], -1)
    turned = rotary * cosine_table[:, None, :] + swapped * sine_table[:, None, :]
    return jnp.concatenate([turned, values[..., ROT:]], -1)


def turn_back(values, cosine_table, sine_table):
    rotary = values[..., :ROT]
    scaled = rotary * sine_table[:, None, :]
    swapped = jnp.concatenate([scaled[..., ROT // 2 :], -scaled[..., : ROT // 2]], -1)
    turned = rotary * cosine_table[:, None, :] + swapped
    return jnp.concatenate([turned, values[..., ROT:]], -1)


def sequence_layout(lengths, group_rows):
    seq_count = lengths.shape[0]
    seq_ends = jnp.cumsum(lengths)
    where_in = jnp.arange(group_rows, dtype=jnp.int32)
    seg_ids = jnp.sum((where_in[:, None] >= seq_ends[None, :]).astype(jnp.int32), 1)
    starts = seq_ends - lengths
    chosen = (seg_ids[:, None] == jnp.arange(seq_count, dtype=jnp.int32)[None, :]).astype(jnp.int32)
    positions = where_in - jnp.sum(chosen * starts[None, :], 1)
    return (seg_ids, positions)


def dot(left, right):
    return jnp.dot(left, right, preferred_element_type=jnp.float32)


def dot_rows(left, right):
    return lax.dot_general(left, right, CONTRACT_ROWS, preferred_element_type=jnp.float32)


def dot_cols(left, right):
    return lax.dot_general(left, right, CONTRACT_COLS, preferred_element_type=jnp.float32)


def bit_of(index, bit):
    return lax.rem(lax.div(index, 1 << bit), 2)


def flip(index, bit):
    return index + (1 << bit) * (1 - 2 * bit_of(index, bit))


def plane_orders(replicas):
    far = list(range(1, replicas.bit_length() - 1))
    return far, far[1:] + far[:1]


def remote(src, dst, sems, at, device):
    return pltpu.make_async_remote_copy(
        src_ref=src,
        dst_ref=dst,
        send_sem=sems.at[(0,) + at],
        recv_sem=sems.at[(1,) + at],
        device_id=device,
        device_id_type=MESH,
    )


def greet(rep, place, replicas, shards_n):
    barrier = pltpu.get_barrier_semaphore()
    bits = replicas.bit_length() - 1
    for bit in range(bits):
        pl.semaphore_signal(
            barrier, inc=1, device_id={"replica": flip(rep, bit)}, device_id_type=MESH
        )
    for step in range(1, shards_n):
        pl.semaphore_signal(
            barrier,
            inc=1,
            device_id={"shard": lax.rem(place + step, shards_n)},
            device_id_type=MESH,
        )
    pl.semaphore_wait(barrier, bits + shards_n - 1)


def columns_kernel(
    replicas,
    shards_n,
    small_ref,
    up_ref,
    qkv_ref,
    small_out,
    up_out,
    qkv_out,
    own_sem,
    small_sem,
    turn_sem,
    plane_sem,
):
    rep, place = lax.axis_index("replica"), lax.axis_index("shard")
    bits = replicas.bit_length() - 1
    part, hidden = up_out.shape[1:]
    wide = qkv_out.shape[3]
    full = wide * shards_n
    rows = part // replicas
    orders = [order + [0] for order in plane_orders(replicas)]
    starts = []
    for order in orders:
        start = 0
        for level, bit in enumerate(order):
            start = start + bit_of(rep, bit) * (rows << level)
        starts.append(start)
    greet(rep, place, replicas, shards_n)

    def up_source(shard, path):
        return up_ref.at[
            pl.ds(starts[path], rows),
            pl.ds(pl.multiple_of(shard * hidden + path * (hidden // 2), 128), hidden // 2),
        ]

    def up_target(shard, start, count, path):
        return up_out.at[shard, pl.ds(start, count), pl.ds(path * (hidden // 2), hidden // 2)]

    def qkv_source(third, shard, path):
        return qkv_ref.at[
            pl.ds(starts[path], rows),
            pl.ds(
                pl.multiple_of(third * full + shard * wide + path * (wide // 2), 128), wide // 2
            ),
        ]

    def qkv_target(third, shard, start, count, path):
        return qkv_out.at[
            third, shard, pl.ds(start, count), pl.ds(path * (wide // 2), wide // 2)
        ]

    def source(thing, shard, path):
        return up_source(shard, path) if thing == 0 else qkv_source(thing - 1, shard, path)

    def target(thing, shard, start, count, path):
        if thing == 0:
            return up_target(shard, start, count, path)
        return qkv_target(thing - 1, shard, start, count, path)

    items = [(thing, step) for thing in range(4) for step in range(1, shards_n)]

    def turned(item, path, sending):
        thing, step = items[item]
        to = lax.rem(place + step, shards_n)
        shard = place if sending else lax.rem(place - step + shards_n, shards_n)
        return remote(
            source(thing, to, path),
            target(thing, shard, starts[path], rows, path),
            turn_sem,
            (item, path),
            {"shard": to},
        )

    def spread(item, path, level):
        thing, step = items[item]
        shard = lax.rem(place - step + shards_n, shards_n)
        order = orders[path]
        start = 0
        for above in range(level, bits):
            start = start + bit_of(rep, order[above]) * (rows << above)
        here = target(thing, shard, pl.multiple_of(start, rows), rows << level, path)
        return remote(
            here, here, plane_sem, (item, path, level), {"replica": flip(rep, order[level])}
        )

    def small_copy(step, sending):
        to = lax.rem(place + step, shards_n)
        shard = place if sending else lax.rem(place - step + shards_n, shards_n)
        return remote(small_ref, small_out.at[shard], small_sem, (step,), {"shard": to})

    for item in range(len(items)):
        for path in range(2):
            turned(item, path, True).start()
    for step in range(1, shards_n):
        small_copy(step, True).start()
    own = [
        pltpu.make_async_copy(small_ref, small_out.at[place], own_sem.at[0]),
        pltpu.make_async_copy(
            up_ref.at[:, pl.ds(pl.multiple_of(place * hidden, 128), hidden)],
            up_out.at[place],
            own_sem.at[1],
        ),
    ] + [
        pltpu.make_async_copy(
            qkv_ref.at[:, pl.ds(pl.multiple_of(third * full + place * wide, 128), wide)],
            qkv_out.at[third, place],
            own_sem.at[2 + third],
        )
        for third in range(3)
    ]
    for copy in own:
        copy.start()
    for tick in range(len(items) + bits):
        for level in reversed(range(bits + 1)):
            item = tick - level
            if not 0 <= item < len(items):
                continue
            for path in range(2):
                if level == 0:
                    turned(item, path, False).wait_recv()
                else:
                    spread(item, path, level - 1).wait_recv()
                if level < bits:
                    spread(item, path, level).start()
    for item in range(len(items)):
        for path in range(2):
            turned(item, path, True).wait_send()
            for level in range(bits):
                spread(item, path, level).wait_send()
    for step in range(1, shards_n):
        small_copy(step, False).wait()
    for copy in own:
        copy.wait()


def column_blocks(small, up_weight, qkv_weight):
    replicas, count = lax.axis_size("replica"), lax.axis_size("shard")
    bits = replicas.bit_length() - 1
    part = up_weight.shape[0]
    hidden, wide = up_weight.shape[1] // count, qkv_weight.shape[1] // (3 * count)
    items = 4 * (count - 1)
    any_spec = pl.BlockSpec(memory_space=pl.ANY)
    return pl.pallas_call(
        partial(columns_kernel, replicas, count),
        out_shape=(
            jax.ShapeDtypeStruct((count,) + small.shape, small.dtype),
            jax.ShapeDtypeStruct((count, part, hidden), jnp.bfloat16),
            jax.ShapeDtypeStruct((3, count, part, wide), jnp.bfloat16),
        ),
        in_specs=[any_spec] * 3,
        out_specs=(any_spec,) * 3,
        scratch_shapes=[
            pltpu.SemaphoreType.DMA((5,)),
            pltpu.SemaphoreType.DMA((2, count)),
            pltpu.SemaphoreType.DMA((2, items, 2)),
            pltpu.SemaphoreType.DMA((2, items, 2, bits)),
        ],
        compiler_params=pltpu.CompilerParams(collective_id=0, has_side_effects=True),
        cost_estimate=pl.CostEstimate(flops=0, bytes_accessed=200_000_000, transcendentals=0),
    )(small, up_weight, qkv_weight)


RING = 3
TILE = 256


def grads_kernel(
    replicas,
    shards_n,
    act_ref,
    up_ref,
    mixed_ref,
    mlp_ref,
    attn_ref,
    slope_ref,
    down_ref,
    proj_ref,
    heads_ref,
    rows_ref,
    cols_up_ref,
    cols_qkv_ref,
    tables_ref,
    first_ref,
    stats_ref,
    gains_ref,
    out_ref,
    vec_out,
    sum_out,
    work,
    from_core,
    *rest,
):
    rep, place = lax.axis_index("replica"), lax.axis_index("shard")
    bits = replicas.bit_length() - 1
    far = bits - 1
    from_far = rest[:far]
    (
        big,
        narrow,
        pre,
        joined,
        wide_rows,
        slope,
        heads,
        key_sum,
        value_sum,
        tile_x,
        tile_up,
        tile_qkv,
        shared,
        vec_got,
        vec_sum,
        load_sem,
        core_sem,
        far_sem,
        turn_sem,
        own_sem,
        plane_sem,
        vec_sem,
        sum_sem,
    ) = rest[far:]
    chunks, _, rows, cols = out_ref.shape
    slots = work.shape[0]
    half, side = rows // 2, cols // 2
    piece = rows // replicas
    orders = plane_orders(replicas)
    core = bit_of(rep, 0)
    tokens, width = up_ref.shape
    local = tokens // shards_n
    hiddens = pre.shape[0]
    natives = hiddens + 1
    mine = pl.multiple_of(core * half, half)
    theirs = pl.multiple_of((1 - core) * half, half)

    starts = []
    for order in orders:
        line, size = [core * half], half
        for bit in order:
            size //= 2
            line.append(line[-1] + bit_of(rep, bit) * size)
        starts.append(line)

    def spot(k):
        if k < natives:
            return k + hiddens
        return k - natives if k < natives + hiddens else k

    def load(source, target, number):
        return pltpu.make_async_copy(source, target, load_sem.at[number])

    def narrow_load(k):
        source = act_ref.at[:, pl.ds(k * cols, cols)] if k < hiddens else mixed_ref
        return load(source, narrow.at[k % 2], k % 2)

    def big_load(which):
        return load((up_ref, mlp_ref, attn_ref)[which], big.at[which % 2], 2 + which)

    def pre_loads(k):
        return [
            load(down_ref.at[pl.ds(k * cols, cols), :], wide_rows.at[k % 2], 5 + k % 2),
            load(slope_ref.at[:, pl.ds(k * cols, cols)], slope.at[k % 2], 7 + k % 2),
        ]

    def proj_load():
        return load(proj_ref, wide_rows.at[1], 6)

    def heads_load():
        return load(heads_ref, heads.at[pl.ds(0, 3)], 9)

    def tile_loads(j):
        some = pl.ds(j * TILE, TILE)
        return [
            load(rows_ref.at[:, some], tile_x.at[j % 2], 10 + j % 2),
            load(cols_up_ref.at[some, :], tile_up.at[j % 2], 12 + j % 2),
            load(cols_qkv_ref.at[:, some, :], tile_qkv.at[j % 2], 14 + j % 2),
        ]

    def to_core(k):
        return remote(
            work.at[k % slots, :, pl.ds(theirs, half), :],
            from_core.at[k % RING],
            core_sem,
            (0, k),
            {"replica": flip(rep, 0)},
        )

    def to_far(k, level, path):
        size = half >> (level + 1)
        bit = orders[path][level]
        start = starts[path][level] + (1 - bit_of(rep, bit)) * size
        return remote(
            work.at[k % slots, :, pl.ds(pl.multiple_of(start, size), size), pl.ds(path * side, side)],
            from_far[level].at[k % RING, path],
            far_sem,
            (k, level, path),
            {"replica": flip(rep, bit)},
        )

    def own_piece(k, path, block):
        return work.at[
            k % slots,
            block,
            pl.ds(pl.multiple_of(starts[path][far], piece), piece),
            pl.ds(path * side, side),
        ]

    def place_piece(k, path, block):
        return out_ref.at[
            spot(k),
            block,
            pl.ds(pl.multiple_of(starts[path][far], piece), piece),
            pl.ds(path * side, side),
        ]

    def settle(k, path):
        block = pl.ds(0, shards_n) if k < natives else place
        return pltpu.make_async_copy(
            own_piece(k, path, block), place_piece(k, path, block), own_sem.at[k % 2, path]
        )

    def turned(k, path, step, sending):
        to = lax.rem(place + step, shards_n)
        shard = place if sending else lax.rem(place - step + shards_n, shards_n)
        return remote(
            own_piece(k, path, to),
            place_piece(k, path, shard),
            turn_sem,
            (k - natives, path, step - 1),
            {"shard": to},
        )

    def spread(k, path, level):
        size = piece << level
        bit = orders[path][far - 1 - level]
        here = out_ref.at[
            spot(k),
            :,
            pl.ds(pl.multiple_of(starts[path][far - level], size), size),
            pl.ds(path * side, side),
        ]
        return remote(here, here, plane_sem, (k, level, path), {"replica": flip(rep, bit)})

    def spread_core(k):
        here = out_ref.at[spot(k), :, pl.ds(mine, half), :]
        return remote(here, here, core_sem, (1, k), {"replica": flip(rep, 0)})

    def put(offset, sums):
        for i in range(sums.shape[1] // 128):
            vec_sum[pl.ds(offset // 128 + i, 1), :] = sums[:, i * 128 : (i + 1) * 128]

    def compute(k):
        if k < natives:
            narrow_load(k).wait()
            if k + 1 < natives:
                narrow_load(k + 1).start()
        if k == 0:
            big_load(0).wait()
        if k == natives:
            big_load(1).wait()
            big_load(2).start()
        if k == natives + hiddens:
            big_load(2).wait()
        slot = k % slots
        which = 1 if natives <= k < natives + hiddens else 0

        for begin, send in ((theirs, True), (mine, False)):

            def block(g, carry):
                if k < natives:
                    left = narrow[k % 2, :, pl.ds(begin, half)]
                    right = big[which, :, pl.ds(pl.multiple_of(g * cols, cols), cols)]
                else:
                    left = big[which, :, pl.ds(pl.multiple_of(g * rows + begin, half), half)]
                    if k < natives + hiddens:
                        right = pre[k - natives]
                    else:
                        right = joined[k - natives - hiddens]
                work[slot, g, pl.ds(begin, half), :] = dot_rows(left, right).astype(jnp.bfloat16)
                return carry

            lax.fori_loop(0, shards_n, block, 0)
            if send:
                to_core(k).start()

    def add(k, start, size, left, width, got):
        def block(g, carry):
            where = (k % slots, g, pl.ds(pl.multiple_of(start, size), size), pl.ds(left, width))
            work[where] = (
                work[where].astype(jnp.float32) + got(g).astype(jnp.float32)
            ).astype(jnp.bfloat16)
            return carry

        lax.fori_loop(0, shards_n, block, 0)

    def grad_mixed():
        proj_load().wait()

        def block(i, carry):
            some = pl.ds(pl.multiple_of(i * TILE, TILE), TILE)
            heads[3, some, :] = dot_cols(big[0, some, :], wide_rows[1]).astype(jnp.bfloat16)
            return carry

        lax.fori_loop(0, tokens // TILE, block, 0)
        pre_loads(1)[0].start()
        own = pl.ds(pl.multiple_of(place * cols, cols), cols)
        put(4 * width + place * cols, jnp.sum(big[0, :, own].astype(jnp.float32), 0, keepdims=True))

    def grad_pre(k):
        for copy in pre_loads(k):
            copy.wait()

        def block(i, total):
            some = pl.ds(pl.multiple_of(i * TILE, TILE), TILE)
            found = dot_cols(big[0, some, :], wide_rows[k % 2]) * slope[k % 2, some, :].astype(
                jnp.float32
            )
            low = found.astype(jnp.bfloat16)
            pre[k, some, :] = low
            return total + jnp.sum(low.astype(jnp.float32), 0, keepdims=True)

        total = lax.fori_loop(0, tokens // TILE, block, jnp.zeros((1, cols), jnp.float32))
        put(8 * width + (place * hiddens + k) * cols, total)
        if k + 2 < hiddens:
            for copy in pre_loads(k + 2):
                copy.start()

    def turn_rows(found, some):
        lead = found[:, :128]
        lead = (
            lead * tables_ref[0, some, :]
            + pltpu.roll(lead, 96, 1) * tables_ref[1, some, :]
            - pltpu.roll(lead, 32, 1) * tables_ref[2, some, :]
        )
        return jnp.concatenate([lead, found[:, 128:]], 1)

    def attention(head):
        lanes = pl.ds(head * HEAD, HEAD)
        scale = 1.0 / math.sqrt(HEAD)
        key_sum[...] = jnp.zeros_like(key_sum)
        value_sum[...] = jnp.zeros_like(value_sum)
        sums = [jnp.zeros((1, HEAD), jnp.float32)] * 3
        for i in range(tokens // TILE):
            some, keys = pl.ds(i * TILE, TILE), pl.ds(0, (i + 1) * TILE)
            shape = (TILE, (i + 1) * TILE)
            query = heads[0, some, lanes]
            key = heads[1, keys, lanes]
            scores = dot_cols(query, key) * scale
            at = lax.broadcasted_iota(jnp.int32, shape, 1)
            upto = lax.broadcasted_iota(jnp.int32, shape, 0) + i * TILE
            scores = jnp.where((at >= first_ref[some, :]) & (at <= upto), scores, NEG_LARGE)
            shifted = jnp.exp(scores - jnp.max(scores, -1, keepdims=True))
            probs = shifted / jnp.sum(shifted, -1, keepdims=True)
            grad = heads[3, some, lanes]
            grad_probs = dot_cols(grad, heads[2, keys, lanes])
            delta = jnp.sum(probs * grad_probs, -1, keepdims=True)
            low = (probs * (grad_probs - delta)).astype(jnp.bfloat16)
            found = turn_rows(dot(low, key) * scale, some).astype(jnp.bfloat16)
            joined[0, some, lanes] = found
            sums[0] = sums[0] + jnp.sum(found.astype(jnp.float32), 0, keepdims=True)
            key_sum[keys, :] = key_sum[keys, :] + dot_rows(low, query)
            value_sum[keys, :] = value_sum[keys, :] + dot_rows(probs.astype(jnp.bfloat16), grad)
        for i in range(tokens // TILE):
            some = pl.ds(i * TILE, TILE)
            for third, found in (
                (1, turn_rows(key_sum[some, :] * scale, some)),
                (2, value_sum[some, :]),
            ):
                low = found.astype(jnp.bfloat16)
                joined[third, some, lanes] = low
                sums[third] = sums[third] + jnp.sum(low.astype(jnp.float32), 0, keepdims=True)
        for third in range(3):
            put(5 * width + third * width + place * cols + head * HEAD, sums[third])

    def sum_part(j, step, sending):
        to = lax.rem(place + step, shards_n)
        shard = place if sending else lax.rem(place - step + shards_n, shards_n)
        some = pl.ds(j * TILE, TILE)
        source = shared.at[pl.ds(pl.multiple_of(to * local, local), local), some]
        if step == 0:
            return pltpu.make_async_copy(source, sum_out.at[place, :, some], sum_sem.at[0, j, 0])
        return remote(source, sum_out.at[shard, :, some], sum_sem, (j, step), {"shard": to})

    def tile(j):
        for copy in tile_loads(j):
            copy.wait()
        if j + 1 < width // TILE:
            for copy in tile_loads(j + 1):
                copy.start()
        lanes = pl.ds(j * TILE, TILE)

        def block(i, totals):
            some = pl.ds(pl.multiple_of(i * local, local), local)
            normed = (tile_x[j % 2, some, :].astype(jnp.float32) - stats_ref[0, some, :]) * stats_ref[
                1, some, :
            ]
            mlp = sum(
                dot_cols(pre[k, some, :], tile_up[j % 2, :, k * cols : (k + 1) * cols])
                for k in range(hiddens)
            )
            attn = sum(dot_cols(joined[p, some, :], tile_qkv[j % 2, p]) for p in range(3))
            shared[some, lanes] = (
                attn * gains_ref[0:1, lanes] + mlp * gains_ref[1:2, lanes]
            ).astype(jnp.bfloat16)
            found = (attn * normed, attn, mlp * normed, mlp)
            return tuple(t + jnp.sum(f, 0, keepdims=True) for t, f in zip(totals, found))

        zero = jnp.zeros((1, TILE), jnp.float32)
        totals = lax.fori_loop(0, shards_n, block, (zero,) * 4)
        for number, total in enumerate(totals):
            put(number * width + j * TILE, total)
        for step in range(shards_n):
            sum_part(j, step, True).start()

    def stage(k, number):
        if number == 0:
            compute(k)
        elif number == 1:
            to_core(k).wait()
            add(k, mine, half, 0, cols, lambda g: from_core[k % RING, g])
            for path in range(2):
                to_far(k, 0, path).start()
        elif number <= 1 + far:
            level = number - 2
            for path in range(2):
                to_far(k, level, path).wait()
                size = half >> (level + 1)
                add(
                    k,
                    starts[path][level + 1],
                    size,
                    path * side,
                    side,
                    lambda g: from_far[level][k % RING, path, g],
                )
                if level + 1 < far:
                    to_far(k, level + 1, path).start()
                else:
                    if k >= natives:
                        for step in range(1, shards_n):
                            turned(k, path, step, True).start()
                    settle(k, path).start()
        elif number == 2 + far:
            for path in range(2):
                settle(k, path).wait()
                if k >= natives:
                    for step in range(1, shards_n):
                        turned(k, path, step, False).wait_recv()
                spread(k, path, 0).start()
            if k >= natives:
                for path in range(2):
                    for step in range(1, shards_n):
                        turned(k, path, step, True).wait_send()
        elif number <= 2 + 2 * far:
            level = number - 3 - far
            for path in range(2):
                spread(k, path, level).wait()
                if level + 1 < far:
                    spread(k, path, level + 1).start()
            if level + 1 == far:
                spread_core(k).start()
        else:
            spread_core(k).wait()

    stages = 4 + 2 * far
    n_heads, n_tiles = cols // HEAD, width // TILE
    extras = {0: [grad_mixed, lambda: grad_pre(0)]}
    for k in range(1, hiddens):
        extras.setdefault(k, []).append(partial(grad_pre, k))
    for head in range(n_heads):
        extras.setdefault(1 + head, []).append(partial(attention, head))
    tile_at = hiddens + 1
    for j in range(n_tiles):
        extras.setdefault(tile_at + j, []).append(partial(tile, j))
    vec_at = tile_at + n_tiles

    for copy in [narrow_load(0), big_load(0), proj_load()] + pre_loads(0):
        copy.start()
    pre_loads(1)[1].start()
    for copy in [heads_load(), big_load(1)] + tile_loads(0):
        copy.start()
    vec_sum[...] = jnp.zeros_like(vec_sum)
    greet(rep, place, replicas, shards_n)
    peers = [{"replica": flip(rep, bit)} for bit in range(bits)]
    peers += [{"shard": flip(place, bit)} for bit in range(shards_n.bit_length() - 1)]

    def vec_copy(number):
        return remote(vec_sum, vec_got.at[number], vec_sem, (number,), peers[number])

    for tick in range(max(chunks + stages - 1, vec_at + len(peers) + 1)):
        for number in reversed(range(stages)):
            if 0 <= tick - number < chunks:
                stage(tick - number, number)
        if tick == 1:
            heads_load().wait()
        for extra in extras.get(tick, []):
            extra()
        turn_of = tick - vec_at
        if 0 < turn_of <= len(peers):
            vec_copy(turn_of - 1).wait()
            vec_sum[...] = vec_sum[...] + vec_got[turn_of - 1]
        if 0 <= turn_of < len(peers):
            vec_copy(turn_of).start()
    vec_out[...] = vec_sum[...]
    for j in range(n_tiles):
        for step in range(shards_n):
            sum_part(j, step, False).wait()


def summed_grads(*operands):
    act, up, mixed, mlp_in = operands[:4]
    replicas, count = lax.axis_size("replica"), lax.axis_size("shard")
    bits = replicas.bit_length() - 1
    far = bits - 1
    tokens, width = up.shape
    cols = width // count
    hidden = act.shape[1]
    hiddens = hidden // cols
    natives = hiddens + 1
    chunks = natives + hiddens + 3
    peers = bits + count.bit_length() - 1
    slots = 2 + far
    vector = ((8 * width + count * hidden) // 128, 128)
    any_spec = pl.BlockSpec(memory_space=pl.ANY)
    vmem_spec = pl.BlockSpec(memory_space=pltpu.VMEM)
    low = lambda *shape: pltpu.VMEM(shape, jnp.bfloat16)
    full = lambda *shape: pltpu.VMEM(shape, jnp.float32)
    dma = lambda *shape: pltpu.SemaphoreType.DMA(shape)
    return pl.pallas_call(
        partial(grads_kernel, replicas, count),
        out_shape=(
            jax.ShapeDtypeStruct((chunks, count, cols, cols), jnp.bfloat16),
            jax.ShapeDtypeStruct(vector, jnp.float32),
            jax.ShapeDtypeStruct((count, tokens // count, width), jnp.bfloat16),
        ),
        in_specs=[any_spec] * 12 + [vmem_spec] * 4,
        out_specs=(any_spec, vmem_spec, any_spec),
        scratch_shapes=[
            low(slots, count, cols, cols),
            low(RING, count, cols // 2, cols),
        ]
        + [low(RING, 2, count, cols >> (level + 2), cols // 2) for level in range(far)]
        + [
            low(2, tokens, width),
            low(2, tokens, cols),
            low(hiddens, tokens, cols),
            low(3, tokens, cols),
            low(2, cols, width),
            low(2, tokens, cols),
            low(4, tokens, cols),
            full(tokens, HEAD),
            full(tokens, HEAD),
            low(2, tokens, TILE),
            low(2, TILE, hidden),
            low(2, 3, TILE, cols),
            low(tokens, width),
            full(peers, *vector),
            full(*vector),
            dma(16),
            dma(2, 2, chunks),
            dma(2, chunks, far, 2),
            dma(2, chunks - natives, 2, count - 1),
            dma(2, 2),
            dma(2, chunks, far, 2),
            dma(2, peers),
            dma(2, width // TILE, count),
        ],
        compiler_params=pltpu.CompilerParams(
            collective_id=1, has_side_effects=True, vmem_limit_bytes=60 * 2**20
        ),
        cost_estimate=pl.CostEstimate(
            flops=4 * tokens * chunks * count * cols * cols,
            bytes_accessed=600_000_000,
            transcendentals=0,
        ),
    )(*operands)


def widen_kernel(by_shard, in_ref, out_ref):
    number, count, _, cols = in_ref.shape
    for k in range(number):
        for g in range(count):
            at = (g * number + k if by_shard else k * count + g) * cols
            out_ref[:, at : at + cols] = in_ref[k, g].astype(jnp.float32)


def widen(blocks, first, number, down):
    count, rows, cols = blocks.shape[1:]
    some = 256 if down else 64
    if down:
        shape, depth = (number * rows, count * cols), 1
        grid = (number, rows // some)
        source = lambda k, i: (first + k, 0, i, 0)
        target = lambda k, i: (k * (rows // some) + i, 0)
    else:
        shape, depth = (rows, number * count * cols), number
        grid = (1, rows // some)
        source = lambda k, i: (first // number, 0, i, 0)
        target = lambda k, i: (i, 0)
    return pl.pallas_call(
        partial(widen_kernel, number != 3),
        out_shape=jax.ShapeDtypeStruct(shape, jnp.float32),
        grid=grid,
        in_specs=[pl.BlockSpec((depth, count, some, cols), source)],
        out_specs=pl.BlockSpec((some, shape[1]), target),
        compiler_params=pltpu.CompilerParams(vmem_limit_bytes=32 * 2**20),
    )(blocks)


def shards(
    layer_input,
    attn_gain,
    attn_shift,
    qkv_weight,
    qkv_bias,
    out_weight,
    out_bias,
    mlp_gain,
    mlp_shift,
    up_weight,
    up_bias,
    down_weight,
    down_bias,
    seq_lengths,
    upstream,
):
    local_rows = layer_input.shape[0]
    count = lax.axis_size("shard")
    group_rows = local_rows * count
    place = lax.axis_index("shard")
    heads = HEADS // count
    wide = heads * HEAD
    part = D // count
    hidden = up_bias.shape[0]
    score_scale = 1.0 / math.sqrt(HEAD)

    small = jnp.concatenate(
        [attn_gain, attn_shift, out_bias, mlp_gain, mlp_shift, down_bias, qkv_bias]
    )
    length = small.shape[0]
    small = jnp.pad(small, (0, -length % 2048)).reshape(16, -1)
    small_all, up_cols, qkv_cols = column_blocks(small, up_weight, qkv_weight)
    up_cols = up_cols.reshape(D, hidden)
    qkv_cols = qkv_cols.reshape(3, D, wide)
    small_all = small_all.reshape(count, -1)[:, :length].astype(jnp.float32)
    gain_a, shift_a, bias_o, gain_m, shift_m, bias_d = (
        small_all[:, i * part : (i + 1) * part].reshape(D) for i in range(6)
    )
    bias_j = lax.dynamic_index_in_dim(
        small_all[:, 6 * part :].reshape(3, count, wide), place, 1, keepdims=False
    )

    rows_all = lax.all_gather(layer_input, "shard", axis=0, tiled=True)
    upper, rows_all = lax.optimization_barrier((upstream, rows_all))
    up_all = lax.all_gather(upper, "shard", axis=0, tiled=True)

    seg_ids, positions = sequence_layout(seq_lengths[0], group_rows)
    key_index = jnp.arange(group_rows, dtype=jnp.int32)
    allowed = (seg_ids[:, None] == seg_ids[None, :]) & (key_index[None, :] <= key_index[:, None])
    cosine_table, sine_table = rotation_tables(positions)

    rows_all_f = rows_all.astype(jnp.float32)
    row_mean = jnp.mean(rows_all_f, -1, keepdims=True)
    normed, inverse_std_all = normalize(rows_all_f)
    mlp_in = (normed * gain_m + shift_m).astype(jnp.bfloat16)
    attn_in = (normed * gain_a + shift_a).astype(jnp.bfloat16)

    up_pre = dot(mlp_in, up_cols) + up_bias.astype(jnp.float32)
    cdf = 0.5 * (1.0 + lax.erf(up_pre * math.sqrt(0.5)))
    act_low = (up_pre * cdf).astype(jnp.bfloat16)
    slope = cdf + up_pre * jnp.exp(-0.5 * up_pre * up_pre) * (1.0 / math.sqrt(2.0 * math.pi))

    joined_q, joined_k, joined_v = (dot(attn_in, qkv_cols[i]) + bias_j[i] for i in range(3))
    queries = turn(joined_q.reshape(group_rows, heads, HEAD), cosine_table, sine_table).astype(
        jnp.bfloat16
    )
    keys = turn(joined_k.reshape(group_rows, heads, HEAD), cosine_table, sine_table).astype(
        jnp.bfloat16
    )
    values = joined_v.reshape(group_rows, heads, HEAD).astype(jnp.bfloat16)

    scores = (
        jnp.einsum("qhd,khd->hqk", queries, keys, preferred_element_type=jnp.float32) * score_scale
    )
    scores = jnp.where(allowed[None], scores, NEG_LARGE)
    row_max = jnp.max(scores, -1, keepdims=True)
    shifted = jnp.exp(scores - row_max)
    row_total = jnp.sum(shifted, -1, keepdims=True)
    attn_probs = shifted / row_total
    probs_low = attn_probs.astype(jnp.bfloat16)
    mixed = jnp.einsum("hqk,khd->qhd", probs_low, values, preferred_element_type=jnp.float32)
    mixed_low = mixed.reshape(group_rows, wide).astype(jnp.bfloat16)

    branch_sum = (dot(mixed_low, out_weight) + dot(act_low, down_weight)).astype(jnp.bfloat16)
    branch_own = lax.psum_scatter(branch_sum, "shard", scatter_dimension=0, tiled=True)
    rows_f = layer_input.astype(jnp.float32)
    grad_rows = upstream.astype(jnp.float32)
    heads_all = jnp.stack(
        [queries.reshape(group_rows, wide), keys.reshape(group_rows, wide), values.reshape(group_rows, wide)]
    )
    lane = jnp.arange(128, dtype=jnp.int32)[None, :]
    cosine_lanes = jnp.where(lane < ROT, jnp.tile(cosine_table, (1, 128 // ROT)), 1.0)
    sine_lanes = jnp.tile(sine_table, (1, 128 // ROT))
    tables = jnp.stack(
        [
            cosine_lanes,
            jnp.where(lane < ROT // 2, sine_lanes, 0.0),
            jnp.where((lane >= ROT // 2) & (lane < ROT), sine_lanes, 0.0),
        ]
    )
    grads, vector, normed_parts = summed_grads(
        act_low,
        up_all,
        mixed_low,
        mlp_in,
        attn_in,
        slope.astype(jnp.bfloat16),
        down_weight,
        out_weight,
        heads_all,
        rows_all,
        up_cols,
        qkv_cols,
        tables,
        (key_index - positions)[:, None],
        jnp.stack([row_mean, inverse_std_all]),
        jnp.stack([gain_a, gain_m]),
    )
    grads, branch_own = lax.optimization_barrier((grads, branch_own))
    vector = vector.reshape(-1)
    several = hidden // part
    down_grad = widen(grads, several, several, True)
    out_grad = widen(grads, 2 * several, 1, True)
    up_grad = widen(grads, 0, several, False)
    qkv_grad = widen(grads, 2 * several + 1, 3, False)
    layer_output = (rows_f + branch_own.astype(jnp.float32) + (bias_o + bias_d)).astype(jnp.bfloat16)
    normed_own, inverse_std = normalize(rows_f)
    input_grad = grad_rows + norm_backward(
        jnp.sum(normed_parts.astype(jnp.float32), 0), normed_own, inverse_std
    )
    own = lambda i: lax.dynamic_slice_in_dim(vector, i * D + place * part, part, 0)
    bias_grad = own(4)
    qkv_bias_grad = lax.dynamic_slice_in_dim(vector, 5 * D + place * 3 * part, 3 * part, 0)
    up_bias_grad = lax.dynamic_slice_in_dim(vector, 8 * D + place * hidden, hidden, 0)
    return (
        layer_output,
        input_grad,
        own(0),
        own(1),
        qkv_grad,
        qkv_bias_grad,
        out_grad,
        bias_grad,
        own(2),
        own(3),
        up_grad,
        up_bias_grad,
        down_grad,
        bias_grad,
    )


def solution(mesh):
    in_specs = (
        P(("replica", "shard"), None),
        P("shard"),
        P("shard"),
        P("shard", None),
        P("shard"),
        P("shard", None),
        P("shard"),
        P("shard"),
        P("shard"),
        P("shard", None),
        P("shard"),
        P("shard", None),
        P("shard"),
        P("replica", None),
        P(("replica", "shard"), None),
    )
    out_specs = (
        P(("replica", "shard"), None),
        P(("replica", "shard"), None),
        P("shard"),
        P("shard"),
        P("shard", None),
        P("shard"),
        P("shard", None),
        P("shard"),
        P("shard"),
        P("shard"),
        P("shard", None),
        P("shard"),
        P("shard", None),
        P("shard"),
    )
    return jax.shard_map(shards, mesh=mesh, in_specs=in_specs, out_specs=out_specs, check_vma=False)
```

time: 6160 us -> 562 us (0.09)
  waiting for transfers between devices: 5570 us -> 0.74 us
  Pallas kernels: 0 us -> 395 us
  blocking collectives: 192 us -> 0 us
  matrix products: 254 us -> 63.1 us
    unnamed x17 -> x3, waiting for transfers between devices: 2200 us -> 0.71 us
    all_gather x6 -> x2, waiting for transfers between devices: 1620 us -> 0.01 us  [the longest x1 0.01 us: shards(): rows_all = lax.all_gather(layer_input, 'shard', axis=0, tiled=True)]
    reduce_scatter x4 -> x1, waiting for transfers between devices: 1200 us -> 0.02 us  [shards(): lax.psum_scatter(branch_sum, 'shard', scatter_dimension=0, tiled=True)]
    psum x1 -> x0, waiting for transfers between devices: 548 us -> none  [shards(): lax.psum((attn_parts[0], attn_parts[1], attn_parts[2], attn_parts[3], att...]
    pallas_call x0 -> x6, Pallas kernels: none -> 395 us  [the longest x1 242 us: summed_grads(): pl.pallas_call(partial(grads_kernel, replicas, count), out_shape=(jax.Sha...]
    dot_general x18 -> x7, matrix products: 254 us -> 56.2 us  [the longest x6 51 us: dot(): return jnp.dot(left, right, preferred_element_type=jnp.float32)]
    all_gather x8 -> x0, blocking collectives: 167 us -> none  [the longest x1 42.1 us: fetch_mlp(): lax.all_gather(up_bias, 'shard', axis=0, tiled=True)]
  transfers between devices with their start and end apart: 14 -> 3, of which waited for: 13 -> 0; matrix products, arithmetic and copies ran while one was open for 5% -> 22% of each run, Pallas kernels for 0% -> 65%
where the time goes in v1:
time: 562 us; the launch traced here: 558 us
  Pallas kernels  395 us (70%)
  matrix products  63.1 us (11%)
  local copies, waits for them, and re-layouts  51 us (9%)
  other arithmetic  33.5 us (6%)
  between operations  14.6 us (3%)
    pallas_call x1, Pallas kernels, summed_grads(): pl.pallas_call(partial(grads_kernel, replicas, count), out_shape=(jax.Sha...  242 us
    pallas_call x1, Pallas kernels, column_blocks(): pl.pallas_call(partial(columns_kernel, replicas, count), out_shape=(jax.S...  120 us
    dot_general x6, matrix products, dot(): return jnp.dot(left, right, preferred_element_type=jnp.float32)  51 us
    pallas_call x4, Pallas kernels, widen(): pl.pallas_call(partial(widen_kernel, number != 3), out_shape=jax.ShapeDty...  32.9 us
    unnamed x87, local copies, waits for them, and re-layouts  21.1 us
  transfers between devices with their start and end apart: 3, of which 0 were waited for; matrix products, arithmetic and copies ran while one was open for 22% of the time, Pallas kernels for 65%

profile of v1, /device:TPU:0, one launch (start us, length us, event | category | flops | bytes accessed | tf_op | source)
XLA Modules:
  0.0 558.0 jit_solution(6903116142748170968)
XLA Ops:
  15.1 119.7 %shard_map.254 = (bf16[4,16,384]{2,1,0:T(8,128)(2,1)}, bf16[4,512,2048]{2,1,0:T(8,128)(2,1)}, bf16[3,4,512,512]{3,2,1,0:T(8,128)(2,1)}) custom-call(bf16[16,384]{1,0:T(8,128)(2,1)} %reshape.376.small_ref, bf16[512,8192]{1,0:T(8,128)(2,1)} %up_ref.1, bf16[512,6144]{1,0:T(8,128)(2,1)} %qkv_ref.1), custom_call_target="tpu_custom_call" | custom-call | bytes 200000000 | tf_op jit(solution)/shard_map/pallas_call | solution.py:273
  136.2 1.9 multiply_cosine_fusion
  142.6 1.6 fusion.19
  144.1 5.4 fusion.41
  149.5 3.0 convert_reduce_fusion.2
  154.2 4.5 fusion.8
  158.8 2.4 convolution_add_fusion
  162.8 2.4 convolution_add_fusion.1
  172.2 2.4 copy.120
  174.5 2.3 copy.118
  178.2 2.4 copy.116
  180.6 1.4 copy.123
  182.1 6.3 %add_convert_fusion.1 = bf16[1024,512]{1,0:T(8,128)(2,1)} fusion(bf16[1024,2048]{1,0:T(8,128)(2,1)} %copy-done.9, bf16[2048,512]{1,0:T(8,128)(2,1)} %bitcast.75, f32[512]{0:T(512)S(1)} %bitcast.102), kind=kOutput, calls=%fused_computation.50 | convolution fusion | flops 2148532224 | bytes 7342080 | tf_op jit(solution)/shard_map/dot_general | solution.py:79
  190.2 6.9 %fusion.45 = (f32[2,1024]{1,0:T(2,128)S(1)}, f32[2,1024,1024]{1,2,0:T(8,128)}) fusion(pred[1024,1024]{0,1:T(8,128)(4,1)} %fusion.19, bf16[1024,2,256]{2,0,1:T(8,128)(2,1)S(1)} %maximum_convert_fusion, bf16[1024,2,256]{2,0,1:T(8,128)(2,1)S(1)} %maximum_convert_fusion.1), kind=kOutput, calls=%fused_computation.106 | convolution fusion | flops 1082131456 | bytes 11542528 | tf_op jit(solution)/shard_map/sub | solution.py:916
  198.4 5.1 fusion.32
  203.6 26.6 %fusion.14 = (bf16[1024,2048]{1,0:T(8,128)(2,1)}, bf16[1024,2048]{1,0:T(8,128)(2,1)S(1)}) fusion(f32[2048]{0:T(1024)S(1)} %convert_element_type.102, bf16[1024,2048]{1,0:T(8,128)(2,1)S(1)} %copy-done.10, bf16[2048,2048]{1,0:T(8,128)(2,1)} %bitcast.108), kind=kOutput, calls=%fused_computation.19 | convolution fusion | flops 8615100416 | bytes 20979712 | tf_op jit(solution)/shard_map/dot_general | solution.py:79
  230.2 8.8 %fusion.46 = f32[1024,2048]{1,0:T(8,128)S(1)} fusion(bf16[1024,2048]{1,0:T(8,128)(2,1)S(1)} %get-tuple-element.37.act_ref, bf16[2048,2048]{1,0:T(8,128)(2,1)S(1)} %bitcast.107), kind=kOutput, calls=%fused_computation.107 | convolution fusion | flops 8589934592 | bytes 20971520 | tf_op jit(solution)/shard_map/dot_general | solution.py:79
  239.1 4.6 add_convert_fusion
  248.4 2.3 copy.115.mixed_ref
  250.6 2.1 copy.103
  253.8 2.9 convert_element_type.117
  256.8 1.5 convert_element_type.116
  259.7 3.5 pad_maximum_fusion.heads_ref
  263.3 242.4 %shard_map.255 = (bf16[12,4,512,512]{3,2,1,0:T(8,128)(2,1)}, f32[192,128]{1,0:T(8,128)}, bf16[4,256,2048]{2,1,0:T(8,128)(2,1)}) custom-call(bf16[1024,2048]{1,0:T(8,128)(2,1)} %copy-done.28, bf16[1024,2048]{1,0:T(8,128)(2,1)} %all-gather.5.cloned.1.call-done.up_ref, bf16[1024,512]{1,0:T(8,128)(2,1)} %copy.115.mixed_ref, ...), custom_call_target="tpu_custom_call" | custom-call | flops 51539607552 | bytes 600000000 | tf_op jit(solution)/shard_map/pallas_call | solution.py:758
  505.7 1.4 dynamic_slice.28
  508.4 1.4 fusion.44
  509.7 4.8 convert_reduce_fusion
  515.0 8.8 %shard_map.256 = f32[512,6144]{1,0:T(8,128)} custom-call(bf16[12,4,512,512]{3,2,1,0:T(8,128)(2,1)} %get-tuple-element.33.in_ref), custom_call_target="tpu_custom_call" | custom-call | tf_op jit(solution)/shard_map/pallas_call | solution.py:829
  523.8 3.4 shard_map.257
  527.2 10.3 %shard_map.258 = f32[512,8192]{1,0:T(8,128)} custom-call(bf16[12,4,512,512]{3,2,1,0:T(8,128)(2,1)} %get-tuple-element.33.in_ref), custom_call_target="tpu_custom_call" | custom-call | tf_op jit(solution)/shard_map/pallas_call | solution.py:829
  537.5 10.5 %shard_map.259 = f32[2048,2048]{1,0:T(8,128)} custom-call(bf16[12,4,512,512]{3,2,1,0:T(8,128)(2,1)} %get-tuple-element.33.in_ref), custom_call_target="tpu_custom_call" | custom-call | tf_op jit(solution)/shard_map/pallas_call | solution.py:829
  548.0 2.7 fusion.28
  (149 shorter events, 38.1 us)
Async XLA Ops:
  7.2 142.4 %all-gather.3.cloned.1.call-start = ((), (), s32[]{:S(2)}) async-start(), calls=%async_computation.1 | async-start | bytes 5242880 | tf_op jit(solution)/shard_map/all_gather | solution.py:882
  7.9 255.4 %all-gather.5.cloned.1.call-start = ((), (), s32[]{:S(2)}) async-start(), calls=%async_computation.2 | async-start | bytes 5242880 | tf_op jit(solution)/shard_map/all_gather | solution.py:884
  15.1 120.7 %copy-start.27 = (s32[1,4]{1,0:T(1,128)S(1)}, s32[1,4]{1,0:T(1,128)}, u32[]{:S(2)}) copy-start(s32[1,4]{1,0:T(1,128)} %param.28) | copy-start | bytes 52
  149.5 3.4 copy-start
  154.2 4.5 copy-start.20
  158.7 4.1 copy-start.9
  165.2 3.3 copy-start.23
  168.0 347.1 %reduce-scatter.2.cloned.1.call-start = ((), (), s32[]{:S(2)}) async-start(), calls=%async_computation.3 | async-start | bytes 5242880 | tf_op jit(solution)/shard_map/reduce_scatter | solution.py:924
  182.0 6.4 %copy-start.11 = (f32[1024,2,32]{2,0,1:T(8,128)S(1)}, f32[1024,2,32]{2,0,1:T(8,128)}, u32[]{:S(2)}) copy-start(f32[1024,2,32]{2,0,1:T(8,128)} %copy.122) | copy-start | bytes 786436
  182.0 6.4 %copy-start.12 = (f32[1024,2,32]{2,0,1:T(8,128)S(1)}, f32[1024,2,32]{2,0,1:T(8,128)}, u32[]{:S(2)}) copy-start(f32[1024,2,32]{2,0,1:T(8,128)} %copy.118) | copy-start | bytes 786436
  182.0 6.3 %copy-start.13 = (f32[1024,2,32]{2,0,1:T(8,128)S(1)}, f32[1024,2,32]{2,0,1:T(8,128)}, u32[]{:S(2)}) copy-start(f32[1024,2,32]{2,0,1:T(8,128)} %neg.15) | copy-start | bytes 786436
  182.0 6.3 %copy-start.14 = (f32[1024,2,64]{2,0,1:T(8,128)S(1)}, f32[1024,2,64]{2,0,1:T(8,128)}, u32[]{:S(2)}) copy-start(f32[1024,2,64]{2,0,1:T(8,128)} %copy.120) | copy-start | bytes 1572868
  182.1 6.3 %copy-start.15 = (f32[1024,2,32]{2,0,1:T(8,128)S(1)}, f32[1024,2,32]{2,0,1:T(8,128)}, u32[]{:S(2)}) copy-start(f32[1024,2,32]{2,0,1:T(8,128)} %neg.14) | copy-start | bytes 786436
  182.1 6.3 %copy-start.16 = (f32[1024,2,64]{2,0,1:T(8,128)S(1)}, f32[1024,2,64]{2,0,1:T(8,128)}, u32[]{:S(2)}) copy-start(f32[1024,2,64]{2,0,1:T(8,128)} %copy.116) | copy-start | bytes 1572868
  189.6 7.5 %copy-start.3 = (bf16[1024,2,256]{2,0,1:T(8,128)(2,1)}, bf16[1024,2,256]{2,0,1:T(8,128)(2,1)S(1)}, u32[]{:S(2)}) copy-start(bf16[1024,2,256]{2,0,1:T(8,128)(2,1)S(1)} %maximum_convert_fusion) | copy-start | bytes 3145732
  190.2 6.9 %copy-start.5 = (bf16[1024,2,256]{2,0,1:T(8,128)(2,1)}, bf16[1024,2,256]{2,0,1:T(8,128)(2,1)S(1)}, u32[]{:S(2)}) copy-start(bf16[1024,2,256]{2,0,1:T(8,128)(2,1)S(1)} %maximum_convert_fusion.1) | copy-start | bytes 3145732
  190.2 6.9 %copy-start.7 = (bf16[1024,512]{1,0:T(8,128)(2,1)S(1)}, bf16[1024,512]{1,0:T(8,128)(2,1)}, u32[]{:S(2)}) copy-start(bf16[1024,512]{1,0:T(8,128)(2,1)} %add_convert_fusion.1) | copy-start | bytes 3145732
  198.4 5.2 copy-start.10
  198.4 31.8 %slice-start = ((s8[8388608]{0:T(1024)(128)(4,1)}), s8[4194304]{0:T(1024)(128)(4,1)S(1)}, s32[]{:S(2)}) async-start(s8[8388608]{0:T(1024)(128)(4,1)} %bitcast.106), calls=%async_computation.4 | async-start | bytes 8388608
  203.6 35.5 %copy-start.22 = (bf16[2,256,1024]{2,1,0:T(8,128)(2,1)}, bf16[2,256,1024]{2,1,0:T(8,128)(2,1)S(1)}, u32[]{:S(2)}) copy-start(bf16[2,256,1024]{2,1,0:T(8,128)(2,1)S(1)} %fusion.32) | copy-start | bytes 3145732
  203.6 26.6 %slice-start.1 = ((s8[8388608]{0:T(1024)(128)(4,1)}), s8[4194304]{0:T(1024)(128)(4,1)S(1)}, s32[]{:S(2)}) async-start(s8[8388608]{0:T(1024)(128)(4,1)} %bitcast.106), calls=%async_computation.5 | async-start | bytes 8388608
  230.2 8.9 %copy-start.28 = (bf16[1024,2048]{1,0:T(8,128)(2,1)}, bf16[1024,2048]{1,0:T(8,128)(2,1)S(1)}, u32[]{:S(2)}) copy-start(bf16[1024,2048]{1,0:T(8,128)(2,1)S(1)} %get-tuple-element.37.act_ref) | copy-start | bytes 12582916
  230.2 8.9 %copy-start.26 = (bf16[512,2048]{1,0:T(8,128)(2,1)S(1)}, bf16[512,2048]{1,0:T(8,128)(2,1)}, u32[]{:S(2)}) copy-start(bf16[512,2048]{1,0:T(8,128)(2,1)} %proj_ref.1) | copy-start | bytes 6291460
  243.7 2.5 copy-start.1
  243.7 3.8 copy-start.17
  245.0 5.7 %copy-start.6 = (bf16[1024,2,256]{2,0,1:T(8,128)(2,1)S(1)}, bf16[1024,2,256]{2,0,1:T(8,128)(2,1)}, u32[]{:S(2)}) copy-start(bf16[1024,2,256]{2,0,1:T(8,128)(2,1)} %copy-done.5) | copy-start | bytes 3145732
  246.2 6.5 %copy-start.4 = (bf16[1024,2,256]{2,0,1:T(8,128)(2,1)S(1)}, bf16[1024,2,256]{2,0,1:T(8,128)(2,1)}, u32[]{:S(2)}) copy-start(bf16[1024,2,256]{2,0,1:T(8,128)(2,1)} %copy-done.3) | copy-start | bytes 3145732
  253.8 5.9 %copy-start.8 = (bf16[1024,512]{1,0:T(8,128)(2,1)S(1)}, bf16[1024,512]{1,0:T(8,128)(2,1)}, u32[]{:S(2)}) copy-start(bf16[1024,512]{1,0:T(8,128)(2,1)} %add_convert_fusion.1) | copy-start | bytes 3145732
  509.7 40.9 %copy-start.25 = (f32[512]{0:T(512)}, f32[512]{0:T(512)S(1)}, u32[]{:S(2)}) copy-start(f32[512]{0:T(512)S(1)} %get-tuple-element.103) | copy-start | bytes 6148
  537.5 10.5 %copy-start.2 = (bf16[256,2048]{1,0:T(8,128)(2,1)S(1)}, bf16[256,2048]{1,0:T(8,128)(2,1)}, u32[]{:S(2)}) copy-start(bf16[256,2048]{1,0:T(8,128)(2,1)} %param.29) | copy-start | bytes 3145732
  537.5 10.5 %copy-start.21 = (bf16[256,2048]{1,0:T(8,128)(2,1)S(1)}, bf16[256,2048]{1,0:T(8,128)(2,1)}, u32[]{:S(2)}) copy-start(bf16[256,2048]{1,0:T(8,128)(2,1)} %reduce-scatter.2.cloned.1.call-done) | copy-start | bytes 3145732
  537.5 10.5 %copy-start.24 = (f32[1,4,4,128]{3,1,2,0:T(4,128)S(1)}, f32[1,4,4,128]{3,1,2,0:T(4,128)}, u32[]{:S(2)}) copy-start(f32[1,4,4,128]{3,1,2,0:T(4,128)} %copy.133) | copy-start | bytes 24580
  (2 other events, 2.2 us)
Sparse Core Ops, SparseCore 0:
  9.6 120.0 all-gather.2
  168.1 82.5 all-gather.4
  253.0 75.2 reduce-scatter.1

commit v2 on v1

--- a/solution.py
+++ b/solution.py
@@ -33,46 +33,6 @@
     mean_grad = jnp.mean(grad_normed, -1, keepdims=True)
     mean_cross = jnp.mean(grad_normed * normed, -1, keepdims=True)
     return (grad_normed - mean_grad - normed * mean_cross) * inverse_std
-
-
-def rotation_tables(positions):
-    exponent = jnp.arange(ROT // 2, dtype=jnp.float32) * (2.0 / ROT)
-    inv_freq = jnp.power(jnp.float32(ROPE_BASE), -exponent)
-    angles = positions.astype(jnp.float32)[:, None] * inv_freq[None, :]
-    cosine_table = jnp.cos(angles)
-    sine_table = jnp.sin(angles)
-    return (
-        jnp.concatenate([cosine_table, cosine_table], 1),
-        jnp.concatenate([sine_table, sine_table], 1),
-    )
-
-
-def turn(values, cosine_table, sine_table):
-    rotary = values[..., :ROT]
-    first_half = rotary[..., : ROT // 2]
-    second_half = rotary[..., ROT // 2 :]
-    swapped = jnp.concatenate([-second_half, first_half], -1)
-    turned = rotary * cosine_table[:, None, :] + swapped * sine_table[:, None, :]
-    return jnp.concatenate([turned, values[..., ROT:]], -1)
-
-
-def turn_back(values, cosine_table, sine_table):
-    rotary = values[..., :ROT]
-    scaled = rotary * sine_table[:, None, :]
-    swapped = jnp.concatenate([scaled[..., ROT // 2 :], -scaled[..., : ROT // 2]], -1)
-    turned = rotary * cosine_table[:, None, :] + swapped
-    return jnp.concatenate([turned, values[..., ROT:]], -1)
-
-
-def sequence_layout(lengths, group_rows):
-    seq_count = lengths.shape[0]
-    seq_ends = jnp.cumsum(lengths)
-    where_in = jnp.arange(group_rows, dtype=jnp.int32)
-    seg_ids = jnp.sum((where_in[:, None] >= seq_ends[None, :]).astype(jnp.int32), 1)
-    starts = seq_ends - lengths
-    chosen = (seg_ids[:, None] == jnp.arange(seq_count, dtype=jnp.int32)[None, :]).astype(jnp.int32)
-    positions = where_in - jnp.sum(chosen * starts[None, :], 1)
-    return (seg_ids, positions)
 
 
 def dot(left, right):
@@ -128,26 +88,77 @@
     pl.semaphore_wait(barrier, bits + shards_n - 1)
 
 
-def columns_kernel(
+TILE = 256
+
+
+def causal_probs(query, key, first, row):
+    shape = (query.shape[0], key.shape[0])
+    scores = dot_cols(query, key) * (1.0 / math.sqrt(HEAD))
+    at = lax.broadcasted_iota(jnp.int32, shape, 1)
+    upto = lax.broadcasted_iota(jnp.int32, shape, 0) + row
+    scores = jnp.where((at >= first) & (at <= upto), scores, NEG_LARGE)
+    shifted = jnp.exp(scores - jnp.max(scores, -1, keepdims=True))
+    return shifted / jnp.sum(shifted, -1, keepdims=True)
+
+
+def forward_kernel(
     replicas,
     shards_n,
     small_ref,
     up_ref,
     qkv_ref,
+    x_ref,
+    g_ref,
+    down_ref,
+    proj_ref,
+    bias_ref,
+    tables_ref,
+    first_ref,
     small_out,
     up_out,
     qkv_out,
+    x_out,
+    g_out,
+    mlp_out,
+    attn_out,
+    act_out,
+    slope_out,
+    heads_out,
+    mixed_out,
+    branch_out,
+    stats_out,
+    small_low,
+    small,
+    x_rows,
+    mlp,
+    attn,
+    up,
+    qkv,
+    act,
+    slope,
+    heads,
+    mixed,
+    down,
+    proj,
+    branch,
     own_sem,
+    load_sem,
+    keep_sem,
     small_sem,
     turn_sem,
     plane_sem,
+    hop_sem,
+    g_sem,
 ):
     rep, place = lax.axis_index("replica"), lax.axis_index("shard")
     bits = replicas.bit_length() - 1
-    part, hidden = up_out.shape[1:]
-    wide = qkv_out.shape[3]
-    full = wide * shards_n
+    width, hidden = up_out.shape
+    part = width // shards_n
+    wide = qkv_out.shape[2]
     rows = part // replicas
+    tokens = x_out.shape[0]
+    local = tokens // shards_n
+    cols = down.shape[2]
     orders = [order + [0] for order in plane_orders(replicas)]
     starts = []
     for order in orders:
@@ -155,39 +166,22 @@
         for level, bit in enumerate(order):
             start = start + bit_of(rep, bit) * (rows << level)
         starts.append(start)
-    greet(rep, place, replicas, shards_n)
-
-    def up_source(shard, path):
-        return up_ref.at[
-            pl.ds(starts[path], rows),
-            pl.ds(pl.multiple_of(shard * hidden + path * (hidden // 2), 128), hidden // 2),
-        ]
-
-    def up_target(shard, start, count, path):
-        return up_out.at[shard, pl.ds(start, count), pl.ds(path * (hidden // 2), hidden // 2)]
-
-    def qkv_source(third, shard, path):
-        return qkv_ref.at[
-            pl.ds(starts[path], rows),
-            pl.ds(
-                pl.multiple_of(third * full + shard * wide + path * (wide // 2), 128), wide // 2
-            ),
-        ]
-
-    def qkv_target(third, shard, start, count, path):
-        return qkv_out.at[
-            third, shard, pl.ds(start, count), pl.ds(path * (wide // 2), wide // 2)
-        ]
+
+    items = [(thing, step) for thing in range(4) for step in range(1, shards_n)]
 
     def source(thing, shard, path):
-        return up_source(shard, path) if thing == 0 else qkv_source(thing - 1, shard, path)
+        some = pl.ds(pl.multiple_of(starts[path], rows), rows)
+        if thing == 0:
+            at = shard * hidden + path * (hidden // 2)
+            return up_ref.at[some, pl.ds(pl.multiple_of(at, 128), hidden // 2)]
+        at = (thing - 1) * width + shard * wide + path * (wide // 2)
+        return qkv_ref.at[some, pl.ds(pl.multiple_of(at, 128), wide // 2)]
 
     def target(thing, shard, start, count, path):
+        some = pl.ds(pl.multiple_of(shard * part + start, rows), count)
         if thing == 0:
-            return up_target(shard, start, count, path)
-        return qkv_target(thing - 1, shard, start, count, path)
-
-    items = [(thing, step) for thing in range(4) for step in range(1, shards_n)]
+            return up_out.at[some, pl.ds(path * (hidden // 2), hidden // 2)]
+        return qkv_out.at[thing - 1, some, pl.ds(path * (wide // 2), wide // 2)]
 
     def turned(item, path, sending):
         thing, step = items[item]
@@ -208,7 +202,7 @@
         start = 0
         for above in range(level, bits):
             start = start + bit_of(rep, order[above]) * (rows << above)
-        here = target(thing, shard, pl.multiple_of(start, rows), rows << level, path)
+        here = target(thing, shard, start, rows << level, path)
         return remote(
             here, here, plane_sem, (item, path, level), {"replica": flip(rep, order[level])}
         )
@@ -218,29 +212,7 @@
         shard = place if sending else lax.rem(place - step + shards_n, shards_n)
         return remote(small_ref, small_out.at[shard], small_sem, (step,), {"shard": to})
 
-    for item in range(len(items)):
-        for path in range(2):
-            turned(item, path, True).start()
-    for step in range(1, shards_n):
-        small_copy(step, True).start()
-    own = [
-        pltpu.make_async_copy(small_ref, small_out.at[place], own_sem.at[0]),
-        pltpu.make_async_copy(
-            up_ref.at[:, pl.ds(pl.multiple_of(place * hidden, 128), hidden)],
-            up_out.at[place],
-            own_sem.at[1],
-        ),
-    ] + [
-        pltpu.make_async_copy(
-            qkv_ref.at[:, pl.ds(pl.multiple_of(third * full + place * wide, 128), wide)],
-            qkv_out.at[third, place],
-            own_sem.at[2 + third],
-        )
-        for third in range(3)
-    ]
-    for copy in own:
-        copy.start()
-    for tick in range(len(items) + bits):
+    def column_tick(tick):
         for level in reversed(range(bits + 1)):
             item = tick - level
             if not 0 <= item < len(items):
@@ -252,46 +224,341 @@
                     spread(item, path, level - 1).wait_recv()
                 if level < bits:
                     spread(item, path, level).start()
+
+    def block_rows(block):
+        return pl.ds(pl.multiple_of(block * local, local), local)
+
+    def hop(way, step, sending):
+        sign = 1 - 2 * way
+        block = place - sign * (step if sending else step + 1)
+        there = x_out.at[block_rows(block), :]
+        return remote(
+            x_ref if sending and step == 0 else there,
+            there,
+            hop_sem,
+            (way, step),
+            {"shard": lax.rem(place + sign + shards_n, shards_n)},
+        )
+
+    def upstream_copy(step, sending):
+        to = lax.rem(place + step, shards_n)
+        shard = place if sending else lax.rem(place - step + shards_n, shards_n)
+        return remote(g_ref, g_out.at[block_rows(shard), :], g_sem, (step,), {"shard": to})
+
+    def holds(way, step):
+        return place >= step if way == 0 else place + step < shards_n
+
+    def goes(way, step):
+        onward = place + 1 < shards_n if way == 0 else place >= 1
+        return holds(way, step) & onward
+
+    def send_hop(step):
+        for way in range(2):
+
+            @pl.when(goes(way, step))
+            def _():
+                hop(way, step, True).start()
+
+    def pass_on(step):
+        for way in range(2):
+
+            @pl.when(holds(way, step))
+            def _():
+                hop(way, step - 1, False).wait_recv()
+
+        if step + 1 < shards_n:
+            send_hop(step)
+
+    def load(number, src, dst):
+        return pltpu.make_async_copy(src, dst, load_sem.at[number])
+
+    def keep(number, src, dst):
+        return pltpu.make_async_copy(src, dst, keep_sem.at[number])
+
+    def norm(block, from_ref, slot):
+        copy = load(slot, from_ref, x_rows.at[slot])
+        copy.start()
+        copy.wait()
+
+        def some_rows(i, carry):
+            here = pl.ds(pl.multiple_of(i * 32, 32), 32)
+            there = pl.ds(pl.multiple_of(block * local + i * 32, 32), 32)
+            values = x_rows[slot, here, :].astype(jnp.float32)
+            mean = jnp.mean(values, -1, keepdims=True)
+            centered = values - mean
+            scale = lax.rsqrt(jnp.mean(centered * centered, -1, keepdims=True) + EPSILON)
+            stats_out[0, there, :] = mean
+            stats_out[1, there, :] = scale
+            normed = centered * scale
+            for z in range(shards_n):
+                lanes = slice(z * part, (z + 1) * part)
+                some = normed[:, lanes]
+                attn[there, lanes] = (some * small[z, 0:1, :] + small[z, 1:2, :]).astype(jnp.bfloat16)
+                mlp[there, lanes] = (some * small[z, 3:4, :] + small[z, 4:5, :]).astype(jnp.bfloat16)
+            return carry
+
+        lax.fori_loop(0, local // 32, some_rows, 0)
+
+    def hidden_units(block):
+        here = block_rows(block)
+
+        def some_cols(k, carry):
+            lanes = pl.ds(pl.multiple_of(k * cols, cols), cols)
+            found = dot(mlp[here, :], up[:, lanes]) + bias_ref[0:1, lanes]
+            cdf = 0.5 * (1.0 + lax.erf(found * math.sqrt(0.5)))
+            act[here, lanes] = (found * cdf).astype(jnp.bfloat16)
+            bell = jnp.exp(-0.5 * found * found) * (1.0 / math.sqrt(2.0 * math.pi))
+            slope[here, lanes] = (cdf + found * bell).astype(jnp.bfloat16)
+            return carry
+
+        lax.fori_loop(0, hidden // cols, some_cols, 0)
+
+    def on_step(step, todo):
+        for way in range(2):
+            if step == 0 and way == 1:
+                continue
+            block = place - (1 - 2 * way) * step
+
+            @pl.when(holds(way, step))
+            def _():
+                todo(block, way)
+
+    def project(third):
+        number = third * shards_n + place
+        bias = small[lax.div(number, 3), pl.ds(6 + lax.rem(number, 3), 1), :]
+
+        def some_rows(i, carry):
+            here = pl.ds(pl.multiple_of(i * TILE, TILE), TILE)
+            found = dot(attn[here, :], qkv[third]) + bias
+            for head in range(wide // HEAD):
+                mine = found[:, head * HEAD : (head + 1) * HEAD]
+                if third < 2:
+                    lead = mine[:, :128]
+                    lead = (
+                        lead * tables_ref[0, here, :]
+                        - pltpu.roll(lead, 96, 1) * tables_ref[1, here, :]
+                        + pltpu.roll(lead, 32, 1) * tables_ref[2, here, :]
+                    )
+                    mine = jnp.concatenate([lead, mine[:, 128:]], 1)
+                heads[third, here, head * HEAD : (head + 1) * HEAD] = mine.astype(jnp.bfloat16)
+            return carry
+
+        lax.fori_loop(0, tokens // TILE, some_rows, 0)
+
+    def attend(head):
+        lanes = slice(head * HEAD, (head + 1) * HEAD)
+        for i in range(tokens // TILE):
+            here, keys = slice(i * TILE, (i + 1) * TILE), slice(0, (i + 1) * TILE)
+            probs = causal_probs(heads[0, here, lanes], heads[1, keys, lanes], first_ref[here, :], i * TILE)
+            mixed[here, lanes] = dot(probs.astype(jnp.bfloat16), heads[2, keys, lanes]).astype(jnp.bfloat16)
+
+    def down_load(j):
+        return load(4 + j % 2, down_ref.at[:, pl.ds(j * cols, cols)], down.at[j % 2])
+
+    def branch_keep(j):
+        return keep(6 + j, branch.at[j % 2], branch_out.at[:, pl.ds(j * cols, cols)])
+
+    def branch_cols(j):
+        down_load(j).wait()
+        if j >= 2:
+            branch_keep(j - 2).wait()
+
+        def some_rows(i, carry):
+            here = pl.ds(pl.multiple_of(i * TILE, TILE), TILE)
+            found = dot(act[here, :], down[j % 2]) + dot(mixed[here, :], proj[:, j * cols : (j + 1) * cols])
+            branch[j % 2, here, :] = found.astype(jnp.bfloat16)
+            return carry
+
+        lax.fori_loop(0, tokens // TILE, some_rows, 0)
+        branch_keep(j).start()
+        if j + 2 < width // cols:
+            down_load(j + 2).start()
+
+    greet(rep, place, replicas, shards_n)
+    for step in range(1, shards_n):
+        small_copy(step, True).start()
+    send_hop(0)
+    for item in range(shards_n - 1):
+        for path in range(2):
+            turned(item, path, True).start()
+    own = [
+        (small_ref, small_out.at[place]),
+        (
+            up_ref.at[:, pl.ds(pl.multiple_of(place * hidden, 128), hidden)],
+            up_out.at[pl.ds(pl.multiple_of(place * part, part), part), :],
+        ),
+        (x_ref, x_out.at[block_rows(place), :]),
+        (g_ref, g_out.at[block_rows(place), :]),
+    ] + [
+        (
+            qkv_ref.at[:, pl.ds(pl.multiple_of(third * width + place * wide, 128), wide)],
+            qkv_out.at[third, pl.ds(pl.multiple_of(place * part, part), part), :],
+        )
+        for third in range(3)
+    ]
+    own = [pltpu.make_async_copy(src, dst, own_sem.at[i]) for i, (src, dst) in enumerate(own)]
+    for copy in own:
+        copy.start()
+    down_load(0).start()
+    down_load(1).start()
+    load_proj = load(6, proj_ref, proj)
+    load_proj.start()
+
+    for step in range(1, shards_n):
+        small_copy(step, False).wait()
+    own[0].wait()
+    load_small = load(0, small_out, small_low)
+    load_small.start()
+    load_small.wait()
+    small[...] = small_low[...].astype(jnp.float32)
+    on_step(0, lambda block, way: norm(block, x_ref, way))
+
+    load_up = load(2, up_out, up)
+    load_qkv = load(3, qkv_out, qkv)
+    ticks = list(range(len(items) + bits))
+
+    def some_ticks(number):
+        for tick in ticks[:number]:
+            column_tick(tick)
+        del ticks[:number]
+
+    def arrive(step):
+        pass_on(step)
+        if step == 1:
+            for item in range(shards_n - 1, len(items)):
+                for path in range(2):
+                    turned(item, path, True).start()
+        if step == max(shards_n - 2, 1):
+            for other in range(1, shards_n):
+                upstream_copy(other, True).start()
+        on_step(step, lambda block, way: norm(block, x_out.at[block_rows(block), :], way))
+
+    arrive(1)
+    some_ticks(shards_n - 1 + bits)
+    own[1].wait()
+    load_up.start()
+    for step in range(2, shards_n):
+        arrive(step)
+        some_ticks(2)
+        if step == 2:
+            load_up.wait()
+        on_step(step - 2, lambda block, way: hidden_units(block))
+    keeps = [keep(0, mlp, mlp_out), keep(1, attn, attn_out)]
+    keeps[0].start()
+    keeps[1].start()
+    for step in range(shards_n - 2, shards_n):
+        some_ticks(2)
+        on_step(step, lambda block, way: hidden_units(block))
+    some_ticks(len(ticks))
+    for copy in own[4:]:
+        copy.wait()
+    load_qkv.start()
+    keeps += [keep(2, act, act_out), keep(3, slope, slope_out)]
+    keeps[2].start()
+    keeps[3].start()
+    load_qkv.wait()
+    for third in range(3):
+        project(third)
+    keeps.append(keep(4, heads, heads_out))
+    keeps[4].start()
+    for head in range(wide // HEAD):
+        attend(head)
+    keeps.append(keep(5, mixed, mixed_out))
+    keeps[5].start()
+    load_proj.wait()
+    for j in range(width // cols):
+        branch_cols(j)
+    for step in range(1, shards_n):
+        upstream_copy(step, False).wait()
+    for j in range(max(width // cols - 2, 0), width // cols):
+        branch_keep(j).wait()
+    for copy in keeps:
+        copy.wait()
     for item in range(len(items)):
         for path in range(2):
             turned(item, path, True).wait_send()
             for level in range(bits):
                 spread(item, path, level).wait_send()
-    for step in range(1, shards_n):
-        small_copy(step, False).wait()
-    for copy in own:
+    for step in range(shards_n - 1):
+        for way in range(2):
+
+            @pl.when(goes(way, step))
+            def _():
+                hop(way, step, True).wait_send()
+
+    for copy in own[2:4]:
         copy.wait()
 
 
-def column_blocks(small, up_weight, qkv_weight):
+def forward(small, up_weight, qkv_weight, x, g, down_weight, proj_weight, bias, tables, first):
     replicas, count = lax.axis_size("replica"), lax.axis_size("shard")
     bits = replicas.bit_length() - 1
-    part = up_weight.shape[0]
-    hidden, wide = up_weight.shape[1] // count, qkv_weight.shape[1] // (3 * count)
+    local, width = x.shape
+    tokens = local * count
+    hidden, wide = up_weight.shape[1] // count, width // count
+    cols = wide
     items = 4 * (count - 1)
     any_spec = pl.BlockSpec(memory_space=pl.ANY)
-    return pl.pallas_call(
-        partial(columns_kernel, replicas, count),
-        out_shape=(
-            jax.ShapeDtypeStruct((count,) + small.shape, small.dtype),
-            jax.ShapeDtypeStruct((count, part, hidden), jnp.bfloat16),
-            jax.ShapeDtypeStruct((3, count, part, wide), jnp.bfloat16),
+    vmem_spec = pl.BlockSpec(memory_space=pltpu.VMEM)
+    shapes = dict(
+        small=(count,) + small.shape,
+        up_cols=(width, hidden),
+        qkv_cols=(3, width, wide),
+        x=(tokens, width),
+        g=(tokens, width),
+        mlp_in=(tokens, width),
+        attn_in=(tokens, width),
+        act=(tokens, hidden),
+        slope=(tokens, hidden),
+        heads=(3, tokens, wide),
+        mixed=(tokens, wide),
+        branch=(tokens, width),
+    )
+    low = lambda *shape: pltpu.VMEM(shape, jnp.bfloat16)
+    dma = lambda *shape: pltpu.SemaphoreType.DMA(shape)
+    found = pl.pallas_call(
+        partial(forward_kernel, replicas, count),
+        out_shape=tuple(jax.ShapeDtypeStruct(shape, jnp.bfloat16) for shape in shapes.values())
+        + (jax.ShapeDtypeStruct((2, tokens, 1), jnp.float32),),
+        in_specs=[any_spec] * 7 + [vmem_spec] * 3,
+        out_specs=(any_spec,) * len(shapes) + (vmem_spec,),
+        scratch_shapes=[
+            low(*shapes["small"]),
+            pltpu.VMEM(shapes["small"], jnp.float32),
+            low(2, local, width),
+            low(tokens, width),
+            low(tokens, width),
+            low(width, hidden),
+            low(3, width, wide),
+            low(tokens, hidden),
+            low(tokens, hidden),
+            low(3, tokens, wide),
+            low(tokens, wide),
+            low(2, hidden, cols),
+            low(wide, width),
+            low(2, tokens, cols),
+            dma(7),
+            dma(7),
+            dma(6 + width // cols),
+            dma(2, count),
+            dma(2, items, 2),
+            dma(2, items, 2, bits),
+            dma(2, 2, count - 1),
+            dma(2, count),
+        ],
+        compiler_params=pltpu.CompilerParams(
+            collective_id=0, has_side_effects=True, vmem_limit_bytes=58 * 2**20
         ),
-        in_specs=[any_spec] * 3,
-        out_specs=(any_spec,) * 3,
-        scratch_shapes=[
-            pltpu.SemaphoreType.DMA((5,)),
-            pltpu.SemaphoreType.DMA((2, count)),
-            pltpu.SemaphoreType.DMA((2, items, 2)),
-            pltpu.SemaphoreType.DMA((2, items, 2, bits)),
-        ],
-        compiler_params=pltpu.CompilerParams(collective_id=0, has_side_effects=True),
-        cost_estimate=pl.CostEstimate(flops=0, bytes_accessed=200_000_000, transcendentals=0),
-    )(small, up_weight, qkv_weight)
+        cost_estimate=pl.CostEstimate(
+            flops=2 * tokens * width * (hidden * 2 + wide * 4),
+            bytes_accessed=500_000_000,
+            transcendentals=0,
+        ),
+    )(small, up_weight, qkv_weight, x, g, down_weight, proj_weight, bias, tables, first)
+    return dict(zip(list(shapes) + ["stats"], found))
 
 
 RING = 3
-TILE = 256
 
 
 def grads_kernel(
@@ -312,7 +579,7 @@
     tables_ref,
     first_ref,
     stats_ref,
-    gains_ref,
+    small_ref,
     out_ref,
     vec_out,
     sum_out,
@@ -385,11 +652,14 @@
     def big_load(which):
         return load((up_ref, mlp_ref, attn_ref)[which], big.at[which % 2], 2 + which)
 
+    def down_load(k):
+        return load(down_ref.at[pl.ds(k * cols, cols), :], wide_rows.at[k % 2], 5 + k % 2)
+
+    def slope_load(k):
+        return load(slope_ref.at[:, pl.ds(k * cols, cols)], slope.at[k % 2], 7 + k % 2)
+
     def pre_loads(k):
-        return [
-            load(down_ref.at[pl.ds(k * cols, cols), :], wide_rows.at[k % 2], 5 + k % 2),
-            load(slope_ref.at[:, pl.ds(k * cols, cols)], slope.at[k % 2], 7 + k % 2),
-        ]
+        return [down_load(k), slope_load(k)]
 
     def proj_load():
         return load(proj_ref, wide_rows.at[1], 6)
@@ -531,7 +801,7 @@
             return carry
 
         lax.fori_loop(0, tokens // TILE, block, 0)
-        pre_loads(1)[0].start()
+        down_load(1).start()
         own = pl.ds(pl.multiple_of(place * cols, cols), cols)
         put(4 * width + place * cols, jnp.sum(big[0, :, own].astype(jnp.float32), 0, keepdims=True))
 
@@ -571,15 +841,9 @@
         sums = [jnp.zeros((1, HEAD), jnp.float32)] * 3
         for i in range(tokens // TILE):
             some, keys = pl.ds(i * TILE, TILE), pl.ds(0, (i + 1) * TILE)
-            shape = (TILE, (i + 1) * TILE)
             query = heads[0, some, lanes]
             key = heads[1, keys, lanes]
-            scores = dot_cols(query, key) * scale
-            at = lax.broadcasted_iota(jnp.int32, shape, 1)
-            upto = lax.broadcasted_iota(jnp.int32, shape, 0) + i * TILE
-            scores = jnp.where((at >= first_ref[some, :]) & (at <= upto), scores, NEG_LARGE)
-            shifted = jnp.exp(scores - jnp.max(scores, -1, keepdims=True))
-            probs = shifted / jnp.sum(shifted, -1, keepdims=True)
+            probs = causal_probs(query, key, first_ref[some, :], i * TILE)
             grad = heads[3, some, lanes]
             grad_probs = dot_cols(grad, heads[2, keys, lanes])
             delta = jnp.sum(probs * grad_probs, -1, keepdims=True)
@@ -617,6 +881,8 @@
             for copy in tile_loads(j + 1):
                 copy.start()
         lanes = pl.ds(j * TILE, TILE)
+        owner, begin = divmod(j * TILE, cols)
+        theirs_at = slice(begin, begin + TILE)
 
         def block(i, totals):
             some = pl.ds(pl.multiple_of(i * local, local), local)
@@ -629,7 +895,8 @@
             )
             attn = sum(dot_cols(joined[p, some, :], tile_qkv[j % 2, p]) for p in range(3))
             shared[some, lanes] = (
-                attn * gains_ref[0:1, lanes] + mlp * gains_ref[1:2, lanes]
+                attn * small_ref[owner, 0:1, theirs_at].astype(jnp.float32)
+                + mlp * small_ref[owner, 3:4, theirs_at].astype(jnp.float32)
             ).astype(jnp.bfloat16)
             found = (attn * normed, attn, mlp * normed, mlp)
             return tuple(t + jnp.sum(f, 0, keepdims=True) for t, f in zip(totals, found))
@@ -705,7 +972,7 @@
 
     for copy in [narrow_load(0), big_load(0), proj_load()] + pre_loads(0):
         copy.start()
-    pre_loads(1)[1].start()
+    slope_load(1).start()
     for copy in [heads_load(), big_load(1)] + tile_loads(0):
         copy.start()
     vec_sum[...] = jnp.zeros_like(vec_sum)
@@ -805,35 +1072,86 @@
     )(*operands)
 
 
-def widen_kernel(by_shard, in_ref, out_ref):
-    number, count, _, cols = in_ref.shape
-    for k in range(number):
-        for g in range(count):
-            at = (g * number + k if by_shard else k * count + g) * cols
-            out_ref[:, at : at + cols] = in_ref[k, g].astype(jnp.float32)
-
-
-def widen(blocks, first, number, down):
+def last_kernel(
+    up_blocks,
+    down_blocks,
+    out_blocks,
+    qkv_blocks,
+    parts_ref,
+    branch_ref,
+    x_ref,
+    g_ref,
+    small_ref,
+    layer_out,
+    input_out,
+    up_out,
+    down_out,
+    out_out,
+    qkv_out,
+):
+    number, count, _, cols = up_blocks.shape
+    for g in range(count):
+        lanes = slice(g * cols, (g + 1) * cols)
+        for k in range(number):
+            at = (g * number + k) * cols
+            up_out[:, at : at + cols] = up_blocks[k, g].astype(jnp.float32)
+        for k in range(3):
+            at = (k * count + g) * cols
+            qkv_out[:, at : at + cols] = qkv_blocks[k, g].astype(jnp.float32)
+        down_out[:, lanes] = down_blocks[0, g].astype(jnp.float32)
+        out_out[:, lanes] = out_blocks[0, g].astype(jnp.float32)
+    rows = x_ref[...].astype(jnp.float32)
+    normed, inverse_std = normalize(rows)
+    grad = sum(parts_ref[g].astype(jnp.float32) for g in range(count))
+    input_out[...] = g_ref[...].astype(jnp.float32) + norm_backward(grad, normed, inverse_std)
+    for g in range(count):
+        lanes = slice(g * cols, (g + 1) * cols)
+        bias = small_ref[g, 2:3, :].astype(jnp.float32) + small_ref[g, 5:6, :].astype(jnp.float32)
+        layer_out[:, lanes] = (
+            rows[:, lanes] + branch_ref[:, lanes].astype(jnp.float32) + bias
+        ).astype(jnp.bfloat16)
+
+
+def last(blocks, parts, branch, x, g, small):
     count, rows, cols = blocks.shape[1:]
-    some = 256 if down else 64
-    if down:
-        shape, depth = (number * rows, count * cols), 1
-        grid = (number, rows // some)
-        source = lambda k, i: (first + k, 0, i, 0)
-        target = lambda k, i: (k * (rows // some) + i, 0)
-    else:
-        shape, depth = (rows, number * count * cols), number
-        grid = (1, rows // some)
-        source = lambda k, i: (first // number, 0, i, 0)
-        target = lambda k, i: (i, 0)
+    number = (blocks.shape[0] - 4) // 2
+    local, width = x.shape
+    steps = local // 16
+    some, tall = rows // steps, number * rows // steps
+    turns = rows // tall
+    whole = lambda i: (i, 0)
     return pl.pallas_call(
-        partial(widen_kernel, number != 3),
-        out_shape=jax.ShapeDtypeStruct(shape, jnp.float32),
-        grid=grid,
-        in_specs=[pl.BlockSpec((depth, count, some, cols), source)],
-        out_specs=pl.BlockSpec((some, shape[1]), target),
-        compiler_params=pltpu.CompilerParams(vmem_limit_bytes=32 * 2**20),
-    )(blocks)
+        last_kernel,
+        out_shape=(
+            jax.ShapeDtypeStruct((local, width), jnp.bfloat16),
+            jax.ShapeDtypeStruct((local, width), jnp.float32),
+            jax.ShapeDtypeStruct((rows, number * width), jnp.float32),
+            jax.ShapeDtypeStruct((number * rows, width), jnp.float32),
+            jax.ShapeDtypeStruct((rows, width), jnp.float32),
+            jax.ShapeDtypeStruct((rows, 3 * width), jnp.float32),
+        ),
+        grid=(steps,),
+        in_specs=[
+            pl.BlockSpec((number, count, some, cols), lambda i: (0, 0, i, 0)),
+            pl.BlockSpec((1, count, tall, cols), lambda i: (number + i // turns, 0, i % turns, 0)),
+            pl.BlockSpec((1, count, some, cols), lambda i: (2 * number, 0, i, 0)),
+            pl.BlockSpec((3, count, some, cols), lambda i: ((2 * number + 1) // 3, 0, i, 0)),
+            pl.BlockSpec((count, 16, width), lambda i: (0, i, 0)),
+            pl.BlockSpec((16, width), whole),
+            pl.BlockSpec((16, width), whole),
+            pl.BlockSpec((16, width), whole),
+            pl.BlockSpec(small.shape, lambda i: (0, 0, 0)),
+        ],
+        out_specs=(
+            pl.BlockSpec((16, width), whole),
+            pl.BlockSpec((16, width), whole),
+            pl.BlockSpec((some, number * width), whole),
+            pl.BlockSpec((tall, width), whole),
+            pl.BlockSpec((some, width), whole),
+            pl.BlockSpec((some, 3 * width), whole),
+        ),
+        compiler_params=pltpu.CompilerParams(vmem_limit_bytes=40 * 2**20),
+    )(blocks, blocks, blocks, blocks, parts, branch, x, g, small)
 
 
 def shards(
@@ -857,115 +1175,67 @@
     count = lax.axis_size("shard")
     group_rows = local_rows * count
     place = lax.axis_index("shard")
-    heads = HEADS // count
-    wide = heads * HEAD
     part = D // count
     hidden = up_bias.shape[0]
-    score_scale = 1.0 / math.sqrt(HEAD)
-
-    small = jnp.concatenate(
-        [attn_gain, attn_shift, out_bias, mlp_gain, mlp_shift, down_bias, qkv_bias]
-    )
-    length = small.shape[0]
-    small = jnp.pad(small, (0, -length % 2048)).reshape(16, -1)
-    small_all, up_cols, qkv_cols = column_blocks(small, up_weight, qkv_weight)
-    up_cols = up_cols.reshape(D, hidden)
-    qkv_cols = qkv_cols.reshape(3, D, wide)
-    small_all = small_all.reshape(count, -1)[:, :length].astype(jnp.float32)
-    gain_a, shift_a, bias_o, gain_m, shift_m, bias_d = (
-        small_all[:, i * part : (i + 1) * part].reshape(D) for i in range(6)
-    )
-    bias_j = lax.dynamic_index_in_dim(
-        small_all[:, 6 * part :].reshape(3, count, wide), place, 1, keepdims=False
-    )
-
-    rows_all = lax.all_gather(layer_input, "shard", axis=0, tiled=True)
-    upper, rows_all = lax.optimization_barrier((upstream, rows_all))
-    up_all = lax.all_gather(upper, "shard", axis=0, tiled=True)
-
-    seg_ids, positions = sequence_layout(seq_lengths[0], group_rows)
-    key_index = jnp.arange(group_rows, dtype=jnp.int32)
-    allowed = (seg_ids[:, None] == seg_ids[None, :]) & (key_index[None, :] <= key_index[:, None])
-    cosine_table, sine_table = rotation_tables(positions)
-
-    rows_all_f = rows_all.astype(jnp.float32)
-    row_mean = jnp.mean(rows_all_f, -1, keepdims=True)
-    normed, inverse_std_all = normalize(rows_all_f)
-    mlp_in = (normed * gain_m + shift_m).astype(jnp.bfloat16)
-    attn_in = (normed * gain_a + shift_a).astype(jnp.bfloat16)
-
-    up_pre = dot(mlp_in, up_cols) + up_bias.astype(jnp.float32)
-    cdf = 0.5 * (1.0 + lax.erf(up_pre * math.sqrt(0.5)))
-    act_low = (up_pre * cdf).astype(jnp.bfloat16)
-    slope = cdf + up_pre * jnp.exp(-0.5 * up_pre * up_pre) * (1.0 / math.sqrt(2.0 * math.pi))
-
-    joined_q, joined_k, joined_v = (dot(attn_in, qkv_cols[i]) + bias_j[i] for i in range(3))
-    queries = turn(joined_q.reshape(group_rows, heads, HEAD), cosine_table, sine_table).astype(
-        jnp.bfloat16
-    )
-    keys = turn(joined_k.reshape(group_rows, heads, HEAD), cosine_table, sine_table).astype(
-        jnp.bfloat16
-    )
-    values = joined_v.reshape(group_rows, heads, HEAD).astype(jnp.bfloat16)
-
-    scores = (
-        jnp.einsum("qhd,khd->hqk", queries, keys, preferred_element_type=jnp.float32) * score_scale
-    )
-    scores = jnp.where(allowed[None], scores, NEG_LARGE)
-    row_max = jnp.max(scores, -1, keepdims=True)
-    shifted = jnp.exp(scores - row_max)
-    row_total = jnp.sum(shifted, -1, keepdims=True)
-    attn_probs = shifted / row_total
-    probs_low = attn_probs.astype(jnp.bfloat16)
-    mixed = jnp.einsum("hqk,khd->qhd", probs_low, values, preferred_element_type=jnp.float32)
-    mixed_low = mixed.reshape(group_rows, wide).astype(jnp.bfloat16)
-
-    branch_sum = (dot(mixed_low, out_weight) + dot(act_low, down_weight)).astype(jnp.bfloat16)
-    branch_own = lax.psum_scatter(branch_sum, "shard", scatter_dimension=0, tiled=True)
-    rows_f = layer_input.astype(jnp.float32)
-    grad_rows = upstream.astype(jnp.float32)
-    heads_all = jnp.stack(
-        [queries.reshape(group_rows, wide), keys.reshape(group_rows, wide), values.reshape(group_rows, wide)]
-    )
-    lane = jnp.arange(128, dtype=jnp.int32)[None, :]
-    cosine_lanes = jnp.where(lane < ROT, jnp.tile(cosine_table, (1, 128 // ROT)), 1.0)
-    sine_lanes = jnp.tile(sine_table, (1, 128 // ROT))
+
+    params = [attn_gain, attn_shift, out_bias, mlp_gain, mlp_shift, down_bias]
+    params += [qkv_bias[i * part : (i + 1) * part] for i in range(3)]
+    row = lax.broadcasted_iota(jnp.int32, (16, part), 0)
+    small = jnp.zeros((16, part), jnp.bfloat16)
+    for i, param in enumerate(params):
+        small = jnp.where(row == i, param[None], small)
+
+    token = lax.broadcasted_iota(jnp.int32, (group_rows, 1), 0)
+    first, end = jnp.zeros((group_rows, 1), jnp.int32), 0
+    for i in range(seq_lengths.shape[1]):
+        end = end + seq_lengths[0, i]
+        first = first + jnp.where(token >= end, seq_lengths[0, i], 0)
+    lane = lax.broadcasted_iota(jnp.int32, (1, 128), 1)
+    exponent = lax.rem(lane, ROT // 2).astype(jnp.float32) * (2.0 / ROT)
+    angles = (token - first).astype(jnp.float32) * jnp.power(jnp.float32(ROPE_BASE), -exponent)
+    cosine, sine = jnp.cos(angles), jnp.sin(angles)
     tables = jnp.stack(
         [
-            cosine_lanes,
-            jnp.where(lane < ROT // 2, sine_lanes, 0.0),
-            jnp.where((lane >= ROT // 2) & (lane < ROT), sine_lanes, 0.0),
+            jnp.where(lane < ROT, cosine, 1.0),
+            jnp.where(lane < ROT // 2, sine, 0.0),
+            jnp.where((lane >= ROT // 2) & (lane < ROT), sine, 0.0),
         ]
     )
-    grads, vector, normed_parts = summed_grads(
-        act_low,
-        up_all,
-        mixed_low,
-        mlp_in,
-        attn_in,
-        slope.astype(jnp.bfloat16),
+    known = forward(
+        small,
+        up_weight,
+        qkv_weight,
+        layer_input,
+        upstream,
         down_weight,
         out_weight,
-        heads_all,
-        rows_all,
-        up_cols,
-        qkv_cols,
+        up_bias.astype(jnp.float32)[None],
         tables,
-        (key_index - positions)[:, None],
-        jnp.stack([row_mean, inverse_std_all]),
-        jnp.stack([gain_a, gain_m]),
+        first,
+    )
+    branch_own = lax.psum_scatter(known["branch"], "shard", scatter_dimension=0, tiled=True)
+    grads, vector, normed_parts = summed_grads(
+        known["act"],
+        known["g"],
+        known["mixed"],
+        known["mlp_in"],
+        known["attn_in"],
+        known["slope"],
+        down_weight,
+        out_weight,
+        known["heads"],
+        known["x"],
+        known["up_cols"],
+        known["qkv_cols"],
+        tables,
+        first,
+        known["stats"],
+        known["small"],
     )
     grads, branch_own = lax.optimization_barrier((grads, branch_own))
     vector = vector.reshape(-1)
-    several = hidden // part
-    down_grad = widen(grads, several, several, True)
-    out_grad = widen(grads, 2 * several, 1, True)
-    up_grad = widen(grads, 0, several, False)
-    qkv_grad = widen(grads, 2 * several + 1, 3, False)
-    layer_output = (rows_f + branch_own.astype(jnp.float32) + (bias_o + bias_d)).astype(jnp.bfloat16)
-    normed_own, inverse_std = normalize(rows_f)
-    input_grad = grad_rows + norm_backward(
-        jnp.sum(normed_parts.astype(jnp.float32), 0), normed_own, inverse_std
+    layer_output, input_grad, up_grad, down_grad, out_grad, qkv_grad = last(
+        grads, normed_parts, branch_own, layer_input, upstream, known["small"]
     )
     own = lambda i: lax.dynamic_slice_in_dim(vector, i * D + place * part, part, 0)
     bias_grad = own(4)

time: 562 us -> 536 us (0.954)
  Pallas kernels: 395 us -> 489 us
  matrix products: 63.1 us -> 0 us
  local copies, waits for them, and re-layouts: 51 us -> 10.3 us
  other arithmetic: 33.5 us -> 11.4 us
    pallas_call x5 -> x2, Pallas kernels: 153 us -> 248 us  [the longest x1 220 us: forward(): pl.pallas_call(partial(forward_kernel, replicas, count), out_shape=tuple(...]
    dot_general x7 -> x0, matrix products: 56.2 us -> none  [the longest x6 51 us: dot(): return jnp.dot(left, right, preferred_element_type=jnp.float32)]
    unnamed x87 -> x25, local copies, waits for them, and re-layouts: 21.1 us -> 4.03 us
    convert_element_type x6 -> x0, local copies, waits for them, and re-layouts: 11.2 us -> none  [the longest x2 5.02 us: shards(): turn(joined_k.reshape(group_rows, heads, HEAD), cosine_table, sine_table)]
    reduce_sum x8 -> x0, other arithmetic: 10.2 us -> none  [the longest x1 4.77 us: norm_backward(): mean_grad = jnp.mean(grad_normed, -1, keepdims=True)]
    slice x9 -> x2, local copies, waits for them, and re-layouts: 9.81 us -> 2.16 us  [the longest x1 1.4 us: shards(): end = end + seq_lengths[0, i]]
    sub x1 -> x0, matrix products: 6.87 us -> none  [shards(): shifted = jnp.exp(scores - row_max)]
  transfers between devices with their start and end apart: 3 -> 1, of which waited for: 0 -> 0; matrix products, arithmetic and copies ran while one was open for 22% -> 1% of each run, Pallas kernels for 65% -> 46%
where the time goes in v2:
time: 536 us; the launch traced here: 528 us
  Pallas kernels  489 us (91%)
  between operations  17.3 us (3%)
  other arithmetic  11.4 us (2%)
  local copies, waits for them, and re-layouts  10.3 us (2%)
    pallas_call x1, Pallas kernels, summed_grads(): pl.pallas_call(partial(grads_kernel, replicas, count), out_shape=(jax.Sha...  240 us
    pallas_call x1, Pallas kernels, forward(): pl.pallas_call(partial(forward_kernel, replicas, count), out_shape=tuple(...  220 us
    pallas_call x1, Pallas kernels, last(): pl.pallas_call(last_kernel, out_shape=(jax.ShapeDtypeStruct((local, width...  27.6 us
  transfers between devices with their start and end apart: 1, of which 0 were waited for; matrix products, arithmetic and copies ran while one was open for 1% of the time, Pallas kernels for 46%

profile of v2, /device:TPU:0, one launch (start us, length us, event | category | flops | bytes accessed | tf_op | source)
XLA Modules:
  0.0 527.5 jit_solution(6917946076412909218)
XLA Ops:
  7.2 0.0 copy-start.11
  7.2 0.0 copy-start.10
  7.2 0.0 copy-start.9
  7.2 0.0 copy-start.8
  7.2 0.0 reduce-scatter.2.cloned.1.call-start
  7.4 1.4 fusion.5
  11.4 2.6 subtract_convert_fusion
  14.0 3.6 select_add_fusion.first_ref
  17.6 0.8 fusion.4
  18.3 1.3 broadcast_in_dim.142
  19.6 1.9 fusion.2
  21.6 1.2 pad_maximum_fusion.tables_ref
  22.8 0.0 copy-done.9
  22.8 0.7 select_select_fusion.small_ref
  23.5 220.5 %shard_map.254 = (bf16[4,16,512]{2,1,0:T(8,128)(2,1)}, bf16[2048,2048]{1,0:T(8,128)(2,1)}, bf16[3,2048,512]{2,1,0:T(8,128)(2,1)}, bf16[1024,2048]{1,0:T(8,128)(2...) custom-call(bf16[16,512]{1,0:T(8,128)(2,1)} %select_select_fusion.sm, ...), custom_call_target="tpu_custom_call" | custom-call | flops 25769803776 | bytes 500000000 | tf_op jit(solution)/shard_map/pallas_call | solution.py:519
  244.0 0.0 reduce-scatter.2.cloned.1.call-update
  244.0 0.0 copy-start.1
  244.1 0.0 copy-start.2
  244.1 240.4 %shard_map.255 = (bf16[12,4,512,512]{3,2,1,0:T(8,128)(2,1)}, f32[192,128]{1,0:T(8,128)}, bf16[4,256,2048]{2,1,0:T(8,128)(2,1)}) custom-call(bf16[1024,2048]{1,0:T(8,128)(2,1)} %get-tuple-element.38.act_ref, bf16[1024,2048]{1,0:T(8,128)(2,1)} %get-tuple-element.39.up_ref, bf16[1024,512]{1,0:T(8,128)(2,1)} %get-tuple-element.40.mixed_ref, ...), custom_call_target="tpu_custom_call" | custom-call | flops 51539607552 | bytes 600000000 | tf_op jit(solution)/shard_map/pallas_call | solution.py:1025
  484.5 1.4 dynamic_slice.23
  485.9 1.3 dynamic_slice.27
  487.2 1.4 fusion.3
  488.6 0.0 reduce-scatter.2.cloned.1.call-done.branch_ref
  488.6 0.0 copy-done.1
  488.6 0.0 copy-done.2
  488.6 0.0 copy-done.4
  488.6 0.0 copy-start
  488.6 2.2 copy-done
  490.8 1.2 copy-done.3
  492.0 27.6 %shard_map.256 = (bf16[256,2048]{1,0:T(8,128)(2,1)}, f32[256,2048]{1,0:T(8,128)}, f32[512,8192]{1,0:T(8,128)}, f32[2048,2048]{1,0:T(8,128)}, f32[512,2048]{1,0:T(8,128)}, /*index=5*/f32[512,6144]{1,0:T(8,128)}) custom-call(bf16[12,4,512,512]{3,2,1,0:T(8,128)(2,1)} %get-tuple-element.52.up_blocks.down_blocks.out_blocks.qkv_blocks, ...), custom_call_target="tpu_custom_call" | custom-call | tf_op jit(solution)/shard_map/pallas_call | solution.py:1123
  519.7 0.0 copy-done.5
  519.7 0.6 copy.30
  (18 shorter events, 0.1 us)
Async XLA Ops:
  7.2 15.6 %copy-start.11 = (bf16[512]{0:T(512)(128)(2,1)S(1)}, bf16[512]{0:T(512)(128)(2,1)}, u32[]{:S(2)}) copy-start(bf16[512]{0:T(512)(128)(2,1)} %param.27) | copy-start | bytes 3076
  7.2 15.6 %copy-start.10 = (bf16[512]{0:T(512)(128)(2,1)S(1)}, bf16[512]{0:T(512)(128)(2,1)}, u32[]{:S(2)}) copy-start(bf16[512]{0:T(512)(128)(2,1)} %param.23) | copy-start | bytes 3076
  7.2 15.6 %copy-start.9 = (bf16[512]{0:T(512)(128)(2,1)S(1)}, bf16[512]{0:T(512)(128)(2,1)}, u32[]{:S(2)}) copy-start(bf16[512]{0:T(512)(128)(2,1)} %param.22) | copy-start | bytes 3076
  7.2 15.6 %copy-start.8 = (bf16[512]{0:T(512)(128)(2,1)S(1)}, bf16[512]{0:T(512)(128)(2,1)}, u32[]{:S(2)}) copy-start(bf16[512]{0:T(512)(128)(2,1)} %param.21) | copy-start | bytes 3076
  7.2 15.6 %copy-start.7 = (bf16[512]{0:T(512)(128)(2,1)S(1)}, bf16[512]{0:T(512)(128)(2,1)}, u32[]{:S(2)}) copy-start(bf16[512]{0:T(512)(128)(2,1)} %param.17) | copy-start | bytes 3076
  7.2 15.6 %copy-start.6 = (bf16[512]{0:T(512)(128)(2,1)S(1)}, bf16[512]{0:T(512)(128)(2,1)}, u32[]{:S(2)}) copy-start(bf16[512]{0:T(512)(128)(2,1)} %param.16) | copy-start | bytes 3076
  7.2 481.3 %reduce-scatter.2.cloned.1.call-start = ((), (), s32[]{:S(2)}) async-start(), calls=%async_computation.1 | async-start | bytes 5242880 | tf_op jit(solution)/shard_map/reduce_scatter | solution.py:1216
  244.0 244.5 %copy-start.1 = (bf16[256,2048]{1,0:T(8,128)(2,1)S(1)}, bf16[256,2048]{1,0:T(8,128)(2,1)}, u32[]{:S(2)}) copy-start(bf16[256,2048]{1,0:T(8,128)(2,1)} %x_ref.3) | copy-start | bytes 3145732
  244.1 244.5 %copy-start.2 = (bf16[256,2048]{1,0:T(8,128)(2,1)S(1)}, bf16[256,2048]{1,0:T(8,128)(2,1)}, u32[]{:S(2)}) copy-start(bf16[256,2048]{1,0:T(8,128)(2,1)} %g_ref.3) | copy-start | bytes 3145732
  244.1 244.5 %copy-start.4 = (bf16[4,16,512]{2,1,0:T(8,128)(2,1)S(1)}, bf16[4,16,512]{2,1,0:T(8,128)(2,1)}, u32[]{:S(2)}) copy-start(bf16[4,16,512]{2,1,0:T(8,128)(2,1)} %get-tuple-element.49.small_ref) | copy-start | bytes 196612
  488.6 31.1 %copy-start.5 = (f32[512]{0:T(512)}, f32[512]{0:T(512)S(1)}, u32[]{:S(2)}) copy-start(f32[512]{0:T(512)S(1)} %get-tuple-element.114) | copy-start | bytes 6148
  488.6 2.2 copy-start
  490.8 1.2 copy-start.3
Sparse Core Ops, SparseCore 0:
  244.2 82.6 reduce-scatter.1

commit v3 on v2

--- a/solution.py
+++ b/solution.py
@@ -3,6 +3,7 @@
 
 import jax
 import jax.numpy as jnp
+import numpy as np
 from jax import lax
 from jax.experimental import pallas as pl
 from jax.experimental.pallas import tpu as pltpu
@@ -89,6 +90,7 @@
 
 
 TILE = 256
+TALL = 512
 
 
 def causal_probs(query, key, first, row):
@@ -112,8 +114,8 @@
     down_ref,
     proj_ref,
     bias_ref,
-    tables_ref,
-    first_ref,
+    frequency_ref,
+    lengths_ref,
     small_out,
     up_out,
     qkv_out,
@@ -127,6 +129,8 @@
     mixed_out,
     branch_out,
     stats_out,
+    tables_out,
+    first_out,
     small_low,
     small,
     x_rows,
@@ -167,33 +171,36 @@
             start = start + bit_of(rep, bit) * (rows << level)
         starts.append(start)
 
-    items = [(thing, step) for thing in range(4) for step in range(1, shards_n)]
-
-    def source(thing, shard, path):
+    items = [(thing, step) for thing in range(2) for step in range(1, shards_n)]
+
+    def source(third, shard, path):
         some = pl.ds(pl.multiple_of(starts[path], rows), rows)
-        if thing == 0:
+        if third is None:
             at = shard * hidden + path * (hidden // 2)
             return up_ref.at[some, pl.ds(pl.multiple_of(at, 128), hidden // 2)]
-        at = (thing - 1) * width + shard * wide + path * (wide // 2)
+        at = third * width + shard * wide + path * (wide // 2)
         return qkv_ref.at[some, pl.ds(pl.multiple_of(at, 128), wide // 2)]
 
-    def target(thing, shard, start, count, path):
+    def target(third, shard, start, count, path):
         some = pl.ds(pl.multiple_of(shard * part + start, rows), count)
-        if thing == 0:
+        if third is None:
             return up_out.at[some, pl.ds(path * (hidden // 2), hidden // 2)]
-        return qkv_out.at[thing - 1, some, pl.ds(path * (wide // 2), wide // 2)]
+        return qkv_out.at[third, some, pl.ds(path * (wide // 2), wide // 2)]
 
     def turned(item, path, sending):
         thing, step = items[item]
         to = lax.rem(place + step, shards_n)
         shard = place if sending else lax.rem(place - step + shards_n, shards_n)
-        return remote(
-            source(thing, to, path),
-            target(thing, shard, starts[path], rows, path),
-            turn_sem,
-            (item, path),
-            {"shard": to},
-        )
+        return [
+            remote(
+                source(third, to, path),
+                target(third, shard, starts[path], rows, path),
+                turn_sem,
+                (item, path, third or 0),
+                {"shard": to},
+            )
+            for third in (range(3) if thing else (None,))
+        ]
 
     def spread(item, path, level):
         thing, step = items[item]
@@ -202,7 +209,7 @@
         start = 0
         for above in range(level, bits):
             start = start + bit_of(rep, order[above]) * (rows << above)
-        here = target(thing, shard, start, rows << level, path)
+        here = target(pl.ds(0, 3) if thing else None, shard, start, rows << level, path)
         return remote(
             here, here, plane_sem, (item, path, level), {"replica": flip(rep, order[level])}
         )
@@ -219,7 +226,8 @@
                 continue
             for path in range(2):
                 if level == 0:
-                    turned(item, path, False).wait_recv()
+                    for copy in turned(item, path, False):
+                        copy.wait_recv()
                 else:
                     spread(item, path, level - 1).wait_recv()
                 if level < bits:
@@ -313,6 +321,24 @@
 
         lax.fori_loop(0, hidden // cols, some_cols, 0)
 
+    def tables(i, carry):
+        some = local // 2
+        here = pl.ds(pl.multiple_of(i * some, some), some)
+        token = lax.broadcasted_iota(jnp.int32, (some, 128), 0) + i * some
+        lane = lax.broadcasted_iota(jnp.int32, (some, 128), 1)
+        first, end = jnp.zeros((some, 128), jnp.int32), 0
+        for j in range(lengths_ref.shape[1]):
+            length = lengths_ref[0, j]
+            end = end + length
+            first = first + jnp.where(token >= end, length, 0)
+        first_out[here, :] = first[:, :1]
+        angles = (token - first).astype(jnp.float32) * frequency_ref[0:1, :]
+        sine = jnp.sin(angles)
+        tables_out[0, here, :] = jnp.where(lane < ROT, jnp.cos(angles), 1.0)
+        tables_out[1, here, :] = jnp.where(lane < ROT // 2, sine, 0.0)
+        tables_out[2, here, :] = jnp.where((lane >= ROT // 2) & (lane < ROT), sine, 0.0)
+        return carry
+
     def on_step(step, todo):
         for way in range(2):
             if step == 0 and way == 1:
@@ -328,28 +354,28 @@
         bias = small[lax.div(number, 3), pl.ds(6 + lax.rem(number, 3), 1), :]
 
         def some_rows(i, carry):
-            here = pl.ds(pl.multiple_of(i * TILE, TILE), TILE)
+            here = pl.ds(pl.multiple_of(i * TALL, TALL), TALL)
             found = dot(attn[here, :], qkv[third]) + bias
             for head in range(wide // HEAD):
                 mine = found[:, head * HEAD : (head + 1) * HEAD]
                 if third < 2:
                     lead = mine[:, :128]
                     lead = (
-                        lead * tables_ref[0, here, :]
-                        - pltpu.roll(lead, 96, 1) * tables_ref[1, here, :]
-                        + pltpu.roll(lead, 32, 1) * tables_ref[2, here, :]
+                        lead * tables_out[0, here, :]
+                        - pltpu.roll(lead, 96, 1) * tables_out[1, here, :]
+                        + pltpu.roll(lead, 32, 1) * tables_out[2, here, :]
                     )
                     mine = jnp.concatenate([lead, mine[:, 128:]], 1)
                 heads[third, here, head * HEAD : (head + 1) * HEAD] = mine.astype(jnp.bfloat16)
             return carry
 
-        lax.fori_loop(0, tokens // TILE, some_rows, 0)
+        lax.fori_loop(0, tokens // TALL, some_rows, 0)
 
     def attend(head):
         lanes = slice(head * HEAD, (head + 1) * HEAD)
         for i in range(tokens // TILE):
             here, keys = slice(i * TILE, (i + 1) * TILE), slice(0, (i + 1) * TILE)
-            probs = causal_probs(heads[0, here, lanes], heads[1, keys, lanes], first_ref[here, :], i * TILE)
+            probs = causal_probs(heads[0, here, lanes], heads[1, keys, lanes], first_out[here, :], i * TILE)
             mixed[here, lanes] = dot(probs.astype(jnp.bfloat16), heads[2, keys, lanes]).astype(jnp.bfloat16)
 
     def down_load(j):
@@ -364,12 +390,12 @@
             branch_keep(j - 2).wait()
 
         def some_rows(i, carry):
-            here = pl.ds(pl.multiple_of(i * TILE, TILE), TILE)
+            here = pl.ds(pl.multiple_of(i * TALL, TALL), TALL)
             found = dot(act[here, :], down[j % 2]) + dot(mixed[here, :], proj[:, j * cols : (j + 1) * cols])
             branch[j % 2, here, :] = found.astype(jnp.bfloat16)
             return carry
 
-        lax.fori_loop(0, tokens // TILE, some_rows, 0)
+        lax.fori_loop(0, tokens // TALL, some_rows, 0)
         branch_keep(j).start()
         if j + 2 < width // cols:
             down_load(j + 2).start()
@@ -377,10 +403,11 @@
     greet(rep, place, replicas, shards_n)
     for step in range(1, shards_n):
         small_copy(step, True).start()
-    send_hop(0)
     for item in range(shards_n - 1):
         for path in range(2):
-            turned(item, path, True).start()
+            for copy in turned(item, path, True):
+                copy.start()
+    send_hop(0)
     own = [
         (small_ref, small_out.at[place]),
         (
@@ -404,6 +431,7 @@
     load_proj = load(6, proj_ref, proj)
     load_proj.start()
 
+    lax.fori_loop(0, 2 * shards_n, tables, 0)
     for step in range(1, shards_n):
         small_copy(step, False).wait()
     own[0].wait()
@@ -427,32 +455,40 @@
         if step == 1:
             for item in range(shards_n - 1, len(items)):
                 for path in range(2):
-                    turned(item, path, True).start()
-        if step == max(shards_n - 2, 1):
-            for other in range(1, shards_n):
-                upstream_copy(other, True).start()
+                    for copy in turned(item, path, True):
+                        copy.start()
         on_step(step, lambda block, way: norm(block, x_out.at[block_rows(block), :], way))
 
+    some_ticks(3)
     arrive(1)
-    some_ticks(shards_n - 1 + bits)
+    some_ticks(shards_n - 1 + bits - 3)
     own[1].wait()
     load_up.start()
-    for step in range(2, shards_n):
+    load_up.wait()
+    on_step(0, lambda block, way: hidden_units(block))
+    for step in range(2, shards_n - 1):
         arrive(step)
-        some_ticks(2)
-        if step == 2:
-            load_up.wait()
-        on_step(step - 2, lambda block, way: hidden_units(block))
+    some_ticks(1)
+    on_step(1, lambda block, way: hidden_units(block))
+    some_ticks(1)
+    for way in range(2):
+
+        @pl.when(goes(way, shards_n - 2))
+        def _():
+            hop(way, shards_n - 2, True).wait_send()
+
+    for other in range(1, shards_n):
+        upstream_copy(other, True).start()
+    some_ticks(len(ticks))
+    arrive(shards_n - 1)
     keeps = [keep(0, mlp, mlp_out), keep(1, attn, attn_out)]
     keeps[0].start()
     keeps[1].start()
-    for step in range(shards_n - 2, shards_n):
-        some_ticks(2)
-        on_step(step, lambda block, way: hidden_units(block))
-    some_ticks(len(ticks))
     for copy in own[4:]:
         copy.wait()
     load_qkv.start()
+    for step in range(2, shards_n):
+        on_step(step, lambda block, way: hidden_units(block))
     keeps += [keep(2, act, act_out), keep(3, slope, slope_out)]
     keeps[2].start()
     keeps[3].start()
@@ -476,10 +512,11 @@
         copy.wait()
     for item in range(len(items)):
         for path in range(2):
-            turned(item, path, True).wait_send()
+            for copy in turned(item, path, True):
+                copy.wait_send()
             for level in range(bits):
                 spread(item, path, level).wait_send()
-    for step in range(shards_n - 1):
+    for step in range(shards_n - 2):
         for way in range(2):
 
             @pl.when(goes(way, step))
@@ -490,14 +527,14 @@
         copy.wait()
 
 
-def forward(small, up_weight, qkv_weight, x, g, down_weight, proj_weight, bias, tables, first):
+def forward(small, up_weight, qkv_weight, x, g, down_weight, proj_weight, bias, frequency, lengths):
     replicas, count = lax.axis_size("replica"), lax.axis_size("shard")
     bits = replicas.bit_length() - 1
     local, width = x.shape
     tokens = local * count
     hidden, wide = up_weight.shape[1] // count, width // count
     cols = wide
-    items = 4 * (count - 1)
+    items = 2 * (count - 1)
     any_spec = pl.BlockSpec(memory_space=pl.ANY)
     vmem_spec = pl.BlockSpec(memory_space=pltpu.VMEM)
     shapes = dict(
@@ -519,9 +556,13 @@
     found = pl.pallas_call(
         partial(forward_kernel, replicas, count),
         out_shape=tuple(jax.ShapeDtypeStruct(shape, jnp.bfloat16) for shape in shapes.values())
-        + (jax.ShapeDtypeStruct((2, tokens, 1), jnp.float32),),
-        in_specs=[any_spec] * 7 + [vmem_spec] * 3,
-        out_specs=(any_spec,) * len(shapes) + (vmem_spec,),
+        + (
+            jax.ShapeDtypeStruct((2, tokens, 1), jnp.float32),
+            jax.ShapeDtypeStruct((3, tokens, 128), jnp.float32),
+            jax.ShapeDtypeStruct((tokens, 1), jnp.int32),
+        ),
+        in_specs=[any_spec] * 7 + [vmem_spec] * 2 + [pl.BlockSpec(memory_space=pltpu.SMEM)],
+        out_specs=(any_spec,) * len(shapes) + (vmem_spec,) * 3,
         scratch_shapes=[
             low(*shapes["small"]),
             pltpu.VMEM(shapes["small"], jnp.float32),
@@ -541,7 +582,7 @@
             dma(7),
             dma(6 + width // cols),
             dma(2, count),
-            dma(2, items, 2),
+            dma(2, items, 2, 3),
             dma(2, items, 2, bits),
             dma(2, 2, count - 1),
             dma(2, count),
@@ -554,8 +595,8 @@
             bytes_accessed=500_000_000,
             transcendentals=0,
         ),
-    )(small, up_weight, qkv_weight, x, g, down_weight, proj_weight, bias, tables, first)
-    return dict(zip(list(shapes) + ["stats"], found))
+    )(small, up_weight, qkv_weight, x, g, down_weight, proj_weight, bias, frequency, lengths)
+    return dict(zip(list(shapes) + ["stats", "tables", "first"], found))
 
 
 RING = 3
@@ -757,7 +798,6 @@
             big_load(0).wait()
         if k == natives:
             big_load(1).wait()
-            big_load(2).start()
         if k == natives + hiddens:
             big_load(2).wait()
         slot = k % slots
@@ -960,15 +1000,16 @@
 
     stages = 4 + 2 * far
     n_heads, n_tiles = cols // HEAD, width // TILE
-    extras = {0: [grad_mixed, lambda: grad_pre(0)]}
+    extras = {0: [grad_mixed, partial(grad_pre, 0)]}
     for k in range(1, hiddens):
         extras.setdefault(k, []).append(partial(grad_pre, k))
     for head in range(n_heads):
         extras.setdefault(1 + head, []).append(partial(attention, head))
+    extras[hiddens] = [big_load(2).start]
     tile_at = hiddens + 1
     for j in range(n_tiles):
         extras.setdefault(tile_at + j, []).append(partial(tile, j))
-    vec_at = tile_at + n_tiles
+    vec_at = max(extras) + 1
 
     for copy in [narrow_load(0), big_load(0), proj_load()] + pre_loads(0):
         copy.start()
@@ -987,7 +1028,7 @@
         for number in reversed(range(stages)):
             if 0 <= tick - number < chunks:
                 stage(tick - number, number)
-        if tick == 1:
+        if tick == 0:
             heads_load().wait()
         for extra in extras.get(tick, []):
             extra()
@@ -1150,7 +1191,7 @@
             pl.BlockSpec((some, width), whole),
             pl.BlockSpec((some, 3 * width), whole),
         ),
-        compiler_params=pltpu.CompilerParams(vmem_limit_bytes=40 * 2**20),
+        compiler_params=pltpu.CompilerParams(vmem_limit_bytes=62 * 2**20),
     )(blocks, blocks, blocks, blocks, parts, branch, x, g, small)
 
 
@@ -1185,22 +1226,7 @@
     for i, param in enumerate(params):
         small = jnp.where(row == i, param[None], small)
 
-    token = lax.broadcasted_iota(jnp.int32, (group_rows, 1), 0)
-    first, end = jnp.zeros((group_rows, 1), jnp.int32), 0
-    for i in range(seq_lengths.shape[1]):
-        end = end + seq_lengths[0, i]
-        first = first + jnp.where(token >= end, seq_lengths[0, i], 0)
-    lane = lax.broadcasted_iota(jnp.int32, (1, 128), 1)
-    exponent = lax.rem(lane, ROT // 2).astype(jnp.float32) * (2.0 / ROT)
-    angles = (token - first).astype(jnp.float32) * jnp.power(jnp.float32(ROPE_BASE), -exponent)
-    cosine, sine = jnp.cos(angles), jnp.sin(angles)
-    tables = jnp.stack(
-        [
-            jnp.where(lane < ROT, cosine, 1.0),
-            jnp.where(lane < ROT // 2, sine, 0.0),
-            jnp.where((lane >= ROT // 2) & (lane < ROT), sine, 0.0),
-        ]
-    )
+    frequency = np.power(np.float32(ROPE_BASE), -np.arange(ROT // 2, dtype=np.float32) * np.float32(2.0 / ROT))
     known = forward(
         small,
         up_weight,
@@ -1210,8 +1236,8 @@
         down_weight,
         out_weight,
         up_bias.astype(jnp.float32)[None],
-        tables,
-        first,
+        jnp.asarray(np.tile(frequency, 128 // (ROT // 2))[None]),
+        seq_lengths,
     )
     branch_own = lax.psum_scatter(known["branch"], "shard", scatter_dimension=0, tiled=True)
     grads, vector, normed_parts = summed_grads(
@@ -1227,8 +1253,8 @@
         known["x"],
         known["up_cols"],
         known["qkv_cols"],
-        tables,
-        first,
+        known["tables"],
+        known["first"],
         known["stats"],
         known["small"],
     )

time: 536 us -> 524 us (0.978)
  other arithmetic: 11.4 us -> 2.77 us
  Pallas kernels: 489 us -> 496 us
    pallas_call x1, Pallas kernels: 240 us -> 247 us  [summed_grads(): pl.pallas_call(partial(grads_kernel, replicas, count), out_shape=(jax.Sha...]
  transfers between devices with their start and end apart: 1 -> 1, of which waited for: 0 -> 0; matrix products, arithmetic and copies ran while one was open for 1% -> 1% of each run, Pallas kernels for 46% -> 48%
where the time goes in v3:
time: 524 us; the launch traced here: 518 us
  Pallas kernels  496 us (95%)
  between operations  14.3 us (3%)
  local copies, waits for them, and re-layouts  5.4 us (1%)
    pallas_call x1, Pallas kernels, summed_grads(): pl.pallas_call(partial(grads_kernel, replicas, count), out_shape=(jax.Sha...  247 us
    pallas_call x1, Pallas kernels, forward(): pl.pallas_call(partial(forward_kernel, replicas, count), out_shape=tuple(...  219 us
    pallas_call x1, Pallas kernels, last(): pl.pallas_call(last_kernel, out_shape=(jax.ShapeDtypeStruct((local, width...  29.6 us
  transfers between devices with their start and end apart: 1, of which 0 were waited for; matrix products, arithmetic and copies ran while one was open for 1% of the time, Pallas kernels for 48%

profile of v3, /device:TPU:0, one launch (start us, length us, event | category | flops | bytes accessed | tf_op | source)
XLA Modules:
  0.0 518.1 jit_solution(479724648769584068)
XLA Ops:
  7.2 0.0 reduce-scatter.2.cloned.1.call-start
  7.3 0.8 fusion.1
  8.1 1.3 broadcast_in_dim.77
  9.3 1.5 select_select_fusion.small_ref
  10.8 218.9 %shard_map.263 = (bf16[4,16,512]{2,1,0:T(8,128)(2,1)}, bf16[2048,2048]{1,0:T(8,128)(2,1)}, bf16[3,2048,512]{2,1,0:T(8,128)(2,1)}, bf16[1024,2048]{1,0:T(8,128)(2...) custom-call(bf16[16,512]{1,0:T(8,128)(2,1)} %select_select_fusion.sm, ...), custom_call_target="tpu_custom_call" | custom-call | flops 25769803776 | bytes 500000000 | tf_op jit(solution)/shard_map/pallas_call | solution.py:556
  229.7 0.0 reduce-scatter.2.cloned.1.call-update
  229.8 247.0 %shard_map.264 = (bf16[12,4,512,512]{3,2,1,0:T(8,128)(2,1)}, f32[192,128]{1,0:T(8,128)}, bf16[4,256,2048]{2,1,0:T(8,128)(2,1)}) custom-call(bf16[1024,2048]{1,0:T(8,128)(2,1)} %get-tuple-element.40.act_ref, bf16[1024,2048]{1,0:T(8,128)(2,1)} %get-tuple-element.41.up_ref, bf16[1024,512]{1,0:T(8,128)(2,1)} %get-tuple-element.42.mixed_ref, ...), custom_call_target="tpu_custom_call" | custom-call | flops 51539607552 | bytes 600000000 | tf_op jit(solution)/shard_map/pallas_call | solution.py:1066
  476.8 1.4 dynamic_slice.23
  478.1 1.3 dynamic_slice.27
  479.4 1.4 fusion
  480.8 0.0 copy-start
  480.8 0.0 reduce-scatter.2.cloned.1.call-done.branch_ref
  480.8 29.6 %shard_map.265 = (bf16[256,2048]{1,0:T(8,128)(2,1)}, f32[256,2048]{1,0:T(8,128)}, f32[512,8192]{1,0:T(8,128)}, f32[2048,2048]{1,0:T(8,128)}, f32[512,2048]{1,0:T(8,128)}, /*index=5*/f32[512,6144]{1,0:T(8,128)}) custom-call(bf16[12,4,512,512]{3,2,1,0:T(8,128)(2,1)} %get-tuple-element.56.up_blocks.down_blocks.out_blocks.qkv_blocks, ...), custom_call_target="tpu_custom_call" | custom-call | tf_op jit(solution)/shard_map/pallas_call | solution.py:1164
  510.4 0.0 copy-done
  510.5 0.6 copy.31
  (5 shorter events, 0.0 us)
Async XLA Ops:
  7.2 473.6 %reduce-scatter.2.cloned.1.call-start = ((), (), s32[]{:S(2)}) async-start(), calls=%async_computation.1 | async-start | bytes 5242880 | tf_op jit(solution)/shard_map/reduce_scatter | solution.py:1242
  480.8 29.6 %copy-start = (f32[512]{0:T(512)}, f32[512]{0:T(512)S(1)}, u32[]{:S(2)}) copy-start(f32[512]{0:T(512)S(1)} %get-tuple-element.109) | copy-start | bytes 6148
Sparse Core Ops, SparseCore 0:
  229.9 91.7 reduce-scatter.1

commit v4 on v3

--- a/solution.py
+++ b/solution.py
@@ -450,6 +450,15 @@
             column_tick(tick)
         del ticks[:number]
 
+    def send_upstream(to_ends):
+        for other in range(1, shards_n):
+            to = lax.rem(place + other, shards_n)
+            at_end = (to == 0) | (to == shards_n - 1)
+
+            @pl.when(at_end if to_ends else jnp.logical_not(at_end))
+            def _():
+                upstream_copy(other, True).start()
+
     def arrive(step):
         pass_on(step)
         if step == 1:
@@ -457,6 +466,8 @@
                 for path in range(2):
                     for copy in turned(item, path, True):
                         copy.start()
+        if step == shards_n - 2:
+            send_upstream(False)
         on_step(step, lambda block, way: norm(block, x_out.at[block_rows(block), :], way))
 
     some_ticks(3)
@@ -477,8 +488,7 @@
         def _():
             hop(way, shards_n - 2, True).wait_send()
 
-    for other in range(1, shards_n):
-        upstream_copy(other, True).start()
+    send_upstream(True)
     some_ticks(len(ticks))
     arrive(shards_n - 1)
     keeps = [keep(0, mlp, mlp_out), keep(1, attn, attn_out)]
@@ -665,7 +675,7 @@
     core = bit_of(rep, 0)
     tokens, width = up_ref.shape
     local = tokens // shards_n
-    hiddens = pre.shape[0]
+    hiddens = pre.shape[1] // cols
     natives = hiddens + 1
     mine = pl.multiple_of(core * half, half)
     theirs = pl.multiple_of((1 - core) * half, half)
@@ -713,7 +723,13 @@
         return [
             load(rows_ref.at[:, some], tile_x.at[j % 2], 10 + j % 2),
             load(cols_up_ref.at[some, :], tile_up.at[j % 2], 12 + j % 2),
-            load(cols_qkv_ref.at[:, some, :], tile_qkv.at[j % 2], 14 + j % 2),
+        ] + [
+            load(
+                cols_qkv_ref.at[third, some, :],
+                tile_qkv.at[j % 2, :, pl.ds(third * cols, cols)],
+                14 + 2 * third + j % 2,
+            )
+            for third in range(3)
         ]
 
     def to_core(k):
@@ -803,24 +819,22 @@
         slot = k % slots
         which = 1 if natives <= k < natives + hiddens else 0
 
-        for begin, send in ((theirs, True), (mine, False)):
-
-            def block(g, carry):
-                if k < natives:
-                    left = narrow[k % 2, :, pl.ds(begin, half)]
-                    right = big[which, :, pl.ds(pl.multiple_of(g * cols, cols), cols)]
+        def block(g, carry):
+            if k < natives:
+                left = narrow[k % 2]
+                right = big[which, :, pl.ds(pl.multiple_of(g * cols, cols), cols)]
+            else:
+                left = big[which, :, pl.ds(pl.multiple_of(g * rows, rows), rows)]
+                if k < natives + hiddens:
+                    right = pre[:, (k - natives) * cols : (k - natives + 1) * cols]
                 else:
-                    left = big[which, :, pl.ds(pl.multiple_of(g * rows + begin, half), half)]
-                    if k < natives + hiddens:
-                        right = pre[k - natives]
-                    else:
-                        right = joined[k - natives - hiddens]
-                work[slot, g, pl.ds(begin, half), :] = dot_rows(left, right).astype(jnp.bfloat16)
-                return carry
-
-            lax.fori_loop(0, shards_n, block, 0)
-            if send:
-                to_core(k).start()
+                    third = k - natives - hiddens
+                    right = joined[:, third * cols : (third + 1) * cols]
+            work[slot, g] = dot_rows(left, right).astype(jnp.bfloat16)
+            return carry
+
+        lax.fori_loop(0, shards_n, block, 0)
+        to_core(k).start()
 
     def add(k, start, size, left, width, got):
         def block(g, carry):
@@ -836,11 +850,11 @@
         proj_load().wait()
 
         def block(i, carry):
-            some = pl.ds(pl.multiple_of(i * TILE, TILE), TILE)
+            some = pl.ds(pl.multiple_of(i * TALL, TALL), TALL)
             heads[3, some, :] = dot_cols(big[0, some, :], wide_rows[1]).astype(jnp.bfloat16)
             return carry
 
-        lax.fori_loop(0, tokens // TILE, block, 0)
+        lax.fori_loop(0, tokens // TALL, block, 0)
         down_load(1).start()
         own = pl.ds(pl.multiple_of(place * cols, cols), cols)
         put(4 * width + place * cols, jnp.sum(big[0, :, own].astype(jnp.float32), 0, keepdims=True))
@@ -850,15 +864,15 @@
             copy.wait()
 
         def block(i, total):
-            some = pl.ds(pl.multiple_of(i * TILE, TILE), TILE)
+            some = pl.ds(pl.multiple_of(i * TALL, TALL), TALL)
             found = dot_cols(big[0, some, :], wide_rows[k % 2]) * slope[k % 2, some, :].astype(
                 jnp.float32
             )
             low = found.astype(jnp.bfloat16)
-            pre[k, some, :] = low
+            pre[some, k * cols : (k + 1) * cols] = low
             return total + jnp.sum(low.astype(jnp.float32), 0, keepdims=True)
 
-        total = lax.fori_loop(0, tokens // TILE, block, jnp.zeros((1, cols), jnp.float32))
+        total = lax.fori_loop(0, tokens // TALL, block, jnp.zeros((1, cols), jnp.float32))
         put(8 * width + (place * hiddens + k) * cols, total)
         if k + 2 < hiddens:
             for copy in pre_loads(k + 2):
@@ -889,7 +903,7 @@
             delta = jnp.sum(probs * grad_probs, -1, keepdims=True)
             low = (probs * (grad_probs - delta)).astype(jnp.bfloat16)
             found = turn_rows(dot(low, key) * scale, some).astype(jnp.bfloat16)
-            joined[0, some, lanes] = found
+            joined[some, pl.ds(head * HEAD, HEAD)] = found
             sums[0] = sums[0] + jnp.sum(found.astype(jnp.float32), 0, keepdims=True)
             key_sum[keys, :] = key_sum[keys, :] + dot_rows(low, query)
             value_sum[keys, :] = value_sum[keys, :] + dot_rows(probs.astype(jnp.bfloat16), grad)
@@ -900,7 +914,7 @@
                 (2, value_sum[some, :]),
             ):
                 low = found.astype(jnp.bfloat16)
-                joined[third, some, lanes] = low
+                joined[some, pl.ds(third * cols + head * HEAD, HEAD)] = low
                 sums[third] = sums[third] + jnp.sum(low.astype(jnp.float32), 0, keepdims=True)
         for third in range(3):
             put(5 * width + third * width + place * cols + head * HEAD, sums[third])
@@ -925,15 +939,12 @@
         theirs_at = slice(begin, begin + TILE)
 
         def block(i, totals):
-            some = pl.ds(pl.multiple_of(i * local, local), local)
+            some = pl.ds(pl.multiple_of(i * TALL, TALL), TALL)
             normed = (tile_x[j % 2, some, :].astype(jnp.float32) - stats_ref[0, some, :]) * stats_ref[
                 1, some, :
             ]
-            mlp = sum(
-                dot_cols(pre[k, some, :], tile_up[j % 2, :, k * cols : (k + 1) * cols])
-                for k in range(hiddens)
-            )
-            attn = sum(dot_cols(joined[p, some, :], tile_qkv[j % 2, p]) for p in range(3))
+            mlp = dot_cols(pre[some, :], tile_up[j % 2])
+            attn = dot_cols(joined[some, :], tile_qkv[j % 2])
             shared[some, lanes] = (
                 attn * small_ref[owner, 0:1, theirs_at].astype(jnp.float32)
                 + mlp * small_ref[owner, 3:4, theirs_at].astype(jnp.float32)
@@ -942,7 +953,7 @@
             return tuple(t + jnp.sum(f, 0, keepdims=True) for t, f in zip(totals, found))
 
         zero = jnp.zeros((1, TILE), jnp.float32)
-        totals = lax.fori_loop(0, shards_n, block, (zero,) * 4)
+        totals = lax.fori_loop(0, tokens // TALL, block, (zero,) * 4)
         for number, total in enumerate(totals):
             put(number * width + j * TILE, total)
         for step in range(shards_n):
@@ -1080,8 +1091,8 @@
         + [
             low(2, tokens, width),
             low(2, tokens, cols),
-            low(hiddens, tokens, cols),
-            low(3, tokens, cols),
+            low(tokens, hidden),
+            low(tokens, 3 * cols),
             low(2, cols, width),
             low(2, tokens, cols),
             low(4, tokens, cols),
@@ -1089,11 +1100,11 @@
             full(tokens, HEAD),
             low(2, tokens, TILE),
             low(2, TILE, hidden),
-            low(2, 3, TILE, cols),
+            low(2, TILE, 3 * cols),
             low(tokens, width),
             full(peers, *vector),
             full(*vector),
-            dma(16),
+            dma(20),
             dma(2, 2, chunks),
             dma(2, chunks, far, 2),
             dma(2, chunks - natives, 2, count - 1),

time: 524 us -> 513 us (0.979)
  Pallas kernels: 496 us -> 484 us
    pallas_call x1, Pallas kernels: 247 us -> 235 us  [summed_grads(): pl.pallas_call(partial(grads_kernel, replicas, count), out_shape=(jax.Sha...]
  transfers between devices with their start and end apart: 1 -> 1, of which waited for: 0 -> 0; matrix products, arithmetic and copies ran while one was open for 1% -> 1% of each run, Pallas kernels for 48% -> 46%
where the time goes in v4:
time: 513 us; the launch traced here: 507 us
  Pallas kernels  484 us (94%)
  between operations  14.6 us (3%)
  local copies, waits for them, and re-layouts  5.4 us (1%)
    pallas_call x1, Pallas kernels, summed_grads(): pl.pallas_call(partial(grads_kernel, replicas, count), out_shape=(jax.Sha...  235 us
    pallas_call x1, Pallas kernels, forward(): pl.pallas_call(partial(forward_kernel, replicas, count), out_shape=tuple(...  219 us
    pallas_call x1, Pallas kernels, last(): pl.pallas_call(last_kernel, out_shape=(jax.ShapeDtypeStruct((local, width...  29.6 us
  transfers between devices with their start and end apart: 1, of which 0 were waited for; matrix products, arithmetic and copies ran while one was open for 1% of the time, Pallas kernels for 46%

profile of v4, /device:TPU:0, one launch (start us, length us, event | category | flops | bytes accessed | tf_op | source)
XLA Modules:
  0.0 506.7 jit_solution(14596780215677100263)
XLA Ops:
  7.2 0.0 reduce-scatter.2.cloned.1.call-start
  7.3 0.8 fusion.1
  8.1 1.3 broadcast_in_dim.77
  9.3 1.5 select_select_fusion.small_ref
  10.8 219.2 %shard_map.263 = (bf16[4,16,512]{2,1,0:T(8,128)(2,1)}, bf16[2048,2048]{1,0:T(8,128)(2,1)}, bf16[3,2048,512]{2,1,0:T(8,128)(2,1)}, bf16[1024,2048]{1,0:T(8,128)(2...) custom-call(bf16[16,512]{1,0:T(8,128)(2,1)} %select_select_fusion.sm, ...), custom_call_target="tpu_custom_call" | custom-call | flops 25769803776 | bytes 500000000 | tf_op jit(solution)/shard_map/pallas_call | solution.py:566
  230.0 0.0 reduce-scatter.2.cloned.1.call-update
  230.0 235.0 %shard_map.264 = (bf16[12,4,512,512]{3,2,1,0:T(8,128)(2,1)}, f32[192,128]{1,0:T(8,128)}, bf16[4,256,2048]{2,1,0:T(8,128)(2,1)}) custom-call(bf16[1024,2048]{1,0:T(8,128)(2,1)} %get-tuple-element.40.act_ref, bf16[1024,2048]{1,0:T(8,128)(2,1)} %get-tuple-element.41.up_ref, bf16[1024,512]{1,0:T(8,128)(2,1)} %get-tuple-element.42.mixed_ref, ...), custom_call_target="tpu_custom_call" | custom-call | flops 51539607552 | bytes 600000000 | tf_op jit(solution)/shard_map/pallas_call | solution.py:1077
  465.1 1.4 dynamic_slice.23
  466.5 1.3 dynamic_slice.27
  467.8 1.4 fusion
  469.1 0.0 copy-start
  469.1 0.0 reduce-scatter.2.cloned.1.call-done.branch_ref
  469.2 29.6 %shard_map.265 = (bf16[256,2048]{1,0:T(8,128)(2,1)}, f32[256,2048]{1,0:T(8,128)}, f32[512,8192]{1,0:T(8,128)}, f32[2048,2048]{1,0:T(8,128)}, f32[512,2048]{1,0:T(8,128)}, /*index=5*/f32[512,6144]{1,0:T(8,128)}) custom-call(bf16[12,4,512,512]{3,2,1,0:T(8,128)(2,1)} %get-tuple-element.56.up_blocks.down_blocks.out_blocks.qkv_blocks, ...), custom_call_target="tpu_custom_call" | custom-call | tf_op jit(solution)/shard_map/pallas_call | solution.py:1175
  498.8 0.0 copy-done
  498.8 0.6 copy.31
  (5 shorter events, 0.0 us)
Async XLA Ops:
  7.2 462.0 %reduce-scatter.2.cloned.1.call-start = ((), (), s32[]{:S(2)}) async-start(), calls=%async_computation.1 | async-start | bytes 5242880 | tf_op jit(solution)/shard_map/reduce_scatter | solution.py:1253
  469.1 29.6 %copy-start = (f32[512]{0:T(512)}, f32[512]{0:T(512)S(1)}, u32[]{:S(2)}) copy-start(f32[512]{0:T(512)S(1)} %get-tuple-element.109) | copy-start | bytes 6148
Sparse Core Ops, SparseCore 0:
  230.2 87.9 reduce-scatter.1

commit v5 on v4

--- a/solution.py
+++ b/solution.py
@@ -94,13 +94,32 @@
 
 
 def causal_probs(query, key, first, row):
-    shape = (query.shape[0], key.shape[0])
+    count = query.shape[0]
     scores = dot_cols(query, key) * (1.0 / math.sqrt(HEAD))
-    at = lax.broadcasted_iota(jnp.int32, shape, 1)
-    upto = lax.broadcasted_iota(jnp.int32, shape, 0) + row
-    scores = jnp.where((at >= first) & (at <= upto), scores, NEG_LARGE)
+    at = lax.broadcasted_iota(jnp.int32, scores.shape, 1)
+    scores = jnp.where(at >= first, scores, NEG_LARGE)
+    ahead = lax.broadcasted_iota(jnp.int32, (count, count), 1) > lax.broadcasted_iota(
+        jnp.int32, (count, count), 0
+    )
+    diagonal = jnp.where(ahead, NEG_LARGE, scores[:, row:])
+    scores = jnp.concatenate([scores[:, :row], diagonal], 1) if row else diagonal
     shifted = jnp.exp(scores - jnp.max(scores, -1, keepdims=True))
-    return shifted / jnp.sum(shifted, -1, keepdims=True)
+    return shifted * (1.0 / jnp.sum(shifted, -1, keepdims=True))
+
+
+ERF_AT = 0.3275911
+ERF_TERMS = (0.254829592, -0.284496736, 1.421413741, -1.453152027, 1.061405429)
+
+
+def gelu_and_slope(found):
+    bell = jnp.exp(-0.5 * found * found)
+    t = 1.0 / (1.0 + (ERF_AT * math.sqrt(0.5)) * jnp.abs(found))
+    series = ERF_TERMS[4]
+    for term in ERF_TERMS[3::-1]:
+        series = term + t * series
+    outside = 0.5 * t * series * bell
+    cdf = jnp.where(found >= 0.0, 1.0 - outside, outside)
+    return found * cdf, cdf + found * bell * (1.0 / math.sqrt(2.0 * math.pi))
 
 
 def forward_kernel(
@@ -289,8 +308,8 @@
         copy.wait()
 
         def some_rows(i, carry):
-            here = pl.ds(pl.multiple_of(i * 32, 32), 32)
-            there = pl.ds(pl.multiple_of(block * local + i * 32, 32), 32)
+            here = pl.ds(pl.multiple_of(i * 64, 64), 64)
+            there = pl.ds(pl.multiple_of(block * local + i * 64, 64), 64)
             values = x_rows[slot, here, :].astype(jnp.float32)
             mean = jnp.mean(values, -1, keepdims=True)
             centered = values - mean
@@ -305,21 +324,22 @@
                 mlp[there, lanes] = (some * small[z, 3:4, :] + small[z, 4:5, :]).astype(jnp.bfloat16)
             return carry
 
-        lax.fori_loop(0, local // 32, some_rows, 0)
+        lax.fori_loop(0, local // 64, some_rows, 0)
+
+    broad = hidden // 2
 
     def hidden_units(block):
         here = block_rows(block)
 
         def some_cols(k, carry):
-            lanes = pl.ds(pl.multiple_of(k * cols, cols), cols)
+            lanes = pl.ds(pl.multiple_of(k * broad, broad), broad)
             found = dot(mlp[here, :], up[:, lanes]) + bias_ref[0:1, lanes]
-            cdf = 0.5 * (1.0 + lax.erf(found * math.sqrt(0.5)))
-            act[here, lanes] = (found * cdf).astype(jnp.bfloat16)
-            bell = jnp.exp(-0.5 * found * found) * (1.0 / math.sqrt(2.0 * math.pi))
-            slope[here, lanes] = (cdf + found * bell).astype(jnp.bfloat16)
+            value, rise = gelu_and_slope(found)
+            act[here, lanes] = value.astype(jnp.bfloat16)
+            slope[here, lanes] = rise.astype(jnp.bfloat16)
             return carry
 
-        lax.fori_loop(0, hidden // cols, some_cols, 0)
+        lax.fori_loop(0, hidden // broad, some_cols, 0)
 
     def tables(i, carry):
         some = local // 2
@@ -1134,12 +1154,14 @@
     x_ref,
     g_ref,
     small_ref,
+    vec_ref,
     layer_out,
     input_out,
     up_out,
     down_out,
     out_out,
     qkv_out,
+    *thin_outs,
 ):
     number, count, _, cols = up_blocks.shape
     for g in range(count):
@@ -1163,8 +1185,18 @@
             rows[:, lanes] + branch_ref[:, lanes].astype(jnp.float32) + bias
         ).astype(jnp.bfloat16)
 
-
-def last(blocks, parts, branch, x, g, small):
+    @pl.when(pl.program_id(0) == 0)
+    def _():
+        place = lax.axis_index("shard")
+        width = count * cols
+        for thin, start in zip(thin_outs, (0, 1, 4, 4, 2, 3, 5, 8)):
+            length = thin.shape[0]
+            first = (start * width + place * length) // 128
+            for i in range(length // 128):
+                thin[i * 128 : (i + 1) * 128] = vec_ref[first + i, :]
+
+
+def last(blocks, parts, branch, x, g, small, vector):
     count, rows, cols = blocks.shape[1:]
     number = (blocks.shape[0] - 4) // 2
     local, width = x.shape
@@ -1172,6 +1204,7 @@
     some, tall = rows // steps, number * rows // steps
     turns = rows // tall
     whole = lambda i: (i, 0)
+    thin = [rows] * 6 + [3 * rows, number * rows]
     return pl.pallas_call(
         last_kernel,
         out_shape=(
@@ -1181,7 +1214,8 @@
             jax.ShapeDtypeStruct((number * rows, width), jnp.float32),
             jax.ShapeDtypeStruct((rows, width), jnp.float32),
             jax.ShapeDtypeStruct((rows, 3 * width), jnp.float32),
-        ),
+        )
+        + tuple(jax.ShapeDtypeStruct((length,), jnp.float32) for length in thin),
         grid=(steps,),
         in_specs=[
             pl.BlockSpec((number, count, some, cols), lambda i: (0, 0, i, 0)),
@@ -1193,6 +1227,7 @@
             pl.BlockSpec((16, width), whole),
             pl.BlockSpec((16, width), whole),
             pl.BlockSpec(small.shape, lambda i: (0, 0, 0)),
+            pl.BlockSpec(vector.shape, lambda i: (0, 0)),
         ],
         out_specs=(
             pl.BlockSpec((16, width), whole),
@@ -1201,9 +1236,10 @@
             pl.BlockSpec((tall, width), whole),
             pl.BlockSpec((some, width), whole),
             pl.BlockSpec((some, 3 * width), whole),
-        ),
+        )
+        + tuple(pl.BlockSpec((length,), lambda i: (0,)) for length in thin),
         compiler_params=pltpu.CompilerParams(vmem_limit_bytes=62 * 2**20),
-    )(blocks, blocks, blocks, blocks, parts, branch, x, g, small)
+    )(blocks, blocks, blocks, blocks, parts, branch, x, g, small, vector)
 
 
 def shards(
@@ -1270,29 +1306,24 @@
         known["small"],
     )
     grads, branch_own = lax.optimization_barrier((grads, branch_own))
-    vector = vector.reshape(-1)
-    layer_output, input_grad, up_grad, down_grad, out_grad, qkv_grad = last(
-        grads, normed_parts, branch_own, layer_input, upstream, known["small"]
+    layer_output, input_grad, up_grad, down_grad, out_grad, qkv_grad, *thin = last(
+        grads, normed_parts, branch_own, layer_input, upstream, known["small"], vector
     )
-    own = lambda i: lax.dynamic_slice_in_dim(vector, i * D + place * part, part, 0)
-    bias_grad = own(4)
-    qkv_bias_grad = lax.dynamic_slice_in_dim(vector, 5 * D + place * 3 * part, 3 * part, 0)
-    up_bias_grad = lax.dynamic_slice_in_dim(vector, 8 * D + place * hidden, hidden, 0)
     return (
         layer_output,
         input_grad,
-        own(0),
-        own(1),
+        thin[0],
+        thin[1],
         qkv_grad,
-        qkv_bias_grad,
+        thin[6],
         out_grad,
-        bias_grad,
-        own(2),
-        own(3),
+        thin[2],
+        thin[4],
+        thin[5],
         up_grad,
-        up_bias_grad,
+        thin[7],
         down_grad,
-        bias_grad,
+        thin[3],
     )
 
 

time: 513 us -> 521 us (1.016)
  Pallas kernels: 484 us -> 494 us
    pallas_call x1, Pallas kernels: 235 us -> 243 us  [summed_grads(): pl.pallas_call(partial(grads_kernel, replicas, count), out_shape=(jax.Sha...]
  transfers between devices with their start and end apart: 1 -> 1, of which waited for: 0 -> 0; matrix products, arithmetic and copies ran while one was open for 1% -> 0% of each run, Pallas kernels for 46% -> 47%
where the time goes in v5:
time: 521 us; the launch traced here: 512 us
  Pallas kernels  494 us (95%)
  between operations  14.6 us (3%)
    pallas_call x1, Pallas kernels, summed_grads(): pl.pallas_call(partial(grads_kernel, replicas, count), out_shape=(jax.Sha...  243 us
    pallas_call x1, Pallas kernels, forward(): pl.pallas_call(partial(forward_kernel, replicas, count), out_shape=tuple(...  220 us
    pallas_call x1, Pallas kernels, last(): pl.pallas_call(last_kernel, out_shape=(jax.ShapeDtypeStruct((local, width...  30.5 us
  transfers between devices with their start and end apart: 1, of which 0 were waited for; matrix products, arithmetic and copies ran while one was open for 0% of the time, Pallas kernels for 47%

profile of v5, /device:TPU:0, one launch (start us, length us, event | category | flops | bytes accessed | tf_op | source)
XLA Modules:
  0.0 512.3 jit_solution(6328006628758642246)
XLA Ops:
  7.2 0.0 reduce-scatter.2.cloned.1.call-start
  7.3 0.8 fusion
  8.1 1.3 broadcast_in_dim.77
  9.3 1.5 select_select_fusion.small_ref
  10.8 220.3 %shard_map.263 = (bf16[4,16,512]{2,1,0:T(8,128)(2,1)}, bf16[2048,2048]{1,0:T(8,128)(2,1)}, bf16[3,2048,512]{2,1,0:T(8,128)(2,1)}, bf16[1024,2048]{1,0:T(8,128)(2...) custom-call(bf16[16,512]{1,0:T(8,128)(2,1)} %select_select_fusion.sm, ...), custom_call_target="tpu_custom_call" | custom-call | flops 25769803776 | bytes 500000000 | tf_op jit(solution)/shard_map/pallas_call | solution.py:586
  231.1 0.0 reduce-scatter.2.cloned.1.call-update
  231.1 243.3 %shard_map.264 = (bf16[12,4,512,512]{3,2,1,0:T(8,128)(2,1)}, f32[192,128]{1,0:T(8,128)}, bf16[4,256,2048]{2,1,0:T(8,128)(2,1)}) custom-call(bf16[1024,2048]{1,0:T(8,128)(2,1)} %get-tuple-element.48.act_ref, bf16[1024,2048]{1,0:T(8,128)(2,1)} %get-tuple-element.49.up_ref, bf16[1024,512]{1,0:T(8,128)(2,1)} %get-tuple-element.50.mixed_ref, ...), custom_call_target="tpu_custom_call" | custom-call | flops 51539607552 | bytes 600000000 | tf_op jit(solution)/shard_map/pallas_call | solution.py:1097
  474.4 0.0 reduce-scatter.2.cloned.1.call-done.branch_ref
  474.5 30.5 %shard_map.265 = (bf16[256,2048]{1,0:T(8,128)(2,1)}, f32[256,2048]{1,0:T(8,128)}, f32[512,8192]{1,0:T(8,128)}, f32[2048,2048]{1,0:T(8,128)}, f32[512,2048]{1,0:T...) custom-call(bf16[12,4,512,512]{3,2,1,0:T(8,128)(2,1)} %get-tuple-ele, ...), custom_call_target="tpu_custom_call" | custom-call | tf_op jit(solution)/shard_map/pallas_call | solution.py:1208
  (5 shorter events, 0.0 us)
Async XLA Ops:
  7.2 467.3 %reduce-scatter.2.cloned.1.call-start = ((), (), s32[]{:S(2)}) async-start(), calls=%async_computation.1 | async-start | bytes 5242880 | tf_op jit(solution)/shard_map/reduce_scatter | solution.py:1289
Sparse Core Ops, SparseCore 0:
  231.3 82.1 reduce-scatter.1

commit v6 on v5

--- a/solution.py
+++ b/solution.py
@@ -94,32 +94,13 @@
 
 
 def causal_probs(query, key, first, row):
-    count = query.shape[0]
+    shape = (query.shape[0], key.shape[0])
     scores = dot_cols(query, key) * (1.0 / math.sqrt(HEAD))
-    at = lax.broadcasted_iota(jnp.int32, scores.shape, 1)
-    scores = jnp.where(at >= first, scores, NEG_LARGE)
-    ahead = lax.broadcasted_iota(jnp.int32, (count, count), 1) > lax.broadcasted_iota(
-        jnp.int32, (count, count), 0
-    )
-    diagonal = jnp.where(ahead, NEG_LARGE, scores[:, row:])
-    scores = jnp.concatenate([scores[:, :row], diagonal], 1) if row else diagonal
+    at = lax.broadcasted_iota(jnp.int32, shape, 1)
+    upto = lax.broadcasted_iota(jnp.int32, shape, 0) + row
+    scores = jnp.where((at >= first) & (at <= upto), scores, NEG_LARGE)
     shifted = jnp.exp(scores - jnp.max(scores, -1, keepdims=True))
-    return shifted * (1.0 / jnp.sum(shifted, -1, keepdims=True))
-
-
-ERF_AT = 0.3275911
-ERF_TERMS = (0.254829592, -0.284496736, 1.421413741, -1.453152027, 1.061405429)
-
-
-def gelu_and_slope(found):
-    bell = jnp.exp(-0.5 * found * found)
-    t = 1.0 / (1.0 + (ERF_AT * math.sqrt(0.5)) * jnp.abs(found))
-    series = ERF_TERMS[4]
-    for term in ERF_TERMS[3::-1]:
-        series = term + t * series
-    outside = 0.5 * t * series * bell
-    cdf = jnp.where(found >= 0.0, 1.0 - outside, outside)
-    return found * cdf, cdf + found * bell * (1.0 / math.sqrt(2.0 * math.pi))
+    return shifted / jnp.sum(shifted, -1, keepdims=True)
 
 
 def forward_kernel(
@@ -270,7 +251,23 @@
     def upstream_copy(step, sending):
         to = lax.rem(place + step, shards_n)
         shard = place if sending else lax.rem(place - step + shards_n, shards_n)
-        return remote(g_ref, g_out.at[block_rows(shard), :], g_sem, (step,), {"shard": to})
+        return remote(g_ref, g_out.at[block_rows(shard), :], g_sem, (0, step), {"shard": to})
+
+    def to_end(block, end):
+        there = g_out.at[block_rows(block), :]
+        return remote(there, there, g_sem, (1, block), {"shard": end})
+
+    ends = [(0, 1), (shards_n - 1, shards_n - 2)]
+    passed = [list(range(2, shards_n)), list(range(shards_n - 3, -1, -1))]
+
+    def pass_upstream(number):
+        for (end, beside), blocks in zip(ends, passed):
+
+            @pl.when(place == beside)
+            def _():
+                block = blocks[number]
+                upstream_copy((beside - block) % shards_n, False).wait_recv()
+                to_end(block, end).start()
 
     def holds(way, step):
         return place >= step if way == 0 else place + step < shards_n
@@ -308,8 +305,8 @@
         copy.wait()
 
         def some_rows(i, carry):
-            here = pl.ds(pl.multiple_of(i * 64, 64), 64)
-            there = pl.ds(pl.multiple_of(block * local + i * 64, 64), 64)
+            here = pl.ds(pl.multiple_of(i * 32, 32), 32)
+            there = pl.ds(pl.multiple_of(block * local + i * 32, 32), 32)
             values = x_rows[slot, here, :].astype(jnp.float32)
             mean = jnp.mean(values, -1, keepdims=True)
             centered = values - mean
@@ -324,22 +321,21 @@
                 mlp[there, lanes] = (some * small[z, 3:4, :] + small[z, 4:5, :]).astype(jnp.bfloat16)
             return carry
 
-        lax.fori_loop(0, local // 64, some_rows, 0)
-
-    broad = hidden // 2
+        lax.fori_loop(0, local // 32, some_rows, 0)
 
     def hidden_units(block):
         here = block_rows(block)
 
         def some_cols(k, carry):
-            lanes = pl.ds(pl.multiple_of(k * broad, broad), broad)
+            lanes = pl.ds(pl.multiple_of(k * cols, cols), cols)
             found = dot(mlp[here, :], up[:, lanes]) + bias_ref[0:1, lanes]
-            value, rise = gelu_and_slope(found)
-            act[here, lanes] = value.astype(jnp.bfloat16)
-            slope[here, lanes] = rise.astype(jnp.bfloat16)
+            cdf = 0.5 * (1.0 + lax.erf(found * math.sqrt(0.5)))
+            act[here, lanes] = (found * cdf).astype(jnp.bfloat16)
+            bell = jnp.exp(-0.5 * found * found) * (1.0 / math.sqrt(2.0 * math.pi))
+            slope[here, lanes] = (cdf + found * bell).astype(jnp.bfloat16)
             return carry
 
-        lax.fori_loop(0, hidden // broad, some_cols, 0)
+        lax.fori_loop(0, hidden // cols, some_cols, 0)
 
     def tables(i, carry):
         some = local // 2
@@ -474,8 +470,9 @@
         for other in range(1, shards_n):
             to = lax.rem(place + other, shards_n)
             at_end = (to == 0) | (to == shards_n - 1)
-
-            @pl.when(at_end if to_ends else jnp.logical_not(at_end))
+            beside = ((to == 0) & (place == 1)) | ((to == shards_n - 1) & (place == shards_n - 2))
+
+            @pl.when(beside if to_ends else jnp.logical_not(at_end))
             def _():
                 upstream_copy(other, True).start()
 
@@ -519,12 +516,15 @@
     load_qkv.start()
     for step in range(2, shards_n):
         on_step(step, lambda block, way: hidden_units(block))
+    pass_upstream(0)
     keeps += [keep(2, act, act_out), keep(3, slope, slope_out)]
     keeps[2].start()
     keeps[3].start()
     load_qkv.wait()
     for third in range(3):
         project(third)
+    for number in range(1, shards_n - 2):
+        pass_upstream(number)
     keeps.append(keep(4, heads, heads_out))
     keeps[4].start()
     for head in range(wide // HEAD):
@@ -535,7 +535,41 @@
     for j in range(width // cols):
         branch_cols(j)
     for step in range(1, shards_n):
-        upstream_copy(step, False).wait()
+        origin, onto = lax.rem(place - step + shards_n, shards_n), lax.rem(place + step, shards_n)
+        inner = (place > 0) & (place < shards_n - 1)
+        for end, beside in ends:
+
+            @pl.when((place == end) & (origin == beside))
+            def _():
+                upstream_copy(step, False).wait_recv()
+
+            @pl.when((place == end) & (origin != beside))
+            def _():
+                to_end(origin, end).wait_recv()
+
+            @pl.when((onto == end) & (place == beside))
+            def _():
+                upstream_copy(step, True).wait_send()
+
+        waited = False
+        for (end, beside), blocks in zip(ends, passed):
+            waited = waited | ((place == beside) & (origin != end))
+
+        @pl.when(inner & jnp.logical_not(waited))
+        def _():
+            upstream_copy(step, False).wait_recv()
+
+        @pl.when((onto > 0) & (onto < shards_n - 1))
+        def _():
+            upstream_copy(step, True).wait_send()
+
+    for (end, beside), blocks in zip(ends, passed):
+        for block in blocks:
+
+            @pl.when(place == beside)
+            def _():
+                to_end(block, end).wait_send()
+
     for j in range(max(width // cols - 2, 0), width // cols):
         branch_keep(j).wait()
     for copy in keeps:
@@ -615,7 +649,7 @@
             dma(2, items, 2, 3),
             dma(2, items, 2, bits),
             dma(2, 2, count - 1),
-            dma(2, count),
+            dma(2, 2, count),
         ],
         compiler_params=pltpu.CompilerParams(
             collective_id=0, has_side_effects=True, vmem_limit_bytes=58 * 2**20

time: 521 us -> 526 us (level)
  Pallas kernels: 494 us -> 502 us
    pallas_call x1, Pallas kernels: 220 us -> 236 us  [forward(): pl.pallas_call(partial(forward_kernel, replicas, count), out_shape=tuple(...]
    pallas_call x1, Pallas kernels: 243 us -> 235 us  [summed_grads(): pl.pallas_call(partial(grads_kernel, replicas, count), out_shape=(jax.Sha...]
  transfers between devices with their start and end apart: 1 -> 1, of which waited for: 0 -> 0; matrix products, arithmetic and copies ran while one was open for 0% -> 0% of each run, Pallas kernels for 47% -> 45%
where the time goes in v6:
time: 526 us; the launch traced here: 520 us
  Pallas kernels  502 us (95%)
  between operations  14.6 us (3%)
    pallas_call x1, Pallas kernels, forward(): pl.pallas_call(partial(forward_kernel, replicas, count), out_shape=tuple(...  236 us
    pallas_call x1, Pallas kernels, summed_grads(): pl.pallas_call(partial(grads_kernel, replicas, count), out_shape=(jax.Sha...  235 us
    pallas_call x1, Pallas kernels, last(): pl.pallas_call(last_kernel, out_shape=(jax.ShapeDtypeStruct((local, width...  30.5 us
  transfers between devices with their start and end apart: 1, of which 0 were waited for; matrix products, arithmetic and copies ran while one was open for 0% of the time, Pallas kernels for 45%

profile of v6, /device:TPU:0, one launch (start us, length us, event | category | flops | bytes accessed | tf_op | source)
XLA Modules:
  0.0 519.8 jit_solution(13339362849424144132)
XLA Ops:
  7.2 0.0 reduce-scatter.2.cloned.1.call-start
  7.3 0.8 fusion
  8.1 1.3 broadcast_in_dim.77
  9.3 1.5 select_select_fusion.small_ref
  10.8 236.1 %shard_map.263 = (bf16[4,16,512]{2,1,0:T(8,128)(2,1)}, bf16[2048,2048]{1,0:T(8,128)(2,1)}, bf16[3,2048,512]{2,1,0:T(8,128)(2,1)}, bf16[1024,2048]{1,0:T(8,128)(2...) custom-call(bf16[16,512]{1,0:T(8,128)(2,1)} %select_select_fusion.sm, ...), custom_call_target="tpu_custom_call" | custom-call | flops 25769803776 | bytes 500000000 | tf_op jit(solution)/shard_map/pallas_call | solution.py:620
  246.9 0.0 reduce-scatter.2.cloned.1.call-update
  247.0 235.0 %shard_map.264 = (bf16[12,4,512,512]{3,2,1,0:T(8,128)(2,1)}, f32[192,128]{1,0:T(8,128)}, bf16[4,256,2048]{2,1,0:T(8,128)(2,1)}) custom-call(bf16[1024,2048]{1,0:T(8,128)(2,1)} %get-tuple-element.48.act_ref, bf16[1024,2048]{1,0:T(8,128)(2,1)} %get-tuple-element.49.up_ref, bf16[1024,512]{1,0:T(8,128)(2,1)} %get-tuple-element.50.mixed_ref, ...), custom_call_target="tpu_custom_call" | custom-call | flops 51539607552 | bytes 600000000 | tf_op jit(solution)/shard_map/pallas_call | solution.py:1131
  481.9 0.0 reduce-scatter.2.cloned.1.call-done.branch_ref
  482.0 30.5 %shard_map.265 = (bf16[256,2048]{1,0:T(8,128)(2,1)}, f32[256,2048]{1,0:T(8,128)}, f32[512,8192]{1,0:T(8,128)}, f32[2048,2048]{1,0:T(8,128)}, f32[512,2048]{1,0:T...) custom-call(bf16[12,4,512,512]{3,2,1,0:T(8,128)(2,1)} %get-tuple-ele, ...), custom_call_target="tpu_custom_call" | custom-call | tf_op jit(solution)/shard_map/pallas_call | solution.py:1242
  (5 shorter events, 0.0 us)
Async XLA Ops:
  7.2 474.8 %reduce-scatter.2.cloned.1.call-start = ((), (), s32[]{:S(2)}) async-start(), calls=%async_computation.1 | async-start | bytes 5242880 | tf_op jit(solution)/shard_map/reduce_scatter | solution.py:1323
Sparse Core Ops, SparseCore 0:
  247.1 89.5 reduce-scatter.1

commit v7 on v5

--- a/solution.py
+++ b/solution.py
@@ -94,32 +94,13 @@
 
 
 def causal_probs(query, key, first, row):
-    count = query.shape[0]
+    shape = (query.shape[0], key.shape[0])
     scores = dot_cols(query, key) * (1.0 / math.sqrt(HEAD))
-    at = lax.broadcasted_iota(jnp.int32, scores.shape, 1)
-    scores = jnp.where(at >= first, scores, NEG_LARGE)
-    ahead = lax.broadcasted_iota(jnp.int32, (count, count), 1) > lax.broadcasted_iota(
-        jnp.int32, (count, count), 0
-    )
-    diagonal = jnp.where(ahead, NEG_LARGE, scores[:, row:])
-    scores = jnp.concatenate([scores[:, :row], diagonal], 1) if row else diagonal
+    at = lax.broadcasted_iota(jnp.int32, shape, 1)
+    upto = lax.broadcasted_iota(jnp.int32, shape, 0) + row
+    scores = jnp.where((at >= first) & (at <= upto), scores, NEG_LARGE)
     shifted = jnp.exp(scores - jnp.max(scores, -1, keepdims=True))
-    return shifted * (1.0 / jnp.sum(shifted, -1, keepdims=True))
-
-
-ERF_AT = 0.3275911
-ERF_TERMS = (0.254829592, -0.284496736, 1.421413741, -1.453152027, 1.061405429)
-
-
-def gelu_and_slope(found):
-    bell = jnp.exp(-0.5 * found * found)
-    t = 1.0 / (1.0 + (ERF_AT * math.sqrt(0.5)) * jnp.abs(found))
-    series = ERF_TERMS[4]
-    for term in ERF_TERMS[3::-1]:
-        series = term + t * series
-    outside = 0.5 * t * series * bell
-    cdf = jnp.where(found >= 0.0, 1.0 - outside, outside)
-    return found * cdf, cdf + found * bell * (1.0 / math.sqrt(2.0 * math.pi))
+    return shifted / jnp.sum(shifted, -1, keepdims=True)
 
 
 def forward_kernel(
@@ -238,11 +219,11 @@
         shard = place if sending else lax.rem(place - step + shards_n, shards_n)
         return remote(small_ref, small_out.at[shard], small_sem, (step,), {"shard": to})
 
-    def column_tick(tick):
+    def column_tick(thing, tick):
         for level in reversed(range(bits + 1)):
-            item = tick - level
-            if not 0 <= item < len(items):
+            if not 0 <= tick - level < shards_n - 1:
                 continue
+            item = thing * (shards_n - 1) + tick - level
             for path in range(2):
                 if level == 0:
                     for copy in turned(item, path, False):
@@ -308,8 +289,8 @@
         copy.wait()
 
         def some_rows(i, carry):
-            here = pl.ds(pl.multiple_of(i * 64, 64), 64)
-            there = pl.ds(pl.multiple_of(block * local + i * 64, 64), 64)
+            here = pl.ds(pl.multiple_of(i * 32, 32), 32)
+            there = pl.ds(pl.multiple_of(block * local + i * 32, 32), 32)
             values = x_rows[slot, here, :].astype(jnp.float32)
             mean = jnp.mean(values, -1, keepdims=True)
             centered = values - mean
@@ -324,22 +305,21 @@
                 mlp[there, lanes] = (some * small[z, 3:4, :] + small[z, 4:5, :]).astype(jnp.bfloat16)
             return carry
 
-        lax.fori_loop(0, local // 64, some_rows, 0)
-
-    broad = hidden // 2
+        lax.fori_loop(0, local // 32, some_rows, 0)
 
     def hidden_units(block):
         here = block_rows(block)
 
         def some_cols(k, carry):
-            lanes = pl.ds(pl.multiple_of(k * broad, broad), broad)
+            lanes = pl.ds(pl.multiple_of(k * cols, cols), cols)
             found = dot(mlp[here, :], up[:, lanes]) + bias_ref[0:1, lanes]
-            value, rise = gelu_and_slope(found)
-            act[here, lanes] = value.astype(jnp.bfloat16)
-            slope[here, lanes] = rise.astype(jnp.bfloat16)
+            cdf = 0.5 * (1.0 + lax.erf(found * math.sqrt(0.5)))
+            act[here, lanes] = (found * cdf).astype(jnp.bfloat16)
+            bell = jnp.exp(-0.5 * found * found) * (1.0 / math.sqrt(2.0 * math.pi))
+            slope[here, lanes] = (cdf + found * bell).astype(jnp.bfloat16)
             return carry
 
-        lax.fori_loop(0, hidden // broad, some_cols, 0)
+        lax.fori_loop(0, hidden // cols, some_cols, 0)
 
     def tables(i, carry):
         some = local // 2
@@ -463,12 +443,12 @@
 
     load_up = load(2, up_out, up)
     load_qkv = load(3, qkv_out, qkv)
-    ticks = list(range(len(items) + bits))
-
-    def some_ticks(number):
-        for tick in ticks[:number]:
-            column_tick(tick)
-        del ticks[:number]
+    ticks = [list(range(shards_n - 1 + bits)) for thing in range(2)]
+
+    def some_ticks(thing, number):
+        for tick in ticks[thing][:number]:
+            column_tick(thing, tick)
+        del ticks[thing][:number]
 
     def send_upstream(to_ends):
         for other in range(1, shards_n):
@@ -479,29 +459,32 @@
             def _():
                 upstream_copy(other, True).start()
 
-    def arrive(step):
-        pass_on(step)
-        if step == 1:
-            for item in range(shards_n - 1, len(items)):
-                for path in range(2):
-                    for copy in turned(item, path, True):
-                        copy.start()
-        if step == shards_n - 2:
-            send_upstream(False)
+    def norms(step):
         on_step(step, lambda block, way: norm(block, x_out.at[block_rows(block), :], way))
 
-    some_ticks(3)
-    arrive(1)
-    some_ticks(shards_n - 1 + bits - 3)
+    def units(step):
+        on_step(step, lambda block, way: hidden_units(block))
+
+    some_ticks(0, 3)
+    pass_on(1)
+    norms(1)
+    some_ticks(0, len(ticks[0]))
     own[1].wait()
     load_up.start()
+    for step in range(2, shards_n - 1):
+        pass_on(step)
+    for item in range(shards_n - 1, len(items)):
+        for path in range(2):
+            for copy in turned(item, path, True):
+                copy.start()
+    send_upstream(False)
     load_up.wait()
-    on_step(0, lambda block, way: hidden_units(block))
+    units(0)
     for step in range(2, shards_n - 1):
-        arrive(step)
-    some_ticks(1)
-    on_step(1, lambda block, way: hidden_units(block))
-    some_ticks(1)
+        norms(step)
+    some_ticks(1, 1)
+    units(1)
+    some_ticks(1, 1)
     for way in range(2):
 
         @pl.when(goes(way, shards_n - 2))
@@ -509,16 +492,19 @@
             hop(way, shards_n - 2, True).wait_send()
 
     send_upstream(True)
-    some_ticks(len(ticks))
-    arrive(shards_n - 1)
+    pass_on(shards_n - 1)
+    norms(shards_n - 1)
+    some_ticks(1, 1)
     keeps = [keep(0, mlp, mlp_out), keep(1, attn, attn_out)]
     keeps[0].start()
     keeps[1].start()
+    for step in range(2, shards_n):
+        units(step)
+        some_ticks(1, 1)
+    some_ticks(1, len(ticks[1]))
     for copy in own[4:]:
         copy.wait()
     load_qkv.start()
-    for step in range(2, shards_n):
-        on_step(step, lambda block, way: hidden_units(block))
     keeps += [keep(2, act, act_out), keep(3, slope, slope_out)]
     keeps[2].start()
     keeps[3].start()

time: 521 us -> 509 us (0.977)
  Pallas kernels: 494 us -> 484 us
    pallas_call x1, Pallas kernels: 243 us -> 237 us  [summed_grads(): pl.pallas_call(partial(grads_kernel, replicas, count), out_shape=(jax.Sha...]
where the time goes in v7:
time: 509 us; the launch traced here: 503 us
  Pallas kernels  484 us (95%)
  between operations  14.6 us (3%)
    pallas_call x1, Pallas kernels, summed_grads(): pl.pallas_call(partial(grads_kernel, replicas, count), out_shape=(jax.Sha...  237 us
    pallas_call x1, Pallas kernels, forward(): pl.pallas_call(partial(forward_kernel, replicas, count), out_shape=tuple(...  217 us
    pallas_call x1, Pallas kernels, last(): pl.pallas_call(last_kernel, out_shape=(jax.ShapeDtypeStruct((local, width...  30.5 us
  transfers between devices with their start and end apart: 1, of which 0 were waited for; matrix products, arithmetic and copies ran while one was open for 0% of the time, Pallas kernels for 47%

profile of v7, /device:TPU:0, one launch (start us, length us, event | category | flops | bytes accessed | tf_op | source)
XLA Modules:
  0.0 502.6 jit_solution(7636357855103024307)
XLA Ops:
  7.2 0.0 reduce-scatter.2.cloned.1.call-start
  7.3 0.8 fusion
  8.1 1.3 broadcast_in_dim.77
  9.3 1.5 select_select_fusion.small_ref
  10.8 217.3 %shard_map.263 = (bf16[4,16,512]{2,1,0:T(8,128)(2,1)}, bf16[2048,2048]{1,0:T(8,128)(2,1)}, bf16[3,2048,512]{2,1,0:T(8,128)(2,1)}, bf16[1024,2048]{1,0:T(8,128)(2...) custom-call(bf16[16,512]{1,0:T(8,128)(2,1)} %select_select_fusion.sm, ...), custom_call_target="tpu_custom_call" | custom-call | flops 25769803776 | bytes 500000000 | tf_op jit(solution)/shard_map/pallas_call | solution.py:572
  228.1 0.0 reduce-scatter.2.cloned.1.call-update
  228.1 236.6 %shard_map.264 = (bf16[12,4,512,512]{3,2,1,0:T(8,128)(2,1)}, f32[192,128]{1,0:T(8,128)}, bf16[4,256,2048]{2,1,0:T(8,128)(2,1)}) custom-call(bf16[1024,2048]{1,0:T(8,128)(2,1)} %get-tuple-element.48.act_ref, bf16[1024,2048]{1,0:T(8,128)(2,1)} %get-tuple-element.49.up_ref, bf16[1024,512]{1,0:T(8,128)(2,1)} %get-tuple-element.50.mixed_ref, ...), custom_call_target="tpu_custom_call" | custom-call | flops 51539607552 | bytes 600000000 | tf_op jit(solution)/shard_map/pallas_call | solution.py:1083
  464.8 0.0 reduce-scatter.2.cloned.1.call-done.branch_ref
  464.8 30.5 %shard_map.265 = (bf16[256,2048]{1,0:T(8,128)(2,1)}, f32[256,2048]{1,0:T(8,128)}, f32[512,8192]{1,0:T(8,128)}, f32[2048,2048]{1,0:T(8,128)}, f32[512,2048]{1,0:T...) custom-call(bf16[12,4,512,512]{3,2,1,0:T(8,128)(2,1)} %get-tuple-ele, ...), custom_call_target="tpu_custom_call" | custom-call | tf_op jit(solution)/shard_map/pallas_call | solution.py:1194
  (5 shorter events, 0.0 us)
Async XLA Ops:
  7.2 457.6 %reduce-scatter.2.cloned.1.call-start = ((), (), s32[]{:S(2)}) async-start(), calls=%async_computation.1 | async-start | bytes 5242880 | tf_op jit(solution)/shard_map/reduce_scatter | solution.py:1275
Sparse Core Ops, SparseCore 0:
  228.3 86.8 reduce-scatter.1

commit v8 on v7

--- a/solution.py
+++ b/solution.py
@@ -90,7 +90,7 @@
 
 
 TILE = 256
-TALL = 512
+TALL = 1024
 
 
 def causal_probs(query, key, first, row):
@@ -100,7 +100,7 @@
     upto = lax.broadcasted_iota(jnp.int32, shape, 0) + row
     scores = jnp.where((at >= first) & (at <= upto), scores, NEG_LARGE)
     shifted = jnp.exp(scores - jnp.max(scores, -1, keepdims=True))
-    return shifted / jnp.sum(shifted, -1, keepdims=True)
+    return shifted * (1.0 / jnp.sum(shifted, -1, keepdims=True))
 
 
 def forward_kernel(

time: 509 us -> 505 us (level)
  no operation moved by 1% of the time
where the time goes in v8:
time: 505 us; the launch traced here: 498 us
  Pallas kernels  480 us (95%)
  between operations  14.6 us (3%)
    pallas_call x1, Pallas kernels, summed_grads(): pl.pallas_call(partial(grads_kernel, replicas, count), out_shape=(jax.Sha...  235 us
    pallas_call x1, Pallas kernels, forward(): pl.pallas_call(partial(forward_kernel, replicas, count), out_shape=tuple(...  215 us
    pallas_call x1, Pallas kernels, last(): pl.pallas_call(last_kernel, out_shape=(jax.ShapeDtypeStruct((local, width...  30.5 us
  transfers between devices with their start and end apart: 1, of which 0 were waited for; matrix products, arithmetic and copies ran while one was open for 0% of the time, Pallas kernels for 47%

profile of v8, /device:TPU:0, one launch (start us, length us, event | category | flops | bytes accessed | tf_op | source)
XLA Modules:
  0.0 498.4 jit_solution(8238800117729874039)
XLA Ops:
  7.2 0.0 reduce-scatter.2.cloned.1.call-start
  7.3 0.8 fusion
  8.1 1.3 broadcast_in_dim.77
  9.3 1.5 select_select_fusion.small_ref
  10.8 214.9 %shard_map.263 = (bf16[4,16,512]{2,1,0:T(8,128)(2,1)}, bf16[2048,2048]{1,0:T(8,128)(2,1)}, bf16[3,2048,512]{2,1,0:T(8,128)(2,1)}, bf16[1024,2048]{1,0:T(8,128)(2...) custom-call(bf16[16,512]{1,0:T(8,128)(2,1)} %select_select_fusion.sm, ...), custom_call_target="tpu_custom_call" | custom-call | flops 25769803776 | bytes 500000000 | tf_op jit(solution)/shard_map/pallas_call | solution.py:572
  225.7 0.0 reduce-scatter.2.cloned.1.call-update
  225.7 234.8 %shard_map.264 = (bf16[12,4,512,512]{3,2,1,0:T(8,128)(2,1)}, f32[192,128]{1,0:T(8,128)}, bf16[4,256,2048]{2,1,0:T(8,128)(2,1)}) custom-call(bf16[1024,2048]{1,0:T(8,128)(2,1)} %get-tuple-element.48.act_ref, bf16[1024,2048]{1,0:T(8,128)(2,1)} %get-tuple-element.49.up_ref, bf16[1024,512]{1,0:T(8,128)(2,1)} %get-tuple-element.50.mixed_ref, ...), custom_call_target="tpu_custom_call" | custom-call | flops 51539607552 | bytes 600000000 | tf_op jit(solution)/shard_map/pallas_call | solution.py:1083
  460.5 0.0 reduce-scatter.2.cloned.1.call-done.branch_ref
  460.6 30.5 %shard_map.265 = (bf16[256,2048]{1,0:T(8,128)(2,1)}, f32[256,2048]{1,0:T(8,128)}, f32[512,8192]{1,0:T(8,128)}, f32[2048,2048]{1,0:T(8,128)}, f32[512,2048]{1,0:T...) custom-call(bf16[12,4,512,512]{3,2,1,0:T(8,128)(2,1)} %get-tuple-ele, ...), custom_call_target="tpu_custom_call" | custom-call | tf_op jit(solution)/shard_map/pallas_call | solution.py:1194
  (5 shorter events, 0.0 us)
Async XLA Ops:
  7.2 453.4 %reduce-scatter.2.cloned.1.call-start = ((), (), s32[]{:S(2)}) async-start(), calls=%async_computation.1 | async-start | bytes 5242880 | tf_op jit(solution)/shard_map/reduce_scatter | solution.py:1275
Sparse Core Ops, SparseCore 0:
  225.9 88.2 reduce-scatter.1
